TPU v7x, 32 devices: a whole 2x2x4 slice. The times are simulated.
32 devices in a mesh: row: 16 (over z, y, x), col: 2 (over core).
Axes of the slice: x: 2, y: 2, z: 4, core: 2. Of those that a mesh axis runs over, the one named last changes fastest.
Arguments:
- trailing: bfloat16 [8192, 1024], P('row', 'col'), may hold values from -6 to 6
- u_factor: bfloat16 [16, 2, 512, 256], P('row', 'col'), may hold values from -0.07861328 to 0.07861328
- w_factor: bfloat16 [16, 2, 512, 256], P('row', 'col'), may hold values from -4.1875 to 4.1875
- diag_inverse: bfloat16 [2, 512, 512], P('col'), as said below
- ranks: int32 [16, 2], P('row', 'col'), may hold values from 32 to 256, as said below
- col_rows: int32 [2], replicated, may hold values from 0 to 15, as said below
Outputs:
- updated: float32 [8192, 1024], P('row', 'col')
Inputs may be any that keep to these rules, and one draw needn't show every extreme that they name: `ranks`: each tile's rank; some tile has rank 256 and some has rank 256 // 8. `col_rows`: distinct tile rows. `diag_inverse`: lower triangular, diagonal between 0.5 and 2.
All inputs are finite; a program needn't handle non-finite values.
Results may differ from a plain program's by a relative error of at most 0.0047.
Values may be sent and summed in bfloat16 or wider, within the bound.
No kernel may reach another device: no remote copies, remote signals or barrier semaphores. Data moves between devices by JAX's collectives and lax.ppermute only.
A program may use at most 64 MiB of HBM per device.

v0:
```python
import jax
import jax.numpy as jnp
from jax import lax
from jax.sharding import PartitionSpec as P


def spread(block, axis, source):
    block = jnp.where(lax.axis_index(axis) == source, block, jnp.zeros_like(block))
    return lax.psum(block, axis)


def panel_update(left_rows, right_rows, left_cols, right_cols):
    core = jnp.einsum(
        "ktr,kts->krs", right_rows, right_cols, preferred_element_type=jnp.float32
    ).astype(jnp.bfloat16)
    mixed = jnp.einsum("ktr,krs->kts", left_rows, core, preferred_element_type=jnp.float32).astype(
        jnp.bfloat16
    )
    return jnp.einsum("kts,kus->tu", mixed, left_cols, preferred_element_type=jnp.float32)


def local(trailing, u_factor, w_factor, diag_inverse, ranks, col_rows):
    rank_max = w_factor.shape[3]
    product = jnp.einsum(
        "ktu,kur->ktr", diag_inverse, w_factor[0], preferred_element_type=jnp.float32
    )
    keep = jnp.arange(rank_max, dtype=jnp.int32)[None, :] < ranks[0][:, None]
    solved = jnp.where(keep[:, None, :], product.astype(jnp.bfloat16), jnp.zeros((), jnp.bfloat16))
    paired = jnp.stack([u_factor[0], solved])
    gathered = lax.all_gather(paired, "col", axis=1, tiled=True)
    root = col_rows[lax.axis_index("col")]
    base = trailing.astype(jnp.float32)
    column = spread(gathered, "row", root)
    result = base - panel_update(gathered[0], gathered[1], column[0], column[1])
    return result


def solution(mesh):
    placed = (
        P("row", "col"),
        P("row", "col", None, None),
        P("row", "col", None, None),
        P("col", None, None),
        P("row", "col"),
        P(),
    )
    return jax.shard_map(
        local, mesh=mesh, in_specs=placed, out_specs=P("row", "col"), check_vma=False
    )
```

profile of v0, /device:TPU:0, one launch (start us, length us, event | category | flops | bytes accessed | tf_op | source)
XLA Modules:
  0.0 149.9 jit_solution(6835826235766440568)
XLA Ops:
  6.5 0.0 copy-start
  6.5 0.0 all-gather.2.cloned.1.call-start
  7.3 0.3 copy-done
  7.6 0.0 copy-start.2
  7.6 1.3 fusion.2
  8.9 0.0 copy-done.2
  8.9 0.8 pad_maximum_fusion
  9.7 0.0 all-gather.2.cloned.1.call-update
  9.8 0.0 all-reduce.2.cloned.1.call-start
  9.8 0.0 copy-start.5
  9.8 0.6 copy-done.5
  10.5 0.6 dynamic_slice.3
  11.7 10.0 %all-gather.2.cloned.1.call-done = bf16[2,2,512,256]{3,2,1,0:T(8,128)(2,1)} async-done(((bf16[2,1,512,256]{3,2,1,0:T(8,128)(2,1)}), bf16[2,2,512,256]{3,2,1,0:T(8,128)(2,1)}) %all-gather.2.cloned.1.call-update) | async-done | bytes 1048592 | tf_op jit(solution)/shard_map/all_gather | solution.py:30
  21.7 0.0 copy-start.4
  21.7 2.3 %broadcast_select_fusion = bf16[2,2,512,256]{3,2,1,0:T(8,128)(2,1)} fusion(bf16[2,2,512,256]{3,2,1,0:T(8,128)(2,1)} %all-gather.2.cloned.1.call-done, pred[]{:T(512)S(6)} %eq.3), kind=kLoop, calls=%fused_computation.7 | loop fusion | flops 524288 | bytes 2097153 | tf_op jit(solution)/shard_map/jit(_where)/select_n | solution.py:8
  24.0 0.0 copy-start.1
  24.0 0.0 all-reduce.2.cloned.1.call-update
  24.0 116.0 %all-reduce.2.cloned.1.call-done = bf16[2,2,512,256]{3,2,1,0:T(8,128)(2,1)} async-done(((bf16[2,2,512,256]{3,2,1,0:T(8,128)(2,1)}), bf16[2,2,512,256]{3,2,1,0:T(8,128)(2,1)}) %all-reduce.2.cloned.1.call-update) | async-done | bytes 1048592 | tf_op jit(solution)/shard_map/psum | solution.py:9
  140.0 0.0 copy-done.1
  140.0 0.0 copy-start.3
  140.0 1.5 convolution_convert_fusion.2
  141.4 0.0 copy-done.4
  141.5 0.0 copy-done.3
  141.5 1.5 %fusion = f32[512,512]{1,0:T(8,128)} fusion(bf16[2,256,256]{2,1,0:T(8,128)(2,1)S(1)} %convolution_convert_fusion.2, bf16[512,512]{1,0:T(8,128)(2,1)S(1)} %copy-done.4, bf16[2,2,512,256]{3,2,1,0:T(8,128)(2,1)S(1)} %copy-done.3, bf16[2,2,512,256]{3,2,1,0:T(8,128)(2,1)S(1)} %copy-done.1), kind=kOutput, calls=%fused_computation.1 | convolution fusion | flops 403439616 | bytes 2883584 | tf_op jit(solution)/shard_map/kts,kus->tu/dot_general | solution.py:19
  (1 shorter events, 0.0 us)
Async XLA Ops:
  6.5 1.1 copy-start
  6.5 15.1 %all-gather.2.cloned.1.call-start = ((), (), s32[]{:S(2)}) async-start(), calls=%async_computation | async-start | bytes 1572864 | tf_op jit(solution)/shard_map/all_gather | solution.py:30
  7.6 1.3 copy-start.2
  9.8 130.2 %all-reduce.2.cloned.1.call-start = ((), (), s32[]{:S(2)}) async-start(), calls=%async_computation.1 | async-start | bytes 2097152 | tf_op jit(solution)/shard_map/psum | solution.py:9
  9.8 0.7 copy-start.5
  21.7 119.8 %copy-start.4 = (bf16[512,512]{1,0:T(8,128)(2,1)S(1)}, bf16[512,512]{1,0:T(8,128)(2,1)}, u32[]{:S(2)}) copy-start(bf16[512,512]{1,0:T(8,128)(2,1)} %param.6) | copy-start | bytes 1572868
  24.0 116.0 %copy-start.1 = (bf16[2,2,512,256]{3,2,1,0:T(8,128)(2,1)S(1)}, bf16[2,2,512,256]{3,2,1,0:T(8,128)(2,1)}, u32[]{:S(2)}) copy-start(bf16[2,2,512,256]{3,2,1,0:T(8,128)(2,1)} %all-gather.2.cloned.1.call-done) | copy-start | bytes 3145732
  140.0 1.5 copy-start.3
Sparse Core Ops, SparseCore 0:
  9.9 11.7 all-gather.1
  26.9 112.9 all-reduce.1
where the time goes:
time: 150 us
  waiting for transfers between devices  126 us (84%)
  between operations  14.8 us (10%)
  matrix products  4.31 us (3%)
  other arithmetic  3.17 us (2%)
  local copies, waits for them, and re-layouts  1.61 us (1%)
    psum x1, waiting for transfers between devices, spread(): return lax.psum(block, axis)  116 us
    all_gather x1, waiting for transfers between devices, local(): gathered = lax.all_gather(paired, 'col', axis=1, tiled=True)  9.95 us
  transfers between devices with their start and end apart: 2, of which 2 were waited for; matrix products, arithmetic and copies ran while one was open for 0% of the time, Pallas kernels for 0%

commit v1 on v0

v1 whole, which is shorter than its diff:
```python
import jax
import jax.numpy as jnp
from jax import lax
from jax.sharding import PartitionSpec as P

SPLIT = 2


def bit(value, at):
    return (value >> at) & 1


class Route:
    def __init__(self, rows, cols):
        bits = rows.bit_length() - 1
        low, high = list(range(SPLIT)), list(range(SPLIT, bits))
        self.orders = (low + high, low[::-1] + high[::-1])
        self.rows, self.cols, self.steps = rows, cols, bits
        self.me = lax.axis_index("row")
        self.odd = (lax.axis_index("col") & 1) == 1

    def of(self, row, step):
        even, odd = (bit(row, order[step]) for order in self.orders)
        return jnp.where(self.odd, odd, even)

    def cross(self, block, step):
        pairs = [
            (i * self.cols + c, (i ^ (1 << self.orders[c & 1][step])) * self.cols + c)
            for i in range(self.rows)
            for c in range(self.cols)
        ]
        return lax.ppermute(block, ("row", "col"), pairs)


def swap_cols(block):
    return lax.ppermute(block, "col", [(0, 1), (1, 0)])


def own_columns(slots, cols, col):
    if cols == 2:
        mine = jnp.where(col == 0, slots[0], slots[1])
        other = jnp.where(col == 0, slots[1], slots[0])
        return [mine, swap_cols(other)]
    moved = lax.all_to_all(jnp.stack(slots), "col", 0, 0, tiled=True)
    return [lax.dynamic_index_in_dim(moved, (col + k) % cols, 0, False) for k in range(cols)]


def all_panels(block, cols, col):
    if cols == 2:
        return [block, swap_cols(block)]
    moved = lax.all_gather(block, "col")
    return [lax.dynamic_index_in_dim(moved, (col + k) % cols, 0, False) for k in range(cols)]


def paired(block, route, roots, col):
    cols = route.cols
    height = block.shape[-2] // 4
    part = [
        [block[..., (2 * x + y) * height : (2 * x + y + 1) * height, :] for y in range(2)]
        for x in range(2)
    ]
    part = [[jnp.where(route.odd, part[y][x], part[x][y]) for y in range(2)] for x in range(2)]
    a, b = route.of(route.me, 0) == 1, route.of(route.me, 1) == 1
    near = [
        [route.of(root, step) == route.of(route.me, step) for step in range(route.steps)]
        for root in roots
    ]
    kept = jnp.stack([jnp.where(a, part[1][y], part[0][y]) for y in range(2)])
    sent = jnp.stack([jnp.where(a, part[0][y], part[1][y]) for y in range(2)])
    came = route.cross(sent, 0)
    slots = [jnp.where(n[0], kept, came) for n in near]
    kept = [jnp.where(b, s[1], s[0]) for s in slots]
    came = route.cross(jnp.stack([jnp.where(b, s[0], s[1]) for s in slots]), 1)
    slots = [jnp.where(n[1], k, came[c]) for c, (n, k) in enumerate(zip(near, kept))]
    for step in range(SPLIT, route.steps):
        came = route.cross(jnp.stack(slots), step)
        slots = [jnp.where(n[step], s, came[c]) for c, (n, s) in enumerate(zip(near, slots))]
    held = jnp.stack(own_columns(slots, cols, col))
    came = route.cross(held, 1)
    pair = jnp.stack([jnp.where(b, came, held), jnp.where(b, held, came)])
    came = route.cross(pair, 0)
    whole = [jnp.where(a, came, pair), jnp.where(a, pair, came)]
    whole = [[jnp.where(route.odd, whole[y][x], whole[x][y]) for y in range(2)] for x in range(2)]
    return jnp.concatenate([whole[x][y] for x in range(2) for y in range(2)], axis=-2)


def local(cols, rows, trailing, u_factor, w_factor, diag_inverse, ranks, col_rows):
    rank_max = w_factor.shape[3]
    col = lax.axis_index("col")
    route = Route(rows, cols)
    roots = [col_rows[c] for c in range(cols)]
    product = jnp.dot(diag_inverse[0], w_factor[0, 0], preferred_element_type=jnp.float32)
    keep = jnp.arange(rank_max, dtype=jnp.int32) < ranks[0, 0]
    solved = jnp.where(keep[None, :], product.astype(jnp.bfloat16), jnp.zeros((), jnp.bfloat16))
    block = jnp.stack([u_factor[0, 0], solved])
    row = jnp.stack(all_panels(block, cols, col))
    column = paired(block, route, roots, col)
    core = jnp.einsum(
        "ktr,kts->krs", row[:, 1], column[:, 1], preferred_element_type=jnp.float32
    ).astype(jnp.bfloat16)
    mixed = jnp.einsum("ktr,krs->kts", row[:, 0], core, preferred_element_type=jnp.float32)
    mixed = mixed.astype(jnp.bfloat16)
    change = jnp.einsum("kts,kus->tu", mixed, column[:, 0], preferred_element_type=jnp.float32)
    return trailing.astype(jnp.float32) - change


def solution(mesh):
    placed = (
        P("row", "col"),
        P("row", "col", None, None),
        P("row", "col", None, None),
        P("col", None, None),
        P("row", "col"),
        P(),
    )

    def step(*args):
        return local(mesh.shape["col"], mesh.shape["row"], *args)

    return jax.shard_map(
        step, mesh=mesh, in_specs=placed, out_specs=P("row", "col"), check_vma=False
    )
```

time: 150 us -> 55.5 us (0.37)
  waiting for transfers between devices: 126 us -> 29.5 us
  starting transfers between devices: 0.04 us -> 14.2 us
  between operations: 14.8 us -> 6.04 us
  other arithmetic: 3.17 us -> 0.76 us
    psum x1 -> x0, waiting for transfers between devices: 116 us -> none  [spread(): return lax.psum(block, axis)]
    ppermute x0 -> x8, waiting for transfers between devices: none -> 29.5 us  [the longest x6 28.2 us: cross(): return lax.ppermute(block, ('row', 'col'), pairs)]
    ppermute x0 -> x8, starting transfers between devices: none -> 14.2 us  [the longest x6 14 us: cross(): return lax.ppermute(block, ('row', 'col'), pairs)]
    all_gather x1 -> x0, waiting for transfers between devices: 9.95 us -> none  [local(): gathered = lax.all_gather(paired, 'col', axis=1, tiled=True)]
    select_n x1 -> x7, other arithmetic: 2.32 us -> 0.31 us  [the longest x1 0.07 us: paired(): jnp.where(route.odd, whole[y][x], whole[x][y])]
  transfers between devices with their start and end apart: 2 -> 8, of which waited for: 2 -> 7; matrix products, arithmetic and copies ran while one was open for 0% -> 2% of each run, Pallas kernels for 0% -> 0%
where the time goes in v1:
time: 55.5 us; the launch traced here: 55.2 us
  waiting for transfers between devices  29.5 us (53%)
  starting transfers between devices  14.2 us (26%)
  between operations  6.04 us (11%)
  matrix products  3.16 us (6%)
  local copies, waits for them, and re-layouts  1.62 us (3%)
  other arithmetic  0.76 us (1%)
    ppermute x6, waiting for transfers between devices, cross(): return lax.ppermute(block, ('row', 'col'), pairs)  28.2 us
    ppermute x6, starting transfers between devices, cross(): return lax.ppermute(block, ('row', 'col'), pairs)  14 us
    dot_general x1, matrix products, local(): jnp.einsum('kts,kus->tu', mixed, column[:, 0], preferred_element_type=jnp...  1.55 us
    ppermute x2, waiting for transfers between devices, swap_cols(): return lax.ppermute(block, 'col', [(0, 1), (1, 0)])  1.34 us
    dot_general x1, matrix products, local(): jnp.dot(diag_inverse[0], w_factor[0, 0], preferred_element_type=jnp.float32)  1.24 us
  transfers between devices with their start and end apart: 8, of which 7 were waited for; matrix products, arithmetic and copies ran while one was open for 2% of the time, Pallas kernels for 0%

profile of v1, /device:TPU:0, one launch (start us, length us, event | category | flops | bytes accessed | tf_op | source)
XLA Modules:
  0.0 55.2 jit_solution(13049195498261001625)
XLA Ops:
  0.0 0.0 copy-start
  0.7 0.3 copy-done
  1.1 1.2 %fusion.2 = bf16[1,512,256]{2,1,0:T(8,128)(2,1)S(1)} fusion(bf16[1,512,512]{2,1,0:T(8,128)(2,1)S(1)} %copy-done, bf16[1,1,512,256]{3,2,1,0:T(8,128)(2,1)} %param.8, pred[256]{0:T(512)(128)(4,1)S(1)} %iota_compare_fusion), kind=kOutput, calls=%fused_computation.6 | convolution fusion | flops 134479872 | bytes 1048832 | tf_op jit(solution)/shard_map/dot_general | solution.py:92
  2.3 0.0 copy-done.1
  2.4 0.0 copy-start.2
  2.5 3.0 %collective-permute-start.1 = (bf16[2,2,128,256]{3,2,1,0:T(8,128)(2,1)S(1)}, bf16[2,2,128,256]{3,2,1,0:T(8,128)(2,1)S(1)}, u32[]{:S(2)}, u32[]{:S(2)}) collective-permute-start(bf16[2,2,128,256]{3,2,1,0:T(8,128)(2,1)S(1)} %pad_maximum_fusion.5), channel_id=1, source_target_pairs={{0,2},{1,5},{2,0},{3,7},{4,6},{5,1},{6,4},{7,3},{8,10},{9,13},{10,... | collective-permute-start | bytes 786440 | tf_op jit(solution)/shard_map/ppermute | solution.py:32
  5.5 0.0 copy-done.2
  5.5 0.6 %fusion.22 = (s32[1]{0:T(128)}, s32[1]{0:T(128)}) fusion(s32[2]{0:T(128)S(1)} %copy-done.2), kind=kLoop, calls=%fused_computation.69 | loop fusion | bytes 16 | tf_op jit(solution)/shard_map/slice | solution.py:91
  8.7 1.1 %collective-permute-done.1 = bf16[2,2,128,256]{3,2,1,0:T(8,128)(2,1)S(1)} collective-permute-done((bf16[2,2,128,256]{3,2,1,0:T(8,128)(2,1)S(1)}, bf16[2,2,128,256]{3,2,1,0:T(8,128)(2,1)S(1)}, u32[]{:S(2)}, u32[]{:S(2)}) %collective-permute-start.1) | collective-permute-done | bytes 262176 | tf_op jit(solution)/shard_map/ppermute | solution.py:32
  9.9 2.1 %collective-permute-start.2 = (bf16[2,2,128,256]{3,2,1,0:T(8,128)(2,1)S(1)}, bf16[2,2,128,256]{3,2,1,0:T(8,128)(2,1)S(1)}, u32[]{:S(2)}, u32[]{:S(2)}) collective-permute-start(bf16[2,2,128,256]{3,2,1,0:T(8,128)(2,1)S(1)} %pad_maximum_fusion.6), channel_id=1, source_target_pairs={{0,4},{1,3},{2,6},{3,1},{4,0},{5,7},{6,2},{7,5},{8,12},{9,11},{10,... | collective-permute-start | bytes 786440 | tf_op jit(solution)/shard_map/ppermute | solution.py:32
  12.0 4.4 %collective-permute-done.2 = bf16[2,2,128,256]{3,2,1,0:T(8,128)(2,1)S(1)} collective-permute-done((bf16[2,2,128,256]{3,2,1,0:T(8,128)(2,1)S(1)}, bf16[2,2,128,256]{3,2,1,0:T(8,128)(2,1)S(1)}, u32[]{:S(2)}, u32[]{:S(2)}) %collective-permute-start.2) | collective-permute-done | bytes 262176 | tf_op jit(solution)/shard_map/ppermute | solution.py:32
  16.5 2.1 %collective-permute-start.3 = (bf16[2,2,128,256]{3,2,1,0:T(8,128)(2,1)S(1)}, bf16[2,2,128,256]{3,2,1,0:T(8,128)(2,1)S(1)}, u32[]{:S(2)}, u32[]{:S(2)}) collective-permute-start(bf16[2,2,128,256]{3,2,1,0:T(8,128)(2,1)S(1)} %pad_maximum_fusion.7), channel_id=1, source_target_pairs={{0,8},{1,17},{2,10},{3,19},{4,12},{5,21},{6,14},{7,23},{8,0},{9,25... | collective-permute-start | bytes 786440 | tf_op jit(solution)/shard_map/ppermute | solution.py:32
  21.2 3.4 %collective-permute-done.3 = bf16[2,2,128,256]{3,2,1,0:T(8,128)(2,1)S(1)} collective-permute-done((bf16[2,2,128,256]{3,2,1,0:T(8,128)(2,1)S(1)}, bf16[2,2,128,256]{3,2,1,0:T(8,128)(2,1)S(1)}, u32[]{:S(2)}, u32[]{:S(2)}) %collective-permute-start.3) | collective-permute-done | bytes 262176 | tf_op jit(solution)/shard_map/ppermute | solution.py:32
  24.7 3.3 %collective-permute-start.4 = (bf16[2,2,128,256]{3,2,1,0:T(8,128)(2,1)S(1)}, bf16[2,2,128,256]{3,2,1,0:T(8,128)(2,1)S(1)}, u32[]{:S(2)}, u32[]{:S(2)}) collective-permute-start(bf16[2,2,128,256]{3,2,1,0:T(8,128)(2,1)S(1)} %pad_maximum_fusion.8), channel_id=1, source_target_pairs={{0,16},{1,9},{2,18},{3,11},{4,20},{5,13},{6,22},{7,15},{8,24},{9,1... | collective-permute-start | bytes 786440 | tf_op jit(solution)/shard_map/ppermute | solution.py:32
  27.9 7.2 %collective-permute-done.4 = bf16[2,2,128,256]{3,2,1,0:T(8,128)(2,1)S(1)} collective-permute-done((bf16[2,2,128,256]{3,2,1,0:T(8,128)(2,1)S(1)}, bf16[2,2,128,256]{3,2,1,0:T(8,128)(2,1)S(1)}, u32[]{:S(2)}, u32[]{:S(2)}) %collective-permute-start.4) | collective-permute-done | bytes 262176 | tf_op jit(solution)/shard_map/ppermute | solution.py:32
  35.2 0.1 collective-permute-start.5
  35.3 1.3 %collective-permute-done.5 = bf16[2,128,256]{2,1,0:T(8,128)(2,1)S(1)} collective-permute-done((bf16[2,128,256]{2,1,0:T(8,128)(2,1)S(1)}, bf16[2,128,256]{2,1,0:T(8,128)(2,1)S(1)}, u32[]{:S(2)}, u32[]{:S(2)}) %collective-permute-start.5) | collective-permute-done | bytes 131104 | tf_op jit(solution)/shard_map/ppermute | solution.py:36
  36.6 1.8 %collective-permute-start.6 = (bf16[2,2,128,256]{3,2,1,0:T(8,128)(2,1)S(1)}, bf16[2,2,128,256]{3,2,1,0:T(8,128)(2,1)S(1)}, u32[]{:S(2)}, u32[]{:S(2)}) collective-permute-start(bf16[2,2,128,256]{3,2,1,0:T(8,128)(2,1)S(1)} %pad_maximum_fusion.9), channel_id=1, source_target_pairs={{0,4},{1,3},{2,6},{3,1},{4,0},{5,7},{6,2},{7,5},{8,12},{9,11},{10,... | collective-permute-start | bytes 786440 | tf_op jit(solution)/shard_map/ppermute | solution.py:32
  38.4 4.7 %collective-permute-done.6 = bf16[2,2,128,256]{3,2,1,0:T(8,128)(2,1)S(1)} collective-permute-done((bf16[2,2,128,256]{3,2,1,0:T(8,128)(2,1)S(1)}, bf16[2,2,128,256]{3,2,1,0:T(8,128)(2,1)S(1)}, u32[]{:S(2)}, u32[]{:S(2)}) %collective-permute-start.6) | collective-permute-done | bytes 262176 | tf_op jit(solution)/shard_map/ppermute | solution.py:32
  43.1 0.1 pad_maximum_fusion.3
  43.2 1.7 %collective-permute-start.7 = (bf16[2,2,2,128,256]{4,3,2,1,0:T(8,128)(2,1)S(1)}, bf16[2,2,2,128,256]{4,3,2,1,0:T(8,128)(2,1)S(1)}, u32[]{:S(2)}, u32[]{:S(2)}) collective-permute-start(bf16[2,2,2,128,256]{4,3,2,1,0:T(8,128)(2,1)S(1)} %pad_maximum_fusion.3), channel_id=1, source_target_pairs={{0,2},{1,5},{2,0},{3,7},{4,6},{5,1},{6,4},{7,3},{8,10},{9,13},{10,... | collective-permute-start | bytes 1572872 | tf_op jit(solution)/shard_map/ppermute | solution.py:32
  44.9 0.1 fusion.19
  45.0 0.1 collective-permute-start
  45.0 7.4 %collective-permute-done.7 = bf16[2,2,2,128,256]{4,3,2,1,0:T(8,128)(2,1)S(1)} collective-permute-done((bf16[2,2,2,128,256]{4,3,2,1,0:T(8,128)(2,1)S(1)}, bf16[2,2,2,128,256]{4,3,2,1,0:T(8,128)(2,1)S(1)}, u32[]{:S(2)}, u32[]{:S(2)}) %collective-permute-start.7) | collective-permute-done | bytes 524320 | tf_op jit(solution)/shard_map/ppermute | solution.py:32
  52.4 0.1 broadcast_select_fusion.1
  52.5 0.1 select_bitcast_fusion.1
  52.6 0.1 pad_maximum_fusion
  52.6 0.0 copy-start.3
  52.7 0.0 collective-permute-done
  52.7 0.4 convolution_convert_fusion.2
  53.0 0.6 %copy-done.3 = bf16[512,512]{1,0:T(8,128)(2,1)S(1)} copy-done((bf16[512,512]{1,0:T(8,128)(2,1)S(1)}, bf16[512,512]{1,0:T(8,128)(2,1)}, u32[]{:S(2)}) %copy-start.3) | copy-done | bytes 524312
  53.7 1.5 %fusion = f32[512,512]{1,0:T(8,128)} fusion(bf16[2,256,256]{2,1,0:T(8,128)(2,1)S(1)} %convolution_convert_fusion.2, bf16[512,512]{1,0:T(8,128)(2,1)S(1)} %copy-done.3, bf16[1,2,512,256]{3,2,1,0:T(8,128)(2,1)S(1)} %get-tuple-element.15, bf16[1,2,512,256]{3,2,1,0:T(8,128)(2,1)S(1)} %bitcast.67, bf16[2,2,512,256]{3,2,1,0:T(8,128)(2,1)S(1)} %pad_maximum_fusion), kind=kOutput, calls=%fused_computation.1 | convolution fusion | flops 403701760 | bytes 3407872 | tf_op jit(solution)/shard_map/kts,kus->tu/dot_general | solution.py:103
  (15 shorter events, 0.4 us)
Async XLA Ops:
  0.0 1.1 %copy-start = (bf16[1,512,512]{2,1,0:T(8,128)(2,1)S(1)}, bf16[1,512,512]{2,1,0:T(8,128)(2,1)}, u32[]{:S(2)}) copy-start(bf16[1,512,512]{2,1,0:T(8,128)(2,1)} %param.9) | copy-start | bytes 1572868
  0.0 2.3 %copy-start.1 = (bf16[1,1,512,256]{3,2,1,0:T(8,128)(2,1)S(1)}, bf16[1,1,512,256]{3,2,1,0:T(8,128)(2,1)}, u32[]{:S(2)}) copy-start(bf16[1,1,512,256]{3,2,1,0:T(8,128)(2,1)} %param.7) | copy-start | bytes 786436
  2.4 3.1 %copy-start.2 = (s32[2]{0:T(128)S(1)}, s32[2]{0:T(128)}, u32[]{:S(2)}) copy-start(s32[2]{0:T(128)} %param.11) | copy-start | bytes 28
  2.5 7.4 %collective-permute-start.1 = (bf16[2,2,128,256]{3,2,1,0:T(8,128)(2,1)S(1)}, bf16[2,2,128,256]{3,2,1,0:T(8,128)(2,1)S(1)}, u32[]{:S(2)}, u32[]{:S(2)}) collective-permute-start(bf16[2,2,128,256]{3,2,1,0:T(8,128)(2,1)S(1)} %pad_maximum_fusion.5), channel_id=1, source_target_pairs={{0,2},{1,5},{2,0},{3,7},{4,6},{5,1},{6,4},{7,3},{8,10},{9,13},{10,... | collective-permute-start | bytes 786440 | tf_op jit(solution)/shard_map/ppermute | solution.py:32
  9.9 6.5 %collective-permute-start.2 = (bf16[2,2,128,256]{3,2,1,0:T(8,128)(2,1)S(1)}, bf16[2,2,128,256]{3,2,1,0:T(8,128)(2,1)S(1)}, u32[]{:S(2)}, u32[]{:S(2)}) collective-permute-start(bf16[2,2,128,256]{3,2,1,0:T(8,128)(2,1)S(1)} %pad_maximum_fusion.6), channel_id=1, source_target_pairs={{0,4},{1,3},{2,6},{3,1},{4,0},{5,7},{6,2},{7,5},{8,12},{9,11},{10,... | collective-permute-start | bytes 786440 | tf_op jit(solution)/shard_map/ppermute | solution.py:32
  16.5 8.1 %collective-permute-start.3 = (bf16[2,2,128,256]{3,2,1,0:T(8,128)(2,1)S(1)}, bf16[2,2,128,256]{3,2,1,0:T(8,128)(2,1)S(1)}, u32[]{:S(2)}, u32[]{:S(2)}) collective-permute-start(bf16[2,2,128,256]{3,2,1,0:T(8,128)(2,1)S(1)} %pad_maximum_fusion.7), channel_id=1, source_target_pairs={{0,8},{1,17},{2,10},{3,19},{4,12},{5,21},{6,14},{7,23},{8,0},{9,25... | collective-permute-start | bytes 786440 | tf_op jit(solution)/shard_map/ppermute | solution.py:32
  24.7 10.5 %collective-permute-start.4 = (bf16[2,2,128,256]{3,2,1,0:T(8,128)(2,1)S(1)}, bf16[2,2,128,256]{3,2,1,0:T(8,128)(2,1)S(1)}, u32[]{:S(2)}, u32[]{:S(2)}) collective-permute-start(bf16[2,2,128,256]{3,2,1,0:T(8,128)(2,1)S(1)} %pad_maximum_fusion.8), channel_id=1, source_target_pairs={{0,16},{1,9},{2,18},{3,11},{4,20},{5,13},{6,22},{7,15},{8,24},{9,1... | collective-permute-start | bytes 786440 | tf_op jit(solution)/shard_map/ppermute | solution.py:32
  35.2 1.4 %collective-permute-start.5 = (bf16[2,128,256]{2,1,0:T(8,128)(2,1)S(1)}, bf16[2,128,256]{2,1,0:T(8,128)(2,1)S(1)}, u32[]{:S(2)}, u32[]{:S(2)}) collective-permute-start(bf16[2,128,256]{2,1,0:T(8,128)(2,1)S(1)} %get-tuple-element.22), channel_id=1, source_target_pairs={{0,1},{1,0},{2,3},{3,2},{4,5},{5,4},{6,7},{7,6},{8,9},{9,8},{10,11... | collective-permute-start | bytes 393224 | tf_op jit(solution)/shard_map/ppermute | solution.py:36
  36.6 6.4 %collective-permute-start.6 = (bf16[2,2,128,256]{3,2,1,0:T(8,128)(2,1)S(1)}, bf16[2,2,128,256]{3,2,1,0:T(8,128)(2,1)S(1)}, u32[]{:S(2)}, u32[]{:S(2)}) collective-permute-start(bf16[2,2,128,256]{3,2,1,0:T(8,128)(2,1)S(1)} %pad_maximum_fusion.9), channel_id=1, source_target_pairs={{0,4},{1,3},{2,6},{3,1},{4,0},{5,7},{6,2},{7,5},{8,12},{9,11},{10,... | collective-permute-start | bytes 786440 | tf_op jit(solution)/shard_map/ppermute | solution.py:32
  43.2 9.2 %collective-permute-start.7 = (bf16[2,2,2,128,256]{4,3,2,1,0:T(8,128)(2,1)S(1)}, bf16[2,2,2,128,256]{4,3,2,1,0:T(8,128)(2,1)S(1)}, u32[]{:S(2)}, u32[]{:S(2)}) collective-permute-start(bf16[2,2,2,128,256]{4,3,2,1,0:T(8,128)(2,1)S(1)} %pad_maximum_fusion.3), channel_id=1, source_target_pairs={{0,2},{1,5},{2,0},{3,7},{4,6},{5,1},{6,4},{7,3},{8,10},{9,13},{10,... | collective-permute-start | bytes 1572872 | tf_op jit(solution)/shard_map/ppermute | solution.py:32
  45.0 7.7 %collective-permute-start = (bf16[2,512,256]{2,1,0:T(8,128)(2,1)S(1)}, bf16[2,512,256]{2,1,0:T(8,128)(2,1)S(1)}, u32[]{:S(2)}, u32[]{:S(2)}) collective-permute-start(bf16[2,512,256]{2,1,0:T(8,128)(2,1)S(1)} %get-tuple-element.16), channel_id=1, source_target_pairs={{0,1},{1,0},{2,3},{3,2},{4,5},{5,4},{6,7},{7,6},{8,9},{9,8},{10,11... | collective-permute-start | bytes 1572872 | tf_op jit(solution)/shard_map/ppermute | solution.py:36
  52.6 1.0 %copy-start.3 = (bf16[512,512]{1,0:T(8,128)(2,1)S(1)}, bf16[512,512]{1,0:T(8,128)(2,1)}, u32[]{:S(2)}) copy-start(bf16[512,512]{1,0:T(8,128)(2,1)} %param.6) | copy-start | bytes 1572868

commit v2 on v0

v2 whole, which is shorter than its diff:
```python
import functools

import jax
import jax.numpy as jnp
from jax import lax
from jax.sharding import PartitionSpec as P

LOW = 2
FAN = ((1, 2), (2, 1), (3, 3))


def after(value, earlier):
    return lax.optimization_barrier((value, earlier))[0]


def swap_cols(block):
    return lax.ppermute(block, "col", [(0, 1), (1, 0)])


def all_panels(block, cols, col):
    if cols == 2:
        return jnp.stack([block, swap_cols(block)])
    return jnp.roll(lax.all_gather(block, "col"), -col, axis=0)


class Paths:
    def __init__(self, rows, cols, col_rows, width):
        self.rows, self.cols = rows, cols
        self.row, self.col = lax.axis_index("row"), lax.axis_index("col")
        self.odd = (self.col & 1) == 1
        self.place = self.row & ((1 << LOW) - 1)
        self.apart = jnp.broadcast_to((col_rows ^ self.row)[:, None], (cols, width))
        high = list(range(LOW, rows.bit_length() - 1))
        self.high = [(1 << even, 1 << odd) for even, odd in zip(high, high[::-1])]

    def of(self, pair):
        return jnp.where(self.odd, pair[1], pair[0])

    def cross(self, block, masks):
        rows, cols = range(self.rows), range(self.cols)
        pairs = [(i * self.cols + c, (i ^ masks[c & 1]) * self.cols + c) for i in rows for c in cols]
        return lax.ppermute(block, ("row", "col"), pairs)

    def scatter_start(self, block):
        height, width = block.shape
        parts = block.reshape(1 << LOW, height >> LOW, width)
        part = functools.partial(lax.dynamic_index_in_dim, parts, axis=0, keepdims=False)
        sent = [part(self.place ^ self.of(masks)) for masks in FAN]
        return part(self.place), [self.cross(block, masks) for block, masks in zip(sent, FAN)], sent

    def scatter_end(self, slots, came):
        low = (self.apart & ((1 << LOW) - 1))[:, None, :]
        for masks, block in zip(FAN, came):
            slots = jnp.where(low == self.of(masks), block, slots)
        return slots

    def spread(self, slots, came, step):
        mine = (jnp.arange(self.cols) == self.col)[:, None]
        apart = jnp.sum(jnp.where(mine, self.apart, 0), axis=0)
        return jnp.where((apart & self.of(self.high[step])) == 0, slots, came)

    def own_columns(self, slots):
        if self.cols == 2:
            mine = jnp.where(self.col == 0, slots[0], slots[1])
            other = jnp.where(self.col == 0, slots[1], slots[0])
            return jnp.stack([mine, swap_cols(other)])
        return jnp.roll(lax.all_to_all(slots, "col", 0, 0, tiled=True), -self.col, axis=0)

    def gather_start(self, held):
        return [held, *(self.cross(held, masks) for masks in FAN)]

    def gather_end(self, parts):
        masks = [self.of(masks) for masks in FAN]
        whole = []
        for q in range(1 << LOW):
            part = parts[0]
            for mask, came in zip(masks, parts[1:]):
                part = jnp.where((self.place ^ q) == mask, came, part)
            whole.append(part)
        return jnp.concatenate(whole, axis=1)


def local(cols, rows, trailing, u_factor, w_factor, diag_inverse, ranks, col_rows):
    rank_max = w_factor.shape[3]
    col = lax.axis_index("col")
    left, inverse = u_factor[0, 0], diag_inverse[0]
    keep = jnp.arange(rank_max, dtype=jnp.int32) < ranks[0, 0]
    right = jnp.where(keep[None, :], w_factor[0, 0], jnp.zeros((), jnp.bfloat16))
    first, second = (Paths(rows, cols, c, rank_max) for c in (col_rows, after(col_rows, left)))
    one, came_one, _ = first.scatter_start(right)
    two, came_two, sent = second.scatter_start(left)

    own = all_panels(after(jnp.stack([right, left]), sent), cols, col)
    inverse = all_panels(after(inverse, sent), cols, col)
    right, left = own[:, 0], own[:, 1]
    solve = functools.partial(jnp.einsum, "ktu,kur->ktr", preferred_element_type=jnp.float32)
    solved = solve(inverse, right).astype(jnp.bfloat16)

    one = first.own_columns(first.scatter_end(one, after(came_one, sent)))
    came_one = first.cross(one, first.high[0])
    two = second.own_columns(second.scatter_end(two, after(came_two, one)))
    came_two = second.cross(two, second.high[0])
    last = len(first.high) - 1
    for step in range(last):
        one = first.spread(one, after(came_one, two), step)
        came_one = first.cross(one, first.high[step + 1])
        two = second.spread(two, after(came_two, one), step)
        came_two = second.cross(two, second.high[step + 1])
    one = first.spread(one, after(came_one, (two, solved)), last)
    parts_one = first.gather_start(one)
    two = second.spread(two, after(came_two, parts_one[1]), last)
    parts_two = second.gather_start(two)

    right_col = first.gather_end([after(part, two) for part in parts_one])
    solved_col = solve(inverse, right_col).astype(jnp.bfloat16)
    core = jnp.einsum("ktr,kts->krs", solved, solved_col, preferred_element_type=jnp.float32)
    core = core.astype(jnp.bfloat16)
    mixed = jnp.einsum("ktr,krs->kts", left, core, preferred_element_type=jnp.float32)
    mixed = mixed.astype(jnp.bfloat16)
    left_col = second.gather_end([after(part, mixed) for part in parts_two])
    change = jnp.einsum("kts,kus->tu", mixed, left_col, preferred_element_type=jnp.float32)
    return trailing.astype(jnp.float32) - change


def solution(mesh):
    placed = (
        P("row", "col"),
        P("row", "col", None, None),
        P("row", "col", None, None),
        P("col", None, None),
        P("row", "col"),
        P(),
    )
    step = functools.partial(local, mesh.shape["col"], mesh.shape["row"])
    return jax.shard_map(
        step, mesh=mesh, in_specs=placed, out_specs=P("row", "col"), check_vma=False
    )
```

time: 150 us -> 43.6 us (0.29)
  waiting for transfers between devices: 126 us -> 14 us
  starting transfers between devices: 0.04 us -> 22.1 us
  between operations: 14.8 us -> 0.9 us
  local copies, waits for them, and re-layouts: 1.61 us -> 0.07 us
  other arithmetic: 3.17 us -> 1.67 us
    psum x1 -> x0, waiting for transfers between devices: 116 us -> none  [spread(): return lax.psum(block, axis)]
    ppermute x0 -> x20, starting transfers between devices: none -> 22.1 us  [the longest x16 21.4 us: cross(): return lax.ppermute(block, ('row', 'col'), pairs)]
    ppermute x0 -> x20, waiting for transfers between devices: none -> 14 us  [the longest x16 11.8 us: cross(): return lax.ppermute(block, ('row', 'col'), pairs)]
    all_gather x1 -> x0, waiting for transfers between devices: 9.95 us -> none  [local(): gathered = lax.all_gather(paired, 'col', axis=1, tiled=True)]
    dot_general x3 -> x4, matrix products: 4.31 us -> 4.67 us  [the longest x1 1.69 us: local(): jnp.einsum('ktr,kts->krs', solved, solved_col, preferred_element_type=jnp...]
  transfers between devices with their start and end apart: 2 -> 20, of which waited for: 2 -> 11; matrix products, arithmetic and copies ran while one was open for 0% -> 9% of each run, Pallas kernels for 0% -> 0%
where the time goes in v2:
time: 43.6 us; the launch traced here: 43.4 us
  starting transfers between devices  22.1 us (51%)
  waiting for transfers between devices  14 us (32%)
  matrix products  4.67 us (11%)
  other arithmetic  1.67 us (4%)
  between operations  0.9 us (2%)
    ppermute x16, starting transfers between devices, cross(): return lax.ppermute(block, ('row', 'col'), pairs)  21.4 us
    ppermute x16, waiting for transfers between devices, cross(): return lax.ppermute(block, ('row', 'col'), pairs)  11.8 us
    ppermute x4, waiting for transfers between devices, swap_cols(): return lax.ppermute(block, 'col', [(0, 1), (1, 0)])  2.13 us
    dot_general x1, matrix products, local(): jnp.einsum('ktr,kts->krs', solved, solved_col, preferred_element_type=jnp...  1.69 us
    dot_general x1, matrix products, local(): jnp.einsum('kts,kus->tu', mixed, left_col, preferred_element_type=jnp.flo...  1.45 us
    dot_general x1, matrix products, local(): solved = solve(inverse, right).astype(jnp.bfloat16)  1.24 us
    select_n x2, other arithmetic, local(): jnp.where(keep[None, :], w_factor[0, 0], jnp.zeros((), jnp.bfloat16))  1 us
  transfers between devices with their start and end apart: 20, of which 11 were waited for; matrix products, arithmetic and copies ran while one was open for 9% of the time, Pallas kernels for 0%

profile of v2, /device:TPU:0, one launch (start us, length us, event | category | flops | bytes accessed | tf_op | source)
XLA Modules:
  0.0 43.4 jit_solution(5625300135136859195)
XLA Ops:
  0.7 1.0 %broadcast_select_fusion = bf16[4,128,256]{2,1,0:T(8,128)(2,1)S(1)} fusion(bf16[4,128,256]{2,1,0:T(8,128)(2,1)} %bitcast.49, pred[256]{0:T(512)(128)(4,1)S(1)} %iota_compare_fusion), kind=kLoop, calls=%fused_computation.31 | loop fusion | flops 131072 | bytes 524544 | tf_op jit(solution)/shard_map/jit(_where)/select_n | solution.py:88
  1.7 3.0 %collective-permute-start.2 = (bf16[128,256]{1,0:T(8,128)(2,1)S(1)}, bf16[128,256]{1,0:T(8,128)(2,1)S(1)}, u32[]{:S(2)}, u32[]{:S(2)}) collective-permute-start(bf16[128,256]{1,0:T(8,128)(2,1)S(1)} %get-tuple-element.66), channel_id=1, source_target_pairs={{0,2},{1,5},{2,0},{3,7},{4,6},{5,1},{6,4},{7,3},{8,10},{9,13},{10,... | collective-permute-start | bytes 196616 | tf_op jit(solution)/shard_map/ppermute | solution.py:42
  4.7 1.5 %collective-permute-start.3 = (bf16[128,256]{1,0:T(8,128)(2,1)S(1)}, bf16[128,256]{1,0:T(8,128)(2,1)S(1)}, u32[]{:S(2)}, u32[]{:S(2)}) collective-permute-start(bf16[128,256]{1,0:T(8,128)(2,1)S(1)} %get-tuple-element.65), channel_id=1, source_target_pairs={{0,4},{1,3},{2,6},{3,1},{4,0},{5,7},{6,2},{7,5},{8,12},{9,11},{10,... | collective-permute-start | bytes 196616 | tf_op jit(solution)/shard_map/ppermute | solution.py:42
  6.3 2.0 %collective-permute-start.7 = (bf16[128,256]{1,0:T(8,128)(2,1)S(1)}, bf16[128,256]{1,0:T(8,128)(2,1)S(1)}, u32[]{:S(2)}, u32[]{:S(2)}) collective-permute-start(bf16[128,256]{1,0:T(8,128)(2,1)S(1)} %get-tuple-element.62), channel_id=1, source_target_pairs={{0,2},{1,5},{2,0},{3,7},{4,6},{5,1},{6,4},{7,3},{8,10},{9,13},{10,... | collective-permute-start | bytes 196616 | tf_op jit(solution)/shard_map/ppermute | solution.py:42
  8.3 1.5 %collective-permute-start.8 = (bf16[128,256]{1,0:T(8,128)(2,1)S(1)}, bf16[128,256]{1,0:T(8,128)(2,1)S(1)}, u32[]{:S(2)}, u32[]{:S(2)}) collective-permute-start(bf16[128,256]{1,0:T(8,128)(2,1)S(1)} %get-tuple-element.61), channel_id=1, source_target_pairs={{0,4},{1,3},{2,6},{3,1},{4,0},{5,7},{6,2},{7,5},{8,12},{9,11},{10,... | collective-permute-start | bytes 196616 | tf_op jit(solution)/shard_map/ppermute | solution.py:42
  10.1 0.7 %collective-permute-start.9 = (bf16[128,256]{1,0:T(8,128)(2,1)S(1)}, bf16[128,256]{1,0:T(8,128)(2,1)S(1)}, u32[]{:S(2)}, u32[]{:S(2)}) collective-permute-start(bf16[128,256]{1,0:T(8,128)(2,1)S(1)} %get-tuple-element.60), channel_id=1, source_target_pairs={{0,6},{1,7},{2,4},{3,5},{4,2},{5,3},{6,0},{7,1},{8,14},{9,15},{10,... | collective-permute-start | bytes 196616 | tf_op jit(solution)/shard_map/ppermute | solution.py:42
  10.8 0.6 %collective-permute-done.4 = bf16[128,256]{1,0:T(8,128)(2,1)S(1)} collective-permute-done((bf16[128,256]{1,0:T(8,128)(2,1)S(1)}, bf16[128,256]{1,0:T(8,128)(2,1)S(1)}, u32[]{:S(2)}, u32[]{:S(2)}) %collective-permute-start.4) | collective-permute-done | bytes 65568 | tf_op jit(solution)/shard_map/ppermute | solution.py:42
  11.6 1.2 %collective-permute-done.5 = bf16[128,256]{1,0:T(8,128)(2,1)S(1)} collective-permute-done((bf16[128,256]{1,0:T(8,128)(2,1)S(1)}, bf16[128,256]{1,0:T(8,128)(2,1)S(1)}, u32[]{:S(2)}, u32[]{:S(2)}) %collective-permute-start.5) | collective-permute-done | bytes 65568 | tf_op jit(solution)/shard_map/ppermute | solution.py:17
  13.0 1.6 %collective-permute-start.6 = (bf16[2,128,256]{2,1,0:T(8,128)(2,1)S(1)}, bf16[2,128,256]{2,1,0:T(8,128)(2,1)S(1)}, u32[]{:S(2)}, u32[]{:S(2)}) collective-permute-start(bf16[2,128,256]{2,1,0:T(8,128)(2,1)S(1)} %pad_maximum_fusion.6), channel_id=1, source_target_pairs={{0,8},{1,17},{2,10},{3,19},{4,12},{5,21},{6,14},{7,23},{8,0},{9,25... | collective-permute-start | bytes 393224 | tf_op jit(solution)/shard_map/ppermute | solution.py:42
  14.7 0.7 %collective-permute-done.9 = bf16[128,256]{1,0:T(8,128)(2,1)S(1)} collective-permute-done((bf16[128,256]{1,0:T(8,128)(2,1)S(1)}, bf16[128,256]{1,0:T(8,128)(2,1)S(1)}, u32[]{:S(2)}, u32[]{:S(2)}) %collective-permute-start.9) | collective-permute-done | bytes 65568 | tf_op jit(solution)/shard_map/ppermute | solution.py:42
  15.5 0.5 %collective-permute-start.10 = (bf16[128,256]{1,0:T(8,128)(2,1)S(1)}, bf16[128,256]{1,0:T(8,128)(2,1)S(1)}, u32[]{:S(2)}, u32[]{:S(2)}) collective-permute-start(bf16[128,256]{1,0:T(8,128)(2,1)S(1)} %get-tuple-element.68), channel_id=1, source_target_pairs={{0,1},{1,0},{2,3},{3,2},{4,5},{5,4},{6,7},{7,6},{8,9},{9,8},{10,11... | collective-permute-start | bytes 196616 | tf_op jit(solution)/shard_map/ppermute | solution.py:17
  16.0 0.9 %collective-permute-done.10 = bf16[128,256]{1,0:T(8,128)(2,1)S(1)} collective-permute-done((bf16[128,256]{1,0:T(8,128)(2,1)S(1)}, bf16[128,256]{1,0:T(8,128)(2,1)S(1)}, u32[]{:S(2)}, u32[]{:S(2)}) %collective-permute-start.10) | collective-permute-done | bytes 65568 | tf_op jit(solution)/shard_map/ppermute | solution.py:17
  16.9 1.6 %collective-permute-start.12 = (bf16[2,128,256]{2,1,0:T(8,128)(2,1)S(1)}, bf16[2,128,256]{2,1,0:T(8,128)(2,1)S(1)}, u32[]{:S(2)}, u32[]{:S(2)}) collective-permute-start(bf16[2,128,256]{2,1,0:T(8,128)(2,1)S(1)} %pad_maximum_fusion.7), channel_id=1, source_target_pairs={{0,8},{1,17},{2,10},{3,19},{4,12},{5,21},{6,14},{7,23},{8,0},{9,25... | collective-permute-start | bytes 393224 | tf_op jit(solution)/shard_map/ppermute | solution.py:42
  18.5 0.9 %collective-permute-done.6 = bf16[2,128,256]{2,1,0:T(8,128)(2,1)S(1)} collective-permute-done((bf16[2,128,256]{2,1,0:T(8,128)(2,1)S(1)}, bf16[2,128,256]{2,1,0:T(8,128)(2,1)S(1)}, u32[]{:S(2)}, u32[]{:S(2)}) %collective-permute-start.6) | collective-permute-done | bytes 131104 | tf_op jit(solution)/shard_map/ppermute | solution.py:42
  19.4 2.0 %collective-permute-start.11 = (bf16[2,128,256]{2,1,0:T(8,128)(2,1)S(1)}, bf16[2,128,256]{2,1,0:T(8,128)(2,1)S(1)}, u32[]{:S(2)}, u32[]{:S(2)}) collective-permute-start(bf16[2,128,256]{2,1,0:T(8,128)(2,1)S(1)} %broadcast_select_fusion.3), channel_id=1, source_target_pairs={{0,16},{1,9},{2,18},{3,11},{4,20},{5,13},{6,22},{7,15},{8,24},{9,1... | collective-permute-start | bytes 393224 | tf_op jit(solution)/shard_map/ppermute | solution.py:42
  21.4 4.0 %collective-permute-done.12 = bf16[2,128,256]{2,1,0:T(8,128)(2,1)S(1)} collective-permute-done((bf16[2,128,256]{2,1,0:T(8,128)(2,1)S(1)}, bf16[2,128,256]{2,1,0:T(8,128)(2,1)S(1)}, u32[]{:S(2)}, u32[]{:S(2)}) %collective-permute-start.12) | collective-permute-done | bytes 131104 | tf_op jit(solution)/shard_map/ppermute | solution.py:42
  25.5 0.3 collective-permute-start.14
  25.8 1.2 %convolution_convert_fusion.2 = bf16[2,512,256]{2,1,0:T(8,128)(2,1)} fusion(bf16[1,512,512]{2,1,0:T(8,128)(2,1)S(1)} %bitcast.63, bf16[1,512,512]{2,1,0:T(8,128)(2,1)S(1)} %copy-done.3, bf16[1,2,512,256]{3,2,0,1:T(8,128)(2,1)S(1)} %bitcast.61, bf16[1,2,512,256]{3,2,0,1:T(8,128)(2,1)S(1)} %bitcast.58), kind=kOutput, calls=%fused_computation.4 | convolution fusion | flops 269484032 | bytes 2621440 | tf_op jit(solution)/shard_map/ktu,kur->ktr/dot_general | solution.py:97
  27.0 1.1 %collective-permute-start.15 = (bf16[2,128,256]{2,1,0:T(8,128)(2,1)S(1)}, bf16[2,128,256]{2,1,0:T(8,128)(2,1)S(1)}, u32[]{:S(2)}, u32[]{:S(2)}) collective-permute-start(bf16[2,128,256]{2,1,0:T(8,128)(2,1)S(1)} %broadcast_select_fusion.4), channel_id=1, source_target_pairs={{0,2},{1,5},{2,0},{3,7},{4,6},{5,1},{6,4},{7,3},{8,10},{9,13},{10,... | collective-permute-start | bytes 393224 | tf_op jit(solution)/shard_map/ppermute | solution.py:42
  28.1 1.4 %collective-permute-start.16 = (bf16[2,128,256]{2,1,0:T(8,128)(2,1)S(1)}, bf16[2,128,256]{2,1,0:T(8,128)(2,1)S(1)}, u32[]{:S(2)}, u32[]{:S(2)}) collective-permute-start(bf16[2,128,256]{2,1,0:T(8,128)(2,1)S(1)} %broadcast_select_fusion.4), channel_id=1, source_target_pairs={{0,4},{1,3},{2,6},{3,1},{4,0},{5,7},{6,2},{7,5},{8,12},{9,11},{10,... | collective-permute-start | bytes 393224 | tf_op jit(solution)/shard_map/ppermute | solution.py:42
  29.5 1.1 %collective-permute-start.13 = (bf16[2,128,256]{2,1,0:T(8,128)(2,1)S(1)}, bf16[2,128,256]{2,1,0:T(8,128)(2,1)S(1)}, u32[]{:S(2)}, u32[]{:S(2)}) collective-permute-start(bf16[2,128,256]{2,1,0:T(8,128)(2,1)S(1)} %broadcast_select_fusion.4), channel_id=1, source_target_pairs={{0,6},{1,7},{2,4},{3,5},{4,2},{5,3},{6,0},{7,1},{8,14},{9,15},{10,... | collective-permute-start | bytes 393224 | tf_op jit(solution)/shard_map/ppermute | solution.py:42
  30.6 1.4 %collective-permute-done.14 = bf16[2,128,256]{2,1,0:T(8,128)(2,1)S(1)} collective-permute-done((bf16[2,128,256]{2,1,0:T(8,128)(2,1)S(1)}, bf16[2,128,256]{2,1,0:T(8,128)(2,1)S(1)}, u32[]{:S(2)}, u32[]{:S(2)}) %collective-permute-start.14) | collective-permute-done | bytes 131104 | tf_op jit(solution)/shard_map/ppermute | solution.py:42
  32.0 1.4 %collective-permute-done.15 = bf16[2,128,256]{2,1,0:T(8,128)(2,1)S(1)} collective-permute-done((bf16[2,128,256]{2,1,0:T(8,128)(2,1)S(1)}, bf16[2,128,256]{2,1,0:T(8,128)(2,1)S(1)}, u32[]{:S(2)}, u32[]{:S(2)}) %collective-permute-start.15) | collective-permute-done | bytes 131104 | tf_op jit(solution)/shard_map/ppermute | solution.py:42
  33.5 1.1 %collective-permute-start.19 = (bf16[2,128,256]{2,1,0:T(8,128)(2,1)S(1)}, bf16[2,128,256]{2,1,0:T(8,128)(2,1)S(1)}, u32[]{:S(2)}, u32[]{:S(2)}) collective-permute-start(bf16[2,128,256]{2,1,0:T(8,128)(2,1)S(1)} %broadcast_select_fusion.1), channel_id=1, source_target_pairs={{0,2},{1,5},{2,0},{3,7},{4,6},{5,1},{6,4},{7,3},{8,10},{9,13},{10,... | collective-permute-start | bytes 393224 | tf_op jit(solution)/shard_map/ppermute | solution.py:42
  34.5 1.5 %collective-permute-start.18 = (bf16[2,128,256]{2,1,0:T(8,128)(2,1)S(1)}, bf16[2,128,256]{2,1,0:T(8,128)(2,1)S(1)}, u32[]{:S(2)}, u32[]{:S(2)}) collective-permute-start(bf16[2,128,256]{2,1,0:T(8,128)(2,1)S(1)} %broadcast_select_fusion.1), channel_id=1, source_target_pairs={{0,4},{1,3},{2,6},{3,1},{4,0},{5,7},{6,2},{7,5},{8,12},{9,11},{10,... | collective-permute-start | bytes 393224 | tf_op jit(solution)/shard_map/ppermute | solution.py:42
  36.0 1.0 %collective-permute-start.17 = (bf16[2,128,256]{2,1,0:T(8,128)(2,1)S(1)}, bf16[2,128,256]{2,1,0:T(8,128)(2,1)S(1)}, u32[]{:S(2)}, u32[]{:S(2)}) collective-permute-start(bf16[2,128,256]{2,1,0:T(8,128)(2,1)S(1)} %broadcast_select_fusion.1), channel_id=1, source_target_pairs={{0,6},{1,7},{2,4},{3,5},{4,2},{5,3},{6,0},{7,1},{8,14},{9,15},{10,... | collective-permute-start | bytes 393224 | tf_op jit(solution)/shard_map/ppermute | solution.py:42
  37.1 1.7 %fusion.2 = bf16[2,256,256]{2,1,0:T(8,128)(2,1)S(1)} fusion(bf16[2,512,256]{2,1,0:T(8,128)(2,1)} %convolution_convert_fusion.2, bf16[1,512,512]{2,1,0:T(8,128)(2,1)S(1)} %bitcast.64, bf16[1,512,512]{2,1,0:T(8,128)(2,1)S(1)} %copy-done.3, bf16[2,128,256]{2,1,0:T(8,128)(2,1)S(1)} %get-tuple-element.56, bf16[2,128,256]{2,1,0:T(8,128)(2,1)S(1)} %get-tuple-element.57, ...), kind=kOutput, calls=%fused_computation.6 | convolution fusion | flops 405667840 | bytes 2359296 | tf_op jit(solution)/shard_map/ktr,kts->krs/dot_general | solution.py:116
  38.8 0.3 convolution_convert_fusion
  39.1 0.7 %collective-permute-done.19 = bf16[2,128,256]{2,1,0:T(8,128)(2,1)S(1)} collective-permute-done((bf16[2,128,256]{2,1,0:T(8,128)(2,1)S(1)}, bf16[2,128,256]{2,1,0:T(8,128)(2,1)S(1)}, u32[]{:S(2)}, u32[]{:S(2)}) %collective-permute-start.19) | collective-permute-done | bytes 131104 | tf_op jit(solution)/shard_map/ppermute | solution.py:42
  39.9 0.9 %collective-permute-done.18 = bf16[2,128,256]{2,1,0:T(8,128)(2,1)S(1)} collective-permute-done((bf16[2,128,256]{2,1,0:T(8,128)(2,1)S(1)}, bf16[2,128,256]{2,1,0:T(8,128)(2,1)S(1)}, u32[]{:S(2)}, u32[]{:S(2)}) %collective-permute-start.18) | collective-permute-done | bytes 131104 | tf_op jit(solution)/shard_map/ppermute | solution.py:42
  40.7 1.1 %collective-permute-done.17 = bf16[2,128,256]{2,1,0:T(8,128)(2,1)S(1)} collective-permute-done((bf16[2,128,256]{2,1,0:T(8,128)(2,1)S(1)}, bf16[2,128,256]{2,1,0:T(8,128)(2,1)S(1)}, u32[]{:S(2)}, u32[]{:S(2)}) %collective-permute-start.17) | collective-permute-done | bytes 131104 | tf_op jit(solution)/shard_map/ppermute | solution.py:42
  42.0 1.4 %fusion = f32[512,512]{1,0:T(8,128)} fusion(bf16[2,512,256]{2,1,0:T(8,128)(2,1)S(1)} %convolution_convert_fusion, bf16[512,512]{1,0:T(8,128)(2,1)S(1)} %copy-done.4, bf16[2,128,256]{2,1,0:T(8,128)(2,1)S(1)} %get-tuple-element.52, bf16[2,128,256]{2,1,0:T(8,128)(2,1)S(1)} %get-tuple-element.53, bf16[2,128,256]{2,1,0:T(8,128)(2,1)S(1)} %get-tuple-element.54, ...), kind=kOutput, calls=%fused_computation.1 | convolution fusion | flops 271056896 | bytes 2621440 | tf_op jit(solution)/shard_map/kts,kus->tu/dot_general | solution.py:121
  (48 shorter events, 1.0 us)
Async XLA Ops:
  1.7 4.6 %copy-start.1 = (bf16[1,1,512,256]{3,2,1,0:T(8,128)(2,1)S(1)}, bf16[1,1,512,256]{3,2,1,0:T(8,128)(2,1)}, u32[]{:S(2)}) copy-start(bf16[1,1,512,256]{3,2,1,0:T(8,128)(2,1)} %param.7) | copy-start | bytes 786436
  1.7 8.4 %collective-permute-start.2 = (bf16[128,256]{1,0:T(8,128)(2,1)S(1)}, bf16[128,256]{1,0:T(8,128)(2,1)S(1)}, u32[]{:S(2)}, u32[]{:S(2)}) collective-permute-start(bf16[128,256]{1,0:T(8,128)(2,1)S(1)} %get-tuple-element.66), channel_id=1, source_target_pairs={{0,2},{1,5},{2,0},{3,7},{4,6},{5,1},{6,4},{7,3},{8,10},{9,13},{10,... | collective-permute-start | bytes 196616 | tf_op jit(solution)/shard_map/ppermute | solution.py:42
  4.7 6.1 %collective-permute-start.3 = (bf16[128,256]{1,0:T(8,128)(2,1)S(1)}, bf16[128,256]{1,0:T(8,128)(2,1)S(1)}, u32[]{:S(2)}, u32[]{:S(2)}) collective-permute-start(bf16[128,256]{1,0:T(8,128)(2,1)S(1)} %get-tuple-element.65), channel_id=1, source_target_pairs={{0,4},{1,3},{2,6},{3,1},{4,0},{5,7},{6,2},{7,5},{8,12},{9,11},{10,... | collective-permute-start | bytes 196616 | tf_op jit(solution)/shard_map/ppermute | solution.py:42
  6.2 5.2 %collective-permute-start.4 = (bf16[128,256]{1,0:T(8,128)(2,1)S(1)}, bf16[128,256]{1,0:T(8,128)(2,1)S(1)}, u32[]{:S(2)}, u32[]{:S(2)}) collective-permute-start(bf16[128,256]{1,0:T(8,128)(2,1)S(1)} %get-tuple-element.63), channel_id=1, source_target_pairs={{0,6},{1,7},{2,4},{3,5},{4,2},{5,3},{6,0},{7,1},{8,14},{9,15},{10,... | collective-permute-start | bytes 196616 | tf_op jit(solution)/shard_map/ppermute | solution.py:42
  6.3 3.6 %copy-start = (bf16[1,1,512,256]{3,2,1,0:T(8,128)(2,1)S(1)}, bf16[1,1,512,256]{3,2,1,0:T(8,128)(2,1)}, u32[]{:S(2)}) copy-start(bf16[1,1,512,256]{3,2,1,0:T(8,128)(2,1)} %param.8) | copy-start | bytes 786436
  6.3 6.7 %collective-permute-start.7 = (bf16[128,256]{1,0:T(8,128)(2,1)S(1)}, bf16[128,256]{1,0:T(8,128)(2,1)S(1)}, u32[]{:S(2)}, u32[]{:S(2)}) collective-permute-start(bf16[128,256]{1,0:T(8,128)(2,1)S(1)} %get-tuple-element.62), channel_id=1, source_target_pairs={{0,2},{1,5},{2,0},{3,7},{4,6},{5,1},{6,4},{7,3},{8,10},{9,13},{10,... | collective-permute-start | bytes 196616 | tf_op jit(solution)/shard_map/ppermute | solution.py:42
  8.3 1.5 %copy-start.2 = (s32[2]{0:T(128)S(1)}, s32[2]{0:T(128)}, u32[]{:S(2)}) copy-start(s32[2]{0:T(128)} %param.11) | copy-start | bytes 28
  8.3 6.4 %collective-permute-start.8 = (bf16[128,256]{1,0:T(8,128)(2,1)S(1)}, bf16[128,256]{1,0:T(8,128)(2,1)S(1)}, u32[]{:S(2)}, u32[]{:S(2)}) collective-permute-start(bf16[128,256]{1,0:T(8,128)(2,1)S(1)} %get-tuple-element.61), channel_id=1, source_target_pairs={{0,4},{1,3},{2,6},{3,1},{4,0},{5,7},{6,2},{7,5},{8,12},{9,11},{10,... | collective-permute-start | bytes 196616 | tf_op jit(solution)/shard_map/ppermute | solution.py:42
  10.1 2.8 %copy-start.3 = (bf16[1,512,512]{2,1,0:T(8,128)(2,1)S(1)}, bf16[1,512,512]{2,1,0:T(8,128)(2,1)}, u32[]{:S(2)}) copy-start(bf16[1,512,512]{2,1,0:T(8,128)(2,1)} %param.9) | copy-start | bytes 1572868
  10.1 5.2 %collective-permute-start.9 = (bf16[128,256]{1,0:T(8,128)(2,1)S(1)}, bf16[128,256]{1,0:T(8,128)(2,1)S(1)}, u32[]{:S(2)}, u32[]{:S(2)}) collective-permute-start(bf16[128,256]{1,0:T(8,128)(2,1)S(1)} %get-tuple-element.60), channel_id=1, source_target_pairs={{0,6},{1,7},{2,4},{3,5},{4,2},{5,3},{6,0},{7,1},{8,14},{9,15},{10,... | collective-permute-start | bytes 196616 | tf_op jit(solution)/shard_map/ppermute | solution.py:42
  10.8 15.0 %collective-permute-start = (bf16[2,512,256]{2,1,0:T(8,128)(2,1)S(1)}, bf16[2,512,256]{2,1,0:T(8,128)(2,1)S(1)}, u32[]{:S(2)}, u32[]{:S(2)}) collective-permute-start(bf16[2,512,256]{2,1,0:T(8,128)(2,1)S(1)} %pad_maximum_fusion.5), channel_id=1, source_target_pairs={{0,1},{1,0},{2,3},{3,2},{4,5},{5,4},{6,7},{7,6},{8,9},{9,8},{10,11... | collective-permute-start | bytes 1572872 | tf_op jit(solution)/shard_map/ppermute | solution.py:17
  11.5 1.3 %collective-permute-start.5 = (bf16[128,256]{1,0:T(8,128)(2,1)S(1)}, bf16[128,256]{1,0:T(8,128)(2,1)S(1)}, u32[]{:S(2)}, u32[]{:S(2)}) collective-permute-start(bf16[128,256]{1,0:T(8,128)(2,1)S(1)} %get-tuple-element.70), channel_id=1, source_target_pairs={{0,1},{1,0},{2,3},{3,2},{4,5},{5,4},{6,7},{7,6},{8,9},{9,8},{10,11... | collective-permute-start | bytes 196616 | tf_op jit(solution)/shard_map/ppermute | solution.py:17
  12.8 12.9 %collective-permute-start.1 = (bf16[512,512]{1,0:T(8,128)(2,1)S(1)}, bf16[512,512]{1,0:T(8,128)(2,1)S(1)}, u32[]{:S(2)}, u32[]{:S(2)}) collective-permute-start(bf16[512,512]{1,0:T(8,128)(2,1)S(1)} %bitcast.60), channel_id=1, source_target_pairs={{0,1},{1,0},{2,3},{3,2},{4,5},{5,4},{6,7},{7,6},{8,9},{9,8},{10,11... | collective-permute-start | bytes 1572872 | tf_op jit(solution)/shard_map/ppermute | solution.py:17
  13.0 6.4 %collective-permute-start.6 = (bf16[2,128,256]{2,1,0:T(8,128)(2,1)S(1)}, bf16[2,128,256]{2,1,0:T(8,128)(2,1)S(1)}, u32[]{:S(2)}, u32[]{:S(2)}) collective-permute-start(bf16[2,128,256]{2,1,0:T(8,128)(2,1)S(1)} %pad_maximum_fusion.6), channel_id=1, source_target_pairs={{0,8},{1,17},{2,10},{3,19},{4,12},{5,21},{6,14},{7,23},{8,0},{9,25... | collective-permute-start | bytes 393224 | tf_op jit(solution)/shard_map/ppermute | solution.py:42
  15.5 1.4 %collective-permute-start.10 = (bf16[128,256]{1,0:T(8,128)(2,1)S(1)}, bf16[128,256]{1,0:T(8,128)(2,1)S(1)}, u32[]{:S(2)}, u32[]{:S(2)}) collective-permute-start(bf16[128,256]{1,0:T(8,128)(2,1)S(1)} %get-tuple-element.68), channel_id=1, source_target_pairs={{0,1},{1,0},{2,3},{3,2},{4,5},{5,4},{6,7},{7,6},{8,9},{9,8},{10,11... | collective-permute-start | bytes 196616 | tf_op jit(solution)/shard_map/ppermute | solution.py:17
  16.9 8.6 %collective-permute-start.12 = (bf16[2,128,256]{2,1,0:T(8,128)(2,1)S(1)}, bf16[2,128,256]{2,1,0:T(8,128)(2,1)S(1)}, u32[]{:S(2)}, u32[]{:S(2)}) collective-permute-start(bf16[2,128,256]{2,1,0:T(8,128)(2,1)S(1)} %pad_maximum_fusion.7), channel_id=1, source_target_pairs={{0,8},{1,17},{2,10},{3,19},{4,12},{5,21},{6,14},{7,23},{8,0},{9,25... | collective-permute-start | bytes 393224 | tf_op jit(solution)/shard_map/ppermute | solution.py:42
  19.4 7.6 %collective-permute-start.11 = (bf16[2,128,256]{2,1,0:T(8,128)(2,1)S(1)}, bf16[2,128,256]{2,1,0:T(8,128)(2,1)S(1)}, u32[]{:S(2)}, u32[]{:S(2)}) collective-permute-start(bf16[2,128,256]{2,1,0:T(8,128)(2,1)S(1)} %broadcast_select_fusion.3), channel_id=1, source_target_pairs={{0,16},{1,9},{2,18},{3,11},{4,20},{5,13},{6,22},{7,15},{8,24},{9,1... | collective-permute-start | bytes 393224 | tf_op jit(solution)/shard_map/ppermute | solution.py:42
  25.5 6.6 %collective-permute-start.14 = (bf16[2,128,256]{2,1,0:T(8,128)(2,1)S(1)}, bf16[2,128,256]{2,1,0:T(8,128)(2,1)S(1)}, u32[]{:S(2)}, u32[]{:S(2)}) collective-permute-start(bf16[2,128,256]{2,1,0:T(8,128)(2,1)S(1)} %broadcast_select_fusion.2), channel_id=1, source_target_pairs={{0,16},{1,9},{2,18},{3,11},{4,20},{5,13},{6,22},{7,15},{8,24},{9,1... | collective-permute-start | bytes 393224 | tf_op jit(solution)/shard_map/ppermute | solution.py:42
  27.0 6.4 %collective-permute-start.15 = (bf16[2,128,256]{2,1,0:T(8,128)(2,1)S(1)}, bf16[2,128,256]{2,1,0:T(8,128)(2,1)S(1)}, u32[]{:S(2)}, u32[]{:S(2)}) collective-permute-start(bf16[2,128,256]{2,1,0:T(8,128)(2,1)S(1)} %broadcast_select_fusion.4), channel_id=1, source_target_pairs={{0,2},{1,5},{2,0},{3,7},{4,6},{5,1},{6,4},{7,3},{8,10},{9,13},{10,... | collective-permute-start | bytes 393224 | tf_op jit(solution)/shard_map/ppermute | solution.py:42
  28.1 8.9 %collective-permute-start.16 = (bf16[2,128,256]{2,1,0:T(8,128)(2,1)S(1)}, bf16[2,128,256]{2,1,0:T(8,128)(2,1)S(1)}, u32[]{:S(2)}, u32[]{:S(2)}) collective-permute-start(bf16[2,128,256]{2,1,0:T(8,128)(2,1)S(1)} %broadcast_select_fusion.4), channel_id=1, source_target_pairs={{0,4},{1,3},{2,6},{3,1},{4,0},{5,7},{6,2},{7,5},{8,12},{9,11},{10,... | collective-permute-start | bytes 393224 | tf_op jit(solution)/shard_map/ppermute | solution.py:42
  29.5 7.5 %collective-permute-start.13 = (bf16[2,128,256]{2,1,0:T(8,128)(2,1)S(1)}, bf16[2,128,256]{2,1,0:T(8,128)(2,1)S(1)}, u32[]{:S(2)}, u32[]{:S(2)}) collective-permute-start(bf16[2,128,256]{2,1,0:T(8,128)(2,1)S(1)} %broadcast_select_fusion.4), channel_id=1, source_target_pairs={{0,6},{1,7},{2,4},{3,5},{4,2},{5,3},{6,0},{7,1},{8,14},{9,15},{10,... | collective-permute-start | bytes 393224 | tf_op jit(solution)/shard_map/ppermute | solution.py:42
  33.5 6.4 %collective-permute-start.19 = (bf16[2,128,256]{2,1,0:T(8,128)(2,1)S(1)}, bf16[2,128,256]{2,1,0:T(8,128)(2,1)S(1)}, u32[]{:S(2)}, u32[]{:S(2)}) collective-permute-start(bf16[2,128,256]{2,1,0:T(8,128)(2,1)S(1)} %broadcast_select_fusion.1), channel_id=1, source_target_pairs={{0,2},{1,5},{2,0},{3,7},{4,6},{5,1},{6,4},{7,3},{8,10},{9,13},{10,... | collective-permute-start | bytes 393224 | tf_op jit(solution)/shard_map/ppermute | solution.py:42
  34.5 6.2 %collective-permute-start.18 = (bf16[2,128,256]{2,1,0:T(8,128)(2,1)S(1)}, bf16[2,128,256]{2,1,0:T(8,128)(2,1)S(1)}, u32[]{:S(2)}, u32[]{:S(2)}) collective-permute-start(bf16[2,128,256]{2,1,0:T(8,128)(2,1)S(1)} %broadcast_select_fusion.1), channel_id=1, source_target_pairs={{0,4},{1,3},{2,6},{3,1},{4,0},{5,7},{6,2},{7,5},{8,12},{9,11},{10,... | collective-permute-start | bytes 393224 | tf_op jit(solution)/shard_map/ppermute | solution.py:42
  36.0 5.9 %collective-permute-start.17 = (bf16[2,128,256]{2,1,0:T(8,128)(2,1)S(1)}, bf16[2,128,256]{2,1,0:T(8,128)(2,1)S(1)}, u32[]{:S(2)}, u32[]{:S(2)}) collective-permute-start(bf16[2,128,256]{2,1,0:T(8,128)(2,1)S(1)} %broadcast_select_fusion.1), channel_id=1, source_target_pairs={{0,6},{1,7},{2,4},{3,5},{4,2},{5,3},{6,0},{7,1},{8,14},{9,15},{10,... | collective-permute-start | bytes 393224 | tf_op jit(solution)/shard_map/ppermute | solution.py:42
  39.1 2.8 %copy-start.4 = (bf16[512,512]{1,0:T(8,128)(2,1)S(1)}, bf16[512,512]{1,0:T(8,128)(2,1)}, u32[]{:S(2)}) copy-start(bf16[512,512]{1,0:T(8,128)(2,1)} %param.6) | copy-start | bytes 1572868

commit v3 on v2

--- a/solution.py
+++ b/solution.py
@@ -6,7 +6,8 @@
 from jax.sharding import PartitionSpec as P
 
 LOW = 2
-FAN = ((1, 2), (2, 1), (3, 3))
+FAN = ((1, 1), (2, 2), (3, 3))
+BACK = ((1, 2), (2, 1), (3, 3))
 
 
 def after(value, earlier):
@@ -42,14 +43,14 @@
         return lax.ppermute(block, ("row", "col"), pairs)
 
     def scatter_start(self, block):
-        height, width = block.shape
-        parts = block.reshape(1 << LOW, height >> LOW, width)
-        part = functools.partial(lax.dynamic_index_in_dim, parts, axis=0, keepdims=False)
+        n, height, width = block.shape
+        parts = block.reshape(n, 1 << LOW, height >> LOW, width)
+        part = functools.partial(lax.dynamic_index_in_dim, parts, axis=1, keepdims=False)
         sent = [part(self.place ^ self.of(masks)) for masks in FAN]
         return part(self.place), [self.cross(block, masks) for block, masks in zip(sent, FAN)], sent
 
     def scatter_end(self, slots, came):
-        low = (self.apart & ((1 << LOW) - 1))[:, None, :]
+        low = (self.apart & ((1 << LOW) - 1))[:, None, None, :]
         for masks, block in zip(FAN, came):
             slots = jnp.where(low == self.of(masks), block, slots)
         return slots
@@ -67,10 +68,10 @@
         return jnp.roll(lax.all_to_all(slots, "col", 0, 0, tiled=True), -self.col, axis=0)
 
     def gather_start(self, held):
-        return [held, *(self.cross(held, masks) for masks in FAN)]
+        return [held, *(self.cross(held, masks) for masks in BACK)]
 
     def gather_end(self, parts):
-        masks = [self.of(masks) for masks in FAN]
+        masks = [self.of(masks) for masks in BACK]
         whole = []
         for q in range(1 << LOW):
             part = parts[0]
@@ -87,18 +88,19 @@
     keep = jnp.arange(rank_max, dtype=jnp.int32) < ranks[0, 0]
     right = jnp.where(keep[None, :], w_factor[0, 0], jnp.zeros((), jnp.bfloat16))
     first, second = (Paths(rows, cols, c, rank_max) for c in (col_rows, after(col_rows, left)))
-    one, came_one, _ = first.scatter_start(right)
-    two, came_two, sent = second.scatter_start(left)
+    both = jnp.stack([right, left])
+    slots, came, sent = first.scatter_start(both)
 
-    own = all_panels(after(jnp.stack([right, left]), sent), cols, col)
+    own = all_panels(after(both, sent), cols, col)
     inverse = all_panels(after(inverse, sent), cols, col)
     right, left = own[:, 0], own[:, 1]
     solve = functools.partial(jnp.einsum, "ktu,kur->ktr", preferred_element_type=jnp.float32)
     solved = solve(inverse, right).astype(jnp.bfloat16)
+    base = trailing.astype(jnp.float32)
 
-    one = first.own_columns(first.scatter_end(one, after(came_one, sent)))
+    both = first.own_columns(first.scatter_end(slots, came))
+    one, two = both[:, 0], both[:, 1]
     came_one = first.cross(one, first.high[0])
-    two = second.own_columns(second.scatter_end(two, after(came_two, one)))
     came_two = second.cross(two, second.high[0])
     last = len(first.high) - 1
     for step in range(last):
@@ -106,9 +108,9 @@
         came_one = first.cross(one, first.high[step + 1])
         two = second.spread(two, after(came_two, one), step)
         came_two = second.cross(two, second.high[step + 1])
-    one = first.spread(one, after(came_one, (two, solved)), last)
+    one = first.spread(one, after(came_one, (two, solved, base)), last)
     parts_one = first.gather_start(one)
-    two = second.spread(two, after(came_two, parts_one[1]), last)
+    two = second.spread(two, after(came_two, one), last)
     parts_two = second.gather_start(two)
 
     right_col = first.gather_end([after(part, two) for part in parts_one])
@@ -119,7 +121,7 @@
     mixed = mixed.astype(jnp.bfloat16)
     left_col = second.gather_end([after(part, mixed) for part in parts_two])
     change = jnp.einsum("kts,kus->tu", mixed, left_col, preferred_element_type=jnp.float32)
-    return trailing.astype(jnp.float32) - change
+    return base - change
 
 
 def solution(mesh):

time: 43.6 us -> 42.1 us (0.966)
  starting transfers between devices: 22.1 us -> 17.3 us
  waiting for transfers between devices: 14 us -> 15.8 us
  local copies, waits for them, and re-layouts: 0.07 us -> 1.57 us
    ppermute x16 -> x13, starting transfers between devices: 21.4 us -> 17.2 us  [cross(): return lax.ppermute(block, ('row', 'col'), pairs)]
    ppermute x16 -> x13, waiting for transfers between devices: 11.8 us -> 14.6 us  [cross(): return lax.ppermute(block, ('row', 'col'), pairs)]
    unnamed x10, local copies, waits for them, and re-layouts: 0.03 us -> 1.57 us
    ppermute x4 -> x3, waiting for transfers between devices: 2.13 us -> 1.23 us  [swap_cols(): return lax.ppermute(block, 'col', [(0, 1), (1, 0)])]
    ppermute x4 -> x3, starting transfers between devices: 0.72 us -> 0.14 us  [swap_cols(): return lax.ppermute(block, 'col', [(0, 1), (1, 0)])]
  transfers between devices with their start and end apart: 20 -> 16, of which waited for: 11 -> 12; matrix products, arithmetic and copies ran while one was open for 9% -> 9% of each run, Pallas kernels for 0% -> 0%
where the time goes in v3:
time: 42.1 us; the launch traced here: 41.9 us
  starting transfers between devices  17.3 us (41%)
  waiting for transfers between devices  15.8 us (38%)
  matrix products  4.66 us (11%)
  other arithmetic  1.65 us (4%)
  local copies, waits for them, and re-layouts  1.57 us (4%)
  between operations  0.88 us (2%)
    ppermute x13, starting transfers between devices, cross(): return lax.ppermute(block, ('row', 'col'), pairs)  17.2 us
    ppermute x13, waiting for transfers between devices, cross(): return lax.ppermute(block, ('row', 'col'), pairs)  14.6 us
    dot_general x1, matrix products, local(): jnp.einsum('ktr,kts->krs', solved, solved_col, preferred_element_type=jnp...  1.69 us
    unnamed x10, local copies, waits for them, and re-layouts  1.57 us
    dot_general x1, matrix products, local(): jnp.einsum('kts,kus->tu', mixed, left_col, preferred_element_type=jnp.flo...  1.44 us
    dot_general x1, matrix products, local(): solved = solve(inverse, right).astype(jnp.bfloat16)  1.24 us
    ppermute x3, waiting for transfers between devices, swap_cols(): return lax.ppermute(block, 'col', [(0, 1), (1, 0)])  1.23 us
    select_n x2, other arithmetic, local(): jnp.where(keep[None, :], w_factor[0, 0], jnp.zeros((), jnp.bfloat16))  1.04 us
  transfers between devices with their start and end apart: 16, of which 12 were waited for; matrix products, arithmetic and copies ran while one was open for 9% of the time, Pallas kernels for 0%

profile of v3, /device:TPU:0, one launch (start us, length us, event | category | flops | bytes accessed | tf_op | source)
XLA Modules:
  0.0 41.9 jit_solution(5076527628542759254)
XLA Ops:
  0.7 1.0 %broadcast_select_fusion = bf16[1,4,128,256]{3,2,1,0:T(8,128)(2,1)S(1)} fusion(bf16[1,4,128,256]{3,2,1,0:T(8,128)(2,1)} %bitcast.44, pred[256]{0:T(512)(128)(4,1)S(1)} %iota_compare_fusion), kind=kLoop, calls=%fused_computation.42 | loop fusion | flops 131072 | bytes 524544 | tf_op jit(solution)/shard_map/jit(_where)/select_n | solution.py:89
  1.8 4.0 %collective-permute-start.2 = (bf16[2,128,256]{2,1,0:T(8,128)(2,1)S(1)}, bf16[2,128,256]{2,1,0:T(8,128)(2,1)S(1)}, u32[]{:S(2)}, u32[]{:S(2)}) collective-permute-start(bf16[2,128,256]{2,1,0:T(8,128)(2,1)S(1)} %get-tuple-element.48), channel_id=1, source_target_pairs={{0,6},{1,7},{2,4},{3,5},{4,2},{5,3},{6,0},{7,1},{8,14},{9,15},{10,... | collective-permute-start | bytes 393224 | tf_op jit(solution)/shard_map/ppermute | solution.py:43
  5.8 0.5 %collective-permute-start.3 = (bf16[2,128,256]{2,1,0:T(8,128)(2,1)S(1)}, bf16[2,128,256]{2,1,0:T(8,128)(2,1)S(1)}, u32[]{:S(2)}, u32[]{:S(2)}) collective-permute-start(bf16[2,128,256]{2,1,0:T(8,128)(2,1)S(1)} %get-tuple-element.47), channel_id=1, source_target_pairs={{0,4},{1,5},{2,6},{3,7},{4,0},{5,1},{6,2},{7,3},{8,12},{9,13},{10,... | collective-permute-start | bytes 393224 | tf_op jit(solution)/shard_map/ppermute | solution.py:43
  6.3 0.1 collective-permute-start.4
  6.6 0.9 %copy-done.3 = bf16[1,512,512]{2,1,0:T(8,128)(2,1)S(1)} copy-done((bf16[1,512,512]{2,1,0:T(8,128)(2,1)S(1)}, bf16[1,512,512]{2,1,0:T(8,128)(2,1)}, u32[]{:S(2)}) %copy-start.3) | copy-done | bytes 524312
  7.5 0.7 %copy-done.2 = s32[2]{0:T(128)S(1)} copy-done((s32[2]{0:T(128)S(1)}, s32[2]{0:T(128)}, u32[]{:S(2)}) %copy-start.2) | copy-done | bytes 32
  8.2 1.5 %collective-permute-done.2 = bf16[2,128,256]{2,1,0:T(8,128)(2,1)S(1)} collective-permute-done((bf16[2,128,256]{2,1,0:T(8,128)(2,1)S(1)}, bf16[2,128,256]{2,1,0:T(8,128)(2,1)S(1)}, u32[]{:S(2)}, u32[]{:S(2)}) %collective-permute-start.2) | collective-permute-done | bytes 131104 | tf_op jit(solution)/shard_map/ppermute | solution.py:43
  9.7 2.4 %collective-permute-done.3 = bf16[2,128,256]{2,1,0:T(8,128)(2,1)S(1)} collective-permute-done((bf16[2,128,256]{2,1,0:T(8,128)(2,1)S(1)}, bf16[2,128,256]{2,1,0:T(8,128)(2,1)S(1)}, u32[]{:S(2)}, u32[]{:S(2)}) %collective-permute-start.3) | collective-permute-done | bytes 131104 | tf_op jit(solution)/shard_map/ppermute | solution.py:43
  12.1 0.2 collective-permute-done.4
  12.3 0.1 select_select_fusion
  12.7 1.2 %collective-permute-done.5 = bf16[2,128,256]{2,1,0:T(8,128)(2,1)S(1)} collective-permute-done((bf16[2,128,256]{2,1,0:T(8,128)(2,1)S(1)}, bf16[2,128,256]{2,1,0:T(8,128)(2,1)S(1)}, u32[]{:S(2)}, u32[]{:S(2)}) %collective-permute-start.5) | collective-permute-done | bytes 131104 | tf_op jit(solution)/shard_map/ppermute | solution.py:18
  13.9 1.6 %collective-permute-start.6 = (bf16[2,128,256]{2,1,0:T(8,128)(2,1)S(1)}, bf16[2,128,256]{2,1,0:T(8,128)(2,1)S(1)}, u32[]{:S(2)}, u32[]{:S(2)}) collective-permute-start(bf16[2,128,256]{2,1,0:T(8,128)(2,1)S(1)} %get-tuple-element.50), channel_id=1, source_target_pairs={{0,8},{1,17},{2,10},{3,19},{4,12},{5,21},{6,14},{7,23},{8,0},{9,25... | collective-permute-start | bytes 393224 | tf_op jit(solution)/shard_map/ppermute | solution.py:43
  15.6 0.4 %collective-permute-start.8 = (bf16[2,128,256]{2,1,0:T(8,128)(2,1)S(1)}, bf16[2,128,256]{2,1,0:T(8,128)(2,1)S(1)}, u32[]{:S(2)}, u32[]{:S(2)}) collective-permute-start(bf16[2,128,256]{2,1,0:T(8,128)(2,1)S(1)} %get-tuple-element.49), channel_id=1, source_target_pairs={{0,8},{1,17},{2,10},{3,19},{4,12},{5,21},{6,14},{7,23},{8,0},{9,25... | collective-permute-start | bytes 393224 | tf_op jit(solution)/shard_map/ppermute | solution.py:43
  16.0 4.3 %collective-permute-done.6 = bf16[2,128,256]{2,1,0:T(8,128)(2,1)S(1)} collective-permute-done((bf16[2,128,256]{2,1,0:T(8,128)(2,1)S(1)}, bf16[2,128,256]{2,1,0:T(8,128)(2,1)S(1)}, u32[]{:S(2)}, u32[]{:S(2)}) %collective-permute-start.6) | collective-permute-done | bytes 131104 | tf_op jit(solution)/shard_map/ppermute | solution.py:43
  20.3 2.2 %collective-permute-start.7 = (bf16[2,128,256]{2,1,0:T(8,128)(2,1)S(1)}, bf16[2,128,256]{2,1,0:T(8,128)(2,1)S(1)}, u32[]{:S(2)}, u32[]{:S(2)}) collective-permute-start(bf16[2,128,256]{2,1,0:T(8,128)(2,1)S(1)} %broadcast_select_fusion.3), channel_id=1, source_target_pairs={{0,16},{1,9},{2,18},{3,11},{4,20},{5,13},{6,22},{7,15},{8,24},{9,1... | collective-permute-start | bytes 393224 | tf_op jit(solution)/shard_map/ppermute | solution.py:43
  22.5 0.8 %collective-permute-done.8 = bf16[2,128,256]{2,1,0:T(8,128)(2,1)S(1)} collective-permute-done((bf16[2,128,256]{2,1,0:T(8,128)(2,1)S(1)}, bf16[2,128,256]{2,1,0:T(8,128)(2,1)S(1)}, u32[]{:S(2)}, u32[]{:S(2)}) %collective-permute-start.8) | collective-permute-done | bytes 131104 | tf_op jit(solution)/shard_map/ppermute | solution.py:43
  23.3 1.6 %collective-permute-start.10 = (bf16[2,128,256]{2,1,0:T(8,128)(2,1)S(1)}, bf16[2,128,256]{2,1,0:T(8,128)(2,1)S(1)}, u32[]{:S(2)}, u32[]{:S(2)}) collective-permute-start(bf16[2,128,256]{2,1,0:T(8,128)(2,1)S(1)} %broadcast_select_fusion.2), channel_id=1, source_target_pairs={{0,16},{1,9},{2,18},{3,11},{4,20},{5,13},{6,22},{7,15},{8,24},{9,1... | collective-permute-start | bytes 393224 | tf_op jit(solution)/shard_map/ppermute | solution.py:43
  24.9 1.2 %convolution_convert_fusion.2 = bf16[2,512,256]{2,1,0:T(8,128)(2,1)} fusion(bf16[1,512,512]{2,1,0:T(8,128)(2,1)S(1)} %bitcast.53, bf16[1,512,512]{2,1,0:T(8,128)(2,1)S(1)} %copy-done.3, bf16[1,2,512,256]{3,2,0,1:T(8,128)(2,1)S(1)} %bitcast.51, bf16[1,2,512,256]{3,2,0,1:T(8,128)(2,1)S(1)} %bitcast.47), kind=kOutput, calls=%fused_computation.4 | convolution fusion | flops 269484032 | bytes 2621440 | tf_op jit(solution)/shard_map/ktu,kur->ktr/dot_general | solution.py:98
  26.1 0.6 %collective-permute-done.7 = bf16[2,128,256]{2,1,0:T(8,128)(2,1)S(1)} collective-permute-done((bf16[2,128,256]{2,1,0:T(8,128)(2,1)S(1)}, bf16[2,128,256]{2,1,0:T(8,128)(2,1)S(1)}, u32[]{:S(2)}, u32[]{:S(2)}) %collective-permute-start.7) | collective-permute-done | bytes 131104 | tf_op jit(solution)/shard_map/ppermute | solution.py:43
  26.8 1.6 %collective-permute-start.12 = (bf16[2,128,256]{2,1,0:T(8,128)(2,1)S(1)}, bf16[2,128,256]{2,1,0:T(8,128)(2,1)S(1)}, u32[]{:S(2)}, u32[]{:S(2)}) collective-permute-start(bf16[2,128,256]{2,1,0:T(8,128)(2,1)S(1)} %broadcast_select_fusion.4), channel_id=1, source_target_pairs={{0,2},{1,5},{2,0},{3,7},{4,6},{5,1},{6,4},{7,3},{8,10},{9,13},{10,... | collective-permute-start | bytes 393224 | tf_op jit(solution)/shard_map/ppermute | solution.py:43
  28.4 0.4 %collective-permute-start.11 = (bf16[2,128,256]{2,1,0:T(8,128)(2,1)S(1)}, bf16[2,128,256]{2,1,0:T(8,128)(2,1)S(1)}, u32[]{:S(2)}, u32[]{:S(2)}) collective-permute-start(bf16[2,128,256]{2,1,0:T(8,128)(2,1)S(1)} %broadcast_select_fusion.4), channel_id=1, source_target_pairs={{0,4},{1,3},{2,6},{3,1},{4,0},{5,7},{6,2},{7,5},{8,12},{9,11},{10,... | collective-permute-start | bytes 393224 | tf_op jit(solution)/shard_map/ppermute | solution.py:43
  28.8 1.5 %collective-permute-start.9 = (bf16[2,128,256]{2,1,0:T(8,128)(2,1)S(1)}, bf16[2,128,256]{2,1,0:T(8,128)(2,1)S(1)}, u32[]{:S(2)}, u32[]{:S(2)}) collective-permute-start(bf16[2,128,256]{2,1,0:T(8,128)(2,1)S(1)} %broadcast_select_fusion.4), channel_id=1, source_target_pairs={{0,6},{1,7},{2,4},{3,5},{4,2},{5,3},{6,0},{7,1},{8,14},{9,15},{10,... | collective-permute-start | bytes 393224 | tf_op jit(solution)/shard_map/ppermute | solution.py:43
  30.3 0.3 collective-permute-done.10
  30.7 1.6 %collective-permute-start.15 = (bf16[2,128,256]{2,1,0:T(8,128)(2,1)S(1)}, bf16[2,128,256]{2,1,0:T(8,128)(2,1)S(1)}, u32[]{:S(2)}, u32[]{:S(2)}) collective-permute-start(bf16[2,128,256]{2,1,0:T(8,128)(2,1)S(1)} %broadcast_select_fusion.1), channel_id=1, source_target_pairs={{0,2},{1,5},{2,0},{3,7},{4,6},{5,1},{6,4},{7,3},{8,10},{9,13},{10,... | collective-permute-start | bytes 393224 | tf_op jit(solution)/shard_map/ppermute | solution.py:43
  32.4 0.8 %collective-permute-done.12 = bf16[2,128,256]{2,1,0:T(8,128)(2,1)S(1)} collective-permute-done((bf16[2,128,256]{2,1,0:T(8,128)(2,1)S(1)}, bf16[2,128,256]{2,1,0:T(8,128)(2,1)S(1)}, u32[]{:S(2)}, u32[]{:S(2)}) %collective-permute-start.12) | collective-permute-done | bytes 131104 | tf_op jit(solution)/shard_map/ppermute | solution.py:43
  33.2 1.4 %collective-permute-start.13 = (bf16[2,128,256]{2,1,0:T(8,128)(2,1)S(1)}, bf16[2,128,256]{2,1,0:T(8,128)(2,1)S(1)}, u32[]{:S(2)}, u32[]{:S(2)}) collective-permute-start(bf16[2,128,256]{2,1,0:T(8,128)(2,1)S(1)} %broadcast_select_fusion.1), channel_id=1, source_target_pairs={{0,6},{1,7},{2,4},{3,5},{4,2},{5,3},{6,0},{7,1},{8,14},{9,15},{10,... | collective-permute-start | bytes 393224 | tf_op jit(solution)/shard_map/ppermute | solution.py:43
  34.7 0.7 %collective-permute-done.11 = bf16[2,128,256]{2,1,0:T(8,128)(2,1)S(1)} collective-permute-done((bf16[2,128,256]{2,1,0:T(8,128)(2,1)S(1)}, bf16[2,128,256]{2,1,0:T(8,128)(2,1)S(1)}, u32[]{:S(2)}, u32[]{:S(2)}) %collective-permute-start.11) | collective-permute-done | bytes 131104 | tf_op jit(solution)/shard_map/ppermute | solution.py:43
  35.4 1.6 %collective-permute-done.9 = bf16[2,128,256]{2,1,0:T(8,128)(2,1)S(1)} collective-permute-done((bf16[2,128,256]{2,1,0:T(8,128)(2,1)S(1)}, bf16[2,128,256]{2,1,0:T(8,128)(2,1)S(1)}, u32[]{:S(2)}, u32[]{:S(2)}) %collective-permute-start.9) | collective-permute-done | bytes 131104 | tf_op jit(solution)/shard_map/ppermute | solution.py:43
  37.1 1.7 %fusion.2 = bf16[2,256,256]{2,1,0:T(8,128)(2,1)S(1)} fusion(bf16[2,512,256]{2,1,0:T(8,128)(2,1)} %convolution_convert_fusion.2, bf16[1,512,512]{2,1,0:T(8,128)(2,1)S(1)} %bitcast.54, bf16[1,512,512]{2,1,0:T(8,128)(2,1)S(1)} %copy-done.3, bf16[2,128,256]{2,1,0:T(8,128)(2,1)S(1)} %get-tuple-element.42, bf16[2,128,256]{2,1,0:T(8,128)(2,1)S(1)} %get-tuple-element.43, ...), kind=kOutput, calls=%fused_computation.6 | convolution fusion | flops 405667840 | bytes 2359296 | tf_op jit(solution)/shard_map/ktr,kts->krs/dot_general | solution.py:118
  38.8 0.3 convolution_convert_fusion
  39.1 1.3 %collective-permute-done.13 = bf16[2,128,256]{2,1,0:T(8,128)(2,1)S(1)} collective-permute-done((bf16[2,128,256]{2,1,0:T(8,128)(2,1)S(1)}, bf16[2,128,256]{2,1,0:T(8,128)(2,1)S(1)}, u32[]{:S(2)}, u32[]{:S(2)}) %collective-permute-start.13) | collective-permute-done | bytes 131104 | tf_op jit(solution)/shard_map/ppermute | solution.py:43
  40.4 1.4 %fusion = f32[512,512]{1,0:T(8,128)} fusion(bf16[2,512,256]{2,1,0:T(8,128)(2,1)S(1)} %convolution_convert_fusion, bf16[2,128,256]{2,1,0:T(8,128)(2,1)S(1)} %get-tuple-element.38, bf16[2,128,256]{2,1,0:T(8,128)(2,1)S(1)} %get-tuple-element.39, bf16[2,128,256]{2,1,0:T(8,128)(2,1)S(1)} %get-tuple-element.40, bf16[2,128,256]{2,1,0:T(8,128)(2,1)S(1)} %get-tuple-element.37, ...), kind=kOutput, calls=%fused_computation.1 | convolution fusion | flops 271056896 | bytes 2621440 | tf_op jit(solution)/shard_map/kts,kus->tu/dot_general | solution.py:123
  (34 shorter events, 0.8 us)
Async XLA Ops:
  0.7 1.0 %copy-start.1 = (bf16[1,1,512,256]{3,2,1,0:T(8,128)(2,1)S(1)}, bf16[1,1,512,256]{3,2,1,0:T(8,128)(2,1)}, u32[]{:S(2)}) copy-start(bf16[1,1,512,256]{3,2,1,0:T(8,128)(2,1)} %param.7) | copy-start | bytes 786436
  1.7 4.7 %copy-start = (bf16[1,1,512,256]{3,2,1,0:T(8,128)(2,1)S(1)}, bf16[1,1,512,256]{3,2,1,0:T(8,128)(2,1)}, u32[]{:S(2)}) copy-start(bf16[1,1,512,256]{3,2,1,0:T(8,128)(2,1)} %param.8) | copy-start | bytes 786436
  1.8 7.9 %collective-permute-start.2 = (bf16[2,128,256]{2,1,0:T(8,128)(2,1)S(1)}, bf16[2,128,256]{2,1,0:T(8,128)(2,1)S(1)}, u32[]{:S(2)}, u32[]{:S(2)}) collective-permute-start(bf16[2,128,256]{2,1,0:T(8,128)(2,1)S(1)} %get-tuple-element.48), channel_id=1, source_target_pairs={{0,6},{1,7},{2,4},{3,5},{4,2},{5,3},{6,0},{7,1},{8,14},{9,15},{10,... | collective-permute-start | bytes 393224 | tf_op jit(solution)/shard_map/ppermute | solution.py:43
  5.8 6.3 %collective-permute-start.3 = (bf16[2,128,256]{2,1,0:T(8,128)(2,1)S(1)}, bf16[2,128,256]{2,1,0:T(8,128)(2,1)S(1)}, u32[]{:S(2)}, u32[]{:S(2)}) collective-permute-start(bf16[2,128,256]{2,1,0:T(8,128)(2,1)S(1)} %get-tuple-element.47), channel_id=1, source_target_pairs={{0,4},{1,5},{2,6},{3,7},{4,0},{5,1},{6,2},{7,3},{8,12},{9,13},{10,... | collective-permute-start | bytes 393224 | tf_op jit(solution)/shard_map/ppermute | solution.py:43
  6.3 6.0 %collective-permute-start.4 = (bf16[2,128,256]{2,1,0:T(8,128)(2,1)S(1)}, bf16[2,128,256]{2,1,0:T(8,128)(2,1)S(1)}, u32[]{:S(2)}, u32[]{:S(2)}) collective-permute-start(bf16[2,128,256]{2,1,0:T(8,128)(2,1)S(1)} %get-tuple-element.46), channel_id=1, source_target_pairs={{0,2},{1,3},{2,0},{3,1},{4,6},{5,7},{6,4},{7,5},{8,10},{9,11},{10,... | collective-permute-start | bytes 393224 | tf_op jit(solution)/shard_map/ppermute | solution.py:43
  6.4 1.0 %copy-start.3 = (bf16[1,512,512]{2,1,0:T(8,128)(2,1)S(1)}, bf16[1,512,512]{2,1,0:T(8,128)(2,1)}, u32[]{:S(2)}) copy-start(bf16[1,512,512]{2,1,0:T(8,128)(2,1)} %param.9) | copy-start | bytes 1572868
  6.5 18.4 %collective-permute-start = (bf16[2,512,256]{2,1,0:T(8,128)(2,1)S(1)}, bf16[2,512,256]{2,1,0:T(8,128)(2,1)S(1)}, u32[]{:S(2)}, u32[]{:S(2)}) collective-permute-start(bf16[2,512,256]{2,1,0:T(8,128)(2,1)S(1)} %pad_maximum_fusion.5), channel_id=1, source_target_pairs={{0,1},{1,0},{2,3},{3,2},{4,5},{5,4},{6,7},{7,6},{8,9},{9,8},{10,11... | collective-permute-start | bytes 1572872 | tf_op jit(solution)/shard_map/ppermute | solution.py:18
  7.5 0.7 %copy-start.2 = (s32[2]{0:T(128)S(1)}, s32[2]{0:T(128)}, u32[]{:S(2)}) copy-start(s32[2]{0:T(128)} %param.11) | copy-start | bytes 28
  7.5 17.4 %collective-permute-start.1 = (bf16[512,512]{1,0:T(8,128)(2,1)S(1)}, bf16[512,512]{1,0:T(8,128)(2,1)S(1)}, u32[]{:S(2)}, u32[]{:S(2)}) collective-permute-start(bf16[512,512]{1,0:T(8,128)(2,1)S(1)} %bitcast.50), channel_id=1, source_target_pairs={{0,1},{1,0},{2,3},{3,2},{4,5},{5,4},{6,7},{7,6},{8,9},{9,8},{10,11... | collective-permute-start | bytes 1572872 | tf_op jit(solution)/shard_map/ppermute | solution.py:18
  12.5 1.4 %collective-permute-start.5 = (bf16[2,128,256]{2,1,0:T(8,128)(2,1)S(1)}, bf16[2,128,256]{2,1,0:T(8,128)(2,1)S(1)}, u32[]{:S(2)}, u32[]{:S(2)}) collective-permute-start(bf16[2,128,256]{2,1,0:T(8,128)(2,1)S(1)} %get-tuple-element.51), channel_id=1, source_target_pairs={{0,1},{1,0},{2,3},{3,2},{4,5},{5,4},{6,7},{7,6},{8,9},{9,8},{10,11... | collective-permute-start | bytes 393224 | tf_op jit(solution)/shard_map/ppermute | solution.py:18
  13.9 6.4 %collective-permute-start.6 = (bf16[2,128,256]{2,1,0:T(8,128)(2,1)S(1)}, bf16[2,128,256]{2,1,0:T(8,128)(2,1)S(1)}, u32[]{:S(2)}, u32[]{:S(2)}) collective-permute-start(bf16[2,128,256]{2,1,0:T(8,128)(2,1)S(1)} %get-tuple-element.50), channel_id=1, source_target_pairs={{0,8},{1,17},{2,10},{3,19},{4,12},{5,21},{6,14},{7,23},{8,0},{9,25... | collective-permute-start | bytes 393224 | tf_op jit(solution)/shard_map/ppermute | solution.py:43
  15.6 7.8 %collective-permute-start.8 = (bf16[2,128,256]{2,1,0:T(8,128)(2,1)S(1)}, bf16[2,128,256]{2,1,0:T(8,128)(2,1)S(1)}, u32[]{:S(2)}, u32[]{:S(2)}) collective-permute-start(bf16[2,128,256]{2,1,0:T(8,128)(2,1)S(1)} %get-tuple-element.49), channel_id=1, source_target_pairs={{0,8},{1,17},{2,10},{3,19},{4,12},{5,21},{6,14},{7,23},{8,0},{9,25... | collective-permute-start | bytes 393224 | tf_op jit(solution)/shard_map/ppermute | solution.py:43
  20.3 6.5 %collective-permute-start.7 = (bf16[2,128,256]{2,1,0:T(8,128)(2,1)S(1)}, bf16[2,128,256]{2,1,0:T(8,128)(2,1)S(1)}, u32[]{:S(2)}, u32[]{:S(2)}) collective-permute-start(bf16[2,128,256]{2,1,0:T(8,128)(2,1)S(1)} %broadcast_select_fusion.3), channel_id=1, source_target_pairs={{0,16},{1,9},{2,18},{3,11},{4,20},{5,13},{6,22},{7,15},{8,24},{9,1... | collective-permute-start | bytes 393224 | tf_op jit(solution)/shard_map/ppermute | solution.py:43
  23.3 7.3 %collective-permute-start.10 = (bf16[2,128,256]{2,1,0:T(8,128)(2,1)S(1)}, bf16[2,128,256]{2,1,0:T(8,128)(2,1)S(1)}, u32[]{:S(2)}, u32[]{:S(2)}) collective-permute-start(bf16[2,128,256]{2,1,0:T(8,128)(2,1)S(1)} %broadcast_select_fusion.2), channel_id=1, source_target_pairs={{0,16},{1,9},{2,18},{3,11},{4,20},{5,13},{6,22},{7,15},{8,24},{9,1... | collective-permute-start | bytes 393224 | tf_op jit(solution)/shard_map/ppermute | solution.py:43
  26.8 6.5 %collective-permute-start.12 = (bf16[2,128,256]{2,1,0:T(8,128)(2,1)S(1)}, bf16[2,128,256]{2,1,0:T(8,128)(2,1)S(1)}, u32[]{:S(2)}, u32[]{:S(2)}) collective-permute-start(bf16[2,128,256]{2,1,0:T(8,128)(2,1)S(1)} %broadcast_select_fusion.4), channel_id=1, source_target_pairs={{0,2},{1,5},{2,0},{3,7},{4,6},{5,1},{6,4},{7,3},{8,10},{9,13},{10,... | collective-permute-start | bytes 393224 | tf_op jit(solution)/shard_map/ppermute | solution.py:43
  28.4 7.0 %collective-permute-start.11 = (bf16[2,128,256]{2,1,0:T(8,128)(2,1)S(1)}, bf16[2,128,256]{2,1,0:T(8,128)(2,1)S(1)}, u32[]{:S(2)}, u32[]{:S(2)}) collective-permute-start(bf16[2,128,256]{2,1,0:T(8,128)(2,1)S(1)} %broadcast_select_fusion.4), channel_id=1, source_target_pairs={{0,4},{1,3},{2,6},{3,1},{4,0},{5,7},{6,2},{7,5},{8,12},{9,11},{10,... | collective-permute-start | bytes 393224 | tf_op jit(solution)/shard_map/ppermute | solution.py:43
  28.8 8.2 %collective-permute-start.9 = (bf16[2,128,256]{2,1,0:T(8,128)(2,1)S(1)}, bf16[2,128,256]{2,1,0:T(8,128)(2,1)S(1)}, u32[]{:S(2)}, u32[]{:S(2)}) collective-permute-start(bf16[2,128,256]{2,1,0:T(8,128)(2,1)S(1)} %broadcast_select_fusion.4), channel_id=1, source_target_pairs={{0,6},{1,7},{2,4},{3,5},{4,2},{5,3},{6,0},{7,1},{8,14},{9,15},{10,... | collective-permute-start | bytes 393224 | tf_op jit(solution)/shard_map/ppermute | solution.py:43
  30.7 8.4 %collective-permute-start.15 = (bf16[2,128,256]{2,1,0:T(8,128)(2,1)S(1)}, bf16[2,128,256]{2,1,0:T(8,128)(2,1)S(1)}, u32[]{:S(2)}, u32[]{:S(2)}) collective-permute-start(bf16[2,128,256]{2,1,0:T(8,128)(2,1)S(1)} %broadcast_select_fusion.1), channel_id=1, source_target_pairs={{0,2},{1,5},{2,0},{3,7},{4,6},{5,1},{6,4},{7,3},{8,10},{9,13},{10,... | collective-permute-start | bytes 393224 | tf_op jit(solution)/shard_map/ppermute | solution.py:43
  32.3 6.8 %collective-permute-start.14 = (bf16[2,128,256]{2,1,0:T(8,128)(2,1)S(1)}, bf16[2,128,256]{2,1,0:T(8,128)(2,1)S(1)}, u32[]{:S(2)}, u32[]{:S(2)}) collective-permute-start(bf16[2,128,256]{2,1,0:T(8,128)(2,1)S(1)} %broadcast_select_fusion.1), channel_id=1, source_target_pairs={{0,4},{1,3},{2,6},{3,1},{4,0},{5,7},{6,2},{7,5},{8,12},{9,11},{10,... | collective-permute-start | bytes 393224 | tf_op jit(solution)/shard_map/ppermute | solution.py:43
  33.2 7.1 %collective-permute-start.13 = (bf16[2,128,256]{2,1,0:T(8,128)(2,1)S(1)}, bf16[2,128,256]{2,1,0:T(8,128)(2,1)S(1)}, u32[]{:S(2)}, u32[]{:S(2)}) collective-permute-start(bf16[2,128,256]{2,1,0:T(8,128)(2,1)S(1)} %broadcast_select_fusion.1), channel_id=1, source_target_pairs={{0,6},{1,7},{2,4},{3,5},{4,2},{5,3},{6,0},{7,1},{8,14},{9,15},{10,... | collective-permute-start | bytes 393224 | tf_op jit(solution)/shard_map/ppermute | solution.py:43
  39.1 1.4 %copy-start.4 = (bf16[512,512]{1,0:T(8,128)(2,1)S(1)}, bf16[512,512]{1,0:T(8,128)(2,1)}, u32[]{:S(2)}) copy-start(bf16[512,512]{1,0:T(8,128)(2,1)} %param.6) | copy-start | bytes 1572868

commit v4 on v3

--- a/solution.py
+++ b/solution.py
@@ -7,7 +7,7 @@
 
 LOW = 2
 FAN = ((1, 1), (2, 2), (3, 3))
-BACK = ((1, 2), (2, 1), (3, 3))
+BACK = ((2, 2), (1, 1), (3, 3))
 
 
 def after(value, earlier):
@@ -91,8 +91,8 @@
     both = jnp.stack([right, left])
     slots, came, sent = first.scatter_start(both)
 
-    own = all_panels(after(both, sent), cols, col)
-    inverse = all_panels(after(inverse, sent), cols, col)
+    own = all_panels(both, cols, col)
+    inverse = all_panels(after(inverse, own), cols, col)
     right, left = own[:, 0], own[:, 1]
     solve = functools.partial(jnp.einsum, "ktu,kur->ktr", preferred_element_type=jnp.float32)
     solved = solve(inverse, right).astype(jnp.bfloat16)
@@ -108,12 +108,12 @@
         came_one = first.cross(one, first.high[step + 1])
         two = second.spread(two, after(came_two, one), step)
         came_two = second.cross(two, second.high[step + 1])
-    one = first.spread(one, after(came_one, (two, solved, base)), last)
+    one = first.spread(one, after(came_one, (two, base)), last)
     parts_one = first.gather_start(one)
-    two = second.spread(two, after(came_two, one), last)
+    two = second.spread(two, after(came_two, (one, solved)), last)
     parts_two = second.gather_start(two)
 
-    right_col = first.gather_end([after(part, two) for part in parts_one])
+    right_col = first.gather_end(parts_one)
     solved_col = solve(inverse, right_col).astype(jnp.bfloat16)
     core = jnp.einsum("ktr,kts->krs", solved, solved_col, preferred_element_type=jnp.float32)
     core = core.astype(jnp.bfloat16)

time: 42.1 us -> 41.6 us (0.988)
  waiting for transfers between devices: 15.8 us -> 14.5 us
  starting transfers between devices: 17.3 us -> 17.8 us
    ppermute x13, waiting for transfers between devices: 14.6 us -> 13.3 us  [cross(): return lax.ppermute(block, ('row', 'col'), pairs)]
    ppermute x13, starting transfers between devices: 17.2 us -> 17.6 us  [cross(): return lax.ppermute(block, ('row', 'col'), pairs)]
  transfers between devices with their start and end apart: 16 -> 16, of which waited for: 12 -> 10; matrix products, arithmetic and copies ran while one was open for 9% -> 10% of each run, Pallas kernels for 0% -> 0%
where the time goes in v4:
time: 41.6 us; the launch traced here: 41.3 us
  starting transfers between devices  17.8 us (43%)
  waiting for transfers between devices  14.5 us (35%)
  matrix products  4.9 us (12%)
  other arithmetic  1.67 us (4%)
  local copies, waits for them, and re-layouts  1.55 us (4%)
  between operations  0.92 us (2%)
    ppermute x13, starting transfers between devices, cross(): return lax.ppermute(block, ('row', 'col'), pairs)  17.6 us
    ppermute x13, waiting for transfers between devices, cross(): return lax.ppermute(block, ('row', 'col'), pairs)  13.3 us
    dot_general x1, matrix products, local(): jnp.einsum('ktr,kts->krs', solved, solved_col, preferred_element_type=jnp...  1.68 us
    unnamed x10, local copies, waits for them, and re-layouts  1.55 us
    dot_general x1, matrix products, local(): solved = solve(inverse, right).astype(jnp.bfloat16)  1.48 us
    dot_general x1, matrix products, local(): jnp.einsum('kts,kus->tu', mixed, left_col, preferred_element_type=jnp.flo...  1.45 us
    ppermute x3, waiting for transfers between devices, swap_cols(): return lax.ppermute(block, 'col', [(0, 1), (1, 0)])  1.19 us
    select_n x2, other arithmetic, local(): jnp.where(keep[None, :], w_factor[0, 0], jnp.zeros((), jnp.bfloat16))  1.04 us
  transfers between devices with their start and end apart: 16, of which 10 were waited for; matrix products, arithmetic and copies ran while one was open for 10% of the time, Pallas kernels for 0%

profile of v4, /device:TPU:0, one launch (start us, length us, event | category | flops | bytes accessed | tf_op | source)
XLA Modules:
  0.0 41.3 jit_solution(17421906410960032684)
XLA Ops:
  0.7 1.0 %broadcast_select_fusion = bf16[1,4,128,256]{3,2,1,0:T(8,128)(2,1)S(1)} fusion(bf16[1,4,128,256]{3,2,1,0:T(8,128)(2,1)} %bitcast.45, pred[256]{0:T(512)(128)(4,1)S(1)} %iota_compare_fusion), kind=kLoop, calls=%fused_computation.44 | loop fusion | flops 131072 | bytes 524544 | tf_op jit(solution)/shard_map/jit(_where)/select_n | solution.py:89
  1.8 4.0 %collective-permute-start.2 = (bf16[2,128,256]{2,1,0:T(8,128)(2,1)S(1)}, bf16[2,128,256]{2,1,0:T(8,128)(2,1)S(1)}, u32[]{:S(2)}, u32[]{:S(2)}) collective-permute-start(bf16[2,128,256]{2,1,0:T(8,128)(2,1)S(1)} %get-tuple-element.35), channel_id=1, source_target_pairs={{0,6},{1,7},{2,4},{3,5},{4,2},{5,3},{6,0},{7,1},{8,14},{9,15},{10,... | collective-permute-start | bytes 393224 | tf_op jit(solution)/shard_map/ppermute | solution.py:43
  5.8 0.5 %collective-permute-start.3 = (bf16[2,128,256]{2,1,0:T(8,128)(2,1)S(1)}, bf16[2,128,256]{2,1,0:T(8,128)(2,1)S(1)}, u32[]{:S(2)}, u32[]{:S(2)}) collective-permute-start(bf16[2,128,256]{2,1,0:T(8,128)(2,1)S(1)} %get-tuple-element.36), channel_id=1, source_target_pairs={{0,4},{1,5},{2,6},{3,7},{4,0},{5,1},{6,2},{7,3},{8,12},{9,13},{10,... | collective-permute-start | bytes 393224 | tf_op jit(solution)/shard_map/ppermute | solution.py:43
  6.3 0.1 collective-permute-start.4
  6.6 0.9 %copy-done.3 = bf16[1,512,512]{2,1,0:T(8,128)(2,1)S(1)} copy-done((bf16[1,512,512]{2,1,0:T(8,128)(2,1)S(1)}, bf16[1,512,512]{2,1,0:T(8,128)(2,1)}, u32[]{:S(2)}) %copy-start.3) | copy-done | bytes 524312
  7.5 0.7 %copy-done.2 = s32[2]{0:T(128)S(1)} copy-done((s32[2]{0:T(128)S(1)}, s32[2]{0:T(128)}, u32[]{:S(2)}) %copy-start.2) | copy-done | bytes 32
  8.2 1.5 %collective-permute-done.2 = bf16[2,128,256]{2,1,0:T(8,128)(2,1)S(1)} collective-permute-done((bf16[2,128,256]{2,1,0:T(8,128)(2,1)S(1)}, bf16[2,128,256]{2,1,0:T(8,128)(2,1)S(1)}, u32[]{:S(2)}, u32[]{:S(2)}) %collective-permute-start.2) | collective-permute-done | bytes 131104 | tf_op jit(solution)/shard_map/ppermute | solution.py:43
  9.7 2.4 %collective-permute-done.3 = bf16[2,128,256]{2,1,0:T(8,128)(2,1)S(1)} collective-permute-done((bf16[2,128,256]{2,1,0:T(8,128)(2,1)S(1)}, bf16[2,128,256]{2,1,0:T(8,128)(2,1)S(1)}, u32[]{:S(2)}, u32[]{:S(2)}) %collective-permute-start.3) | collective-permute-done | bytes 131104 | tf_op jit(solution)/shard_map/ppermute | solution.py:43
  12.1 0.2 collective-permute-done.4
  12.3 0.1 select_select_fusion
  12.6 0.1 select_reduce_fusion
  12.7 1.2 %collective-permute-done.5 = bf16[2,128,256]{2,1,0:T(8,128)(2,1)S(1)} collective-permute-done((bf16[2,128,256]{2,1,0:T(8,128)(2,1)S(1)}, bf16[2,128,256]{2,1,0:T(8,128)(2,1)S(1)}, u32[]{:S(2)}, u32[]{:S(2)}) %collective-permute-start.5) | collective-permute-done | bytes 131104 | tf_op jit(solution)/shard_map/ppermute | solution.py:18
  13.9 1.6 %collective-permute-start.6 = (bf16[2,128,256]{2,1,0:T(8,128)(2,1)S(1)}, bf16[2,128,256]{2,1,0:T(8,128)(2,1)S(1)}, u32[]{:S(2)}, u32[]{:S(2)}) collective-permute-start(bf16[2,128,256]{2,1,0:T(8,128)(2,1)S(1)} %get-tuple-element.42), channel_id=1, source_target_pairs={{0,8},{1,17},{2,10},{3,19},{4,12},{5,21},{6,14},{7,23},{8,0},{9,25... | collective-permute-start | bytes 393224 | tf_op jit(solution)/shard_map/ppermute | solution.py:43
  15.6 0.4 %collective-permute-start.8 = (bf16[2,128,256]{2,1,0:T(8,128)(2,1)S(1)}, bf16[2,128,256]{2,1,0:T(8,128)(2,1)S(1)}, u32[]{:S(2)}, u32[]{:S(2)}) collective-permute-start(bf16[2,128,256]{2,1,0:T(8,128)(2,1)S(1)} %get-tuple-element.41), channel_id=1, source_target_pairs={{0,8},{1,17},{2,10},{3,19},{4,12},{5,21},{6,14},{7,23},{8,0},{9,25... | collective-permute-start | bytes 393224 | tf_op jit(solution)/shard_map/ppermute | solution.py:43
  16.0 4.3 %collective-permute-done.6 = bf16[2,128,256]{2,1,0:T(8,128)(2,1)S(1)} collective-permute-done((bf16[2,128,256]{2,1,0:T(8,128)(2,1)S(1)}, bf16[2,128,256]{2,1,0:T(8,128)(2,1)S(1)}, u32[]{:S(2)}, u32[]{:S(2)}) %collective-permute-start.6) | collective-permute-done | bytes 131104 | tf_op jit(solution)/shard_map/ppermute | solution.py:43
  20.3 2.2 %collective-permute-start.7 = (bf16[2,128,256]{2,1,0:T(8,128)(2,1)S(1)}, bf16[2,128,256]{2,1,0:T(8,128)(2,1)S(1)}, u32[]{:S(2)}, u32[]{:S(2)}) collective-permute-start(bf16[2,128,256]{2,1,0:T(8,128)(2,1)S(1)} %broadcast_select_fusion.3), channel_id=1, source_target_pairs={{0,16},{1,9},{2,18},{3,11},{4,20},{5,13},{6,22},{7,15},{8,24},{9,1... | collective-permute-start | bytes 393224 | tf_op jit(solution)/shard_map/ppermute | solution.py:43
  22.5 0.8 %collective-permute-done.8 = bf16[2,128,256]{2,1,0:T(8,128)(2,1)S(1)} collective-permute-done((bf16[2,128,256]{2,1,0:T(8,128)(2,1)S(1)}, bf16[2,128,256]{2,1,0:T(8,128)(2,1)S(1)}, u32[]{:S(2)}, u32[]{:S(2)}) %collective-permute-start.8) | collective-permute-done | bytes 131104 | tf_op jit(solution)/shard_map/ppermute | solution.py:43
  23.3 1.6 %collective-permute-start.12 = (bf16[2,128,256]{2,1,0:T(8,128)(2,1)S(1)}, bf16[2,128,256]{2,1,0:T(8,128)(2,1)S(1)}, u32[]{:S(2)}, u32[]{:S(2)}) collective-permute-start(bf16[2,128,256]{2,1,0:T(8,128)(2,1)S(1)} %broadcast_select_fusion.2), channel_id=1, source_target_pairs={{0,16},{1,9},{2,18},{3,11},{4,20},{5,13},{6,22},{7,15},{8,24},{9,1... | collective-permute-start | bytes 393224 | tf_op jit(solution)/shard_map/ppermute | solution.py:43
  24.9 1.8 %collective-permute-done.7 = bf16[2,128,256]{2,1,0:T(8,128)(2,1)S(1)} collective-permute-done((bf16[2,128,256]{2,1,0:T(8,128)(2,1)S(1)}, bf16[2,128,256]{2,1,0:T(8,128)(2,1)S(1)}, u32[]{:S(2)}, u32[]{:S(2)}) %collective-permute-start.7) | collective-permute-done | bytes 131104 | tf_op jit(solution)/shard_map/ppermute | solution.py:43
  26.8 1.6 %collective-permute-start.10 = (bf16[2,128,256]{2,1,0:T(8,128)(2,1)S(1)}, bf16[2,128,256]{2,1,0:T(8,128)(2,1)S(1)}, u32[]{:S(2)}, u32[]{:S(2)}) collective-permute-start(bf16[2,128,256]{2,1,0:T(8,128)(2,1)S(1)} %broadcast_select_fusion.4), channel_id=1, source_target_pairs={{0,2},{1,3},{2,0},{3,1},{4,6},{5,7},{6,4},{7,5},{8,10},{9,11},{10,... | collective-permute-start | bytes 393224 | tf_op jit(solution)/shard_map/ppermute | solution.py:43
  28.4 0.4 %collective-permute-start.11 = (bf16[2,128,256]{2,1,0:T(8,128)(2,1)S(1)}, bf16[2,128,256]{2,1,0:T(8,128)(2,1)S(1)}, u32[]{:S(2)}, u32[]{:S(2)}) collective-permute-start(bf16[2,128,256]{2,1,0:T(8,128)(2,1)S(1)} %broadcast_select_fusion.4), channel_id=1, source_target_pairs={{0,4},{1,5},{2,6},{3,7},{4,0},{5,1},{6,2},{7,3},{8,12},{9,13},{10,... | collective-permute-start | bytes 393224 | tf_op jit(solution)/shard_map/ppermute | solution.py:43
  28.8 1.5 %collective-permute-start.9 = (bf16[2,128,256]{2,1,0:T(8,128)(2,1)S(1)}, bf16[2,128,256]{2,1,0:T(8,128)(2,1)S(1)}, u32[]{:S(2)}, u32[]{:S(2)}) collective-permute-start(bf16[2,128,256]{2,1,0:T(8,128)(2,1)S(1)} %broadcast_select_fusion.4), channel_id=1, source_target_pairs={{0,6},{1,7},{2,4},{3,5},{4,2},{5,3},{6,0},{7,1},{8,14},{9,15},{10,... | collective-permute-start | bytes 393224 | tf_op jit(solution)/shard_map/ppermute | solution.py:43
  30.3 1.5 %convolution_convert_fusion.2 = bf16[2,512,256]{2,1,0:T(8,128)(2,1)S(1)} fusion(bf16[1,512,512]{2,1,0:T(8,128)(2,1)} %bitcast.9, bf16[1,512,512]{2,1,0:T(8,128)(2,1)S(1)} %copy-done.3, bf16[1,2,512,256]{3,2,0,1:T(8,128)(2,1)S(1)} %get-tuple-element.40, bf16[1,2,512,256]{3,2,0,1:T(8,128)(2,1)S(1)} %bitcast.50), kind=kOutput, calls=%fused_computation.9 | convolution fusion | flops 269484032 | bytes 2621440 | tf_op jit(solution)/shard_map/ktu,kur->ktr/dot_general | solution.py:98
  31.9 1.5 %collective-permute-start.15 = (bf16[2,128,256]{2,1,0:T(8,128)(2,1)S(1)}, bf16[2,128,256]{2,1,0:T(8,128)(2,1)S(1)}, u32[]{:S(2)}, u32[]{:S(2)}) collective-permute-start(bf16[2,128,256]{2,1,0:T(8,128)(2,1)S(1)} %broadcast_select_fusion.1), channel_id=1, source_target_pairs={{0,4},{1,5},{2,6},{3,7},{4,0},{5,1},{6,2},{7,3},{8,12},{9,13},{10,... | collective-permute-start | bytes 393224 | tf_op jit(solution)/shard_map/ppermute | solution.py:43
  33.4 0.5 %collective-permute-start.14 = (bf16[2,128,256]{2,1,0:T(8,128)(2,1)S(1)}, bf16[2,128,256]{2,1,0:T(8,128)(2,1)S(1)}, u32[]{:S(2)}, u32[]{:S(2)}) collective-permute-start(bf16[2,128,256]{2,1,0:T(8,128)(2,1)S(1)} %broadcast_select_fusion.1), channel_id=1, source_target_pairs={{0,2},{1,3},{2,0},{3,1},{4,6},{5,7},{6,4},{7,5},{8,10},{9,11},{10,... | collective-permute-start | bytes 393224 | tf_op jit(solution)/shard_map/ppermute | solution.py:43
  33.9 1.5 %collective-permute-start.13 = (bf16[2,128,256]{2,1,0:T(8,128)(2,1)S(1)}, bf16[2,128,256]{2,1,0:T(8,128)(2,1)S(1)}, u32[]{:S(2)}, u32[]{:S(2)}) collective-permute-start(bf16[2,128,256]{2,1,0:T(8,128)(2,1)S(1)} %broadcast_select_fusion.1), channel_id=1, source_target_pairs={{0,6},{1,7},{2,4},{3,5},{4,2},{5,3},{6,0},{7,1},{8,14},{9,15},{10,... | collective-permute-start | bytes 393224 | tf_op jit(solution)/shard_map/ppermute | solution.py:43
  35.4 0.7 %collective-permute-done.9 = bf16[2,128,256]{2,1,0:T(8,128)(2,1)S(1)} collective-permute-done((bf16[2,128,256]{2,1,0:T(8,128)(2,1)S(1)}, bf16[2,128,256]{2,1,0:T(8,128)(2,1)S(1)}, u32[]{:S(2)}, u32[]{:S(2)}) %collective-permute-start.9) | collective-permute-done | bytes 131104 | tf_op jit(solution)/shard_map/ppermute | solution.py:43
  36.2 1.7 %fusion.2 = bf16[2,256,256]{2,1,0:T(8,128)(2,1)S(1)} fusion(bf16[2,512,256]{2,1,0:T(8,128)(2,1)S(1)} %convolution_convert_fusion.2, bf16[1,512,512]{2,1,0:T(8,128)(2,1)} %bitcast.9, bf16[1,512,512]{2,1,0:T(8,128)(2,1)S(1)} %copy-done.3, bf16[2,128,256]{2,1,0:T(8,128)(2,1)S(1)} %get-tuple-element.32, bf16[2,128,256]{2,1,0:T(8,128)(2,1)S(1)} %get-tuple-element.33, ...), kind=kOutput, calls=%fused_computation.11 | convolution fusion | flops 405667840 | bytes 2359296 | tf_op jit(solution)/shard_map/ktr,kts->krs/dot_general | solution.py:118
  37.9 0.3 convolution_convert_fusion
  38.2 0.1 collective-permute-done.15
  38.4 1.4 %collective-permute-done.13 = bf16[2,128,256]{2,1,0:T(8,128)(2,1)S(1)} collective-permute-done((bf16[2,128,256]{2,1,0:T(8,128)(2,1)S(1)}, bf16[2,128,256]{2,1,0:T(8,128)(2,1)S(1)}, u32[]{:S(2)}, u32[]{:S(2)}) %collective-permute-start.13) | collective-permute-done | bytes 131104 | tf_op jit(solution)/shard_map/ppermute | solution.py:43
  39.9 1.4 %fusion = f32[512,512]{1,0:T(8,128)} fusion(bf16[2,512,256]{2,1,0:T(8,128)(2,1)S(1)} %convolution_convert_fusion, bf16[2,128,256]{2,1,0:T(8,128)(2,1)S(1)} %get-tuple-element.28, bf16[2,128,256]{2,1,0:T(8,128)(2,1)S(1)} %get-tuple-element.29, bf16[2,128,256]{2,1,0:T(8,128)(2,1)S(1)} %get-tuple-element.30, bf16[2,128,256]{2,1,0:T(8,128)(2,1)S(1)} %get-tuple-element.27, ...), kind=kOutput, calls=%fused_computation.6 | convolution fusion | flops 271056896 | bytes 2621440 | tf_op jit(solution)/shard_map/kts,kus->tu/dot_general | solution.py:123
  (34 shorter events, 0.7 us)
Async XLA Ops:
  0.7 1.0 %copy-start.1 = (bf16[1,1,512,256]{3,2,1,0:T(8,128)(2,1)S(1)}, bf16[1,1,512,256]{3,2,1,0:T(8,128)(2,1)}, u32[]{:S(2)}) copy-start(bf16[1,1,512,256]{3,2,1,0:T(8,128)(2,1)} %param.7) | copy-start | bytes 786436
  1.7 4.7 %copy-start = (bf16[1,1,512,256]{3,2,1,0:T(8,128)(2,1)S(1)}, bf16[1,1,512,256]{3,2,1,0:T(8,128)(2,1)}, u32[]{:S(2)}) copy-start(bf16[1,1,512,256]{3,2,1,0:T(8,128)(2,1)} %param.8) | copy-start | bytes 786436
  1.8 7.9 %collective-permute-start.2 = (bf16[2,128,256]{2,1,0:T(8,128)(2,1)S(1)}, bf16[2,128,256]{2,1,0:T(8,128)(2,1)S(1)}, u32[]{:S(2)}, u32[]{:S(2)}) collective-permute-start(bf16[2,128,256]{2,1,0:T(8,128)(2,1)S(1)} %get-tuple-element.35), channel_id=1, source_target_pairs={{0,6},{1,7},{2,4},{3,5},{4,2},{5,3},{6,0},{7,1},{8,14},{9,15},{10,... | collective-permute-start | bytes 393224 | tf_op jit(solution)/shard_map/ppermute | solution.py:43
  5.8 6.3 %collective-permute-start.3 = (bf16[2,128,256]{2,1,0:T(8,128)(2,1)S(1)}, bf16[2,128,256]{2,1,0:T(8,128)(2,1)S(1)}, u32[]{:S(2)}, u32[]{:S(2)}) collective-permute-start(bf16[2,128,256]{2,1,0:T(8,128)(2,1)S(1)} %get-tuple-element.36), channel_id=1, source_target_pairs={{0,4},{1,5},{2,6},{3,7},{4,0},{5,1},{6,2},{7,3},{8,12},{9,13},{10,... | collective-permute-start | bytes 393224 | tf_op jit(solution)/shard_map/ppermute | solution.py:43
  6.3 6.0 %collective-permute-start.4 = (bf16[2,128,256]{2,1,0:T(8,128)(2,1)S(1)}, bf16[2,128,256]{2,1,0:T(8,128)(2,1)S(1)}, u32[]{:S(2)}, u32[]{:S(2)}) collective-permute-start(bf16[2,128,256]{2,1,0:T(8,128)(2,1)S(1)} %get-tuple-element.37), channel_id=1, source_target_pairs={{0,2},{1,3},{2,0},{3,1},{4,6},{5,7},{6,4},{7,5},{8,10},{9,11},{10,... | collective-permute-start | bytes 393224 | tf_op jit(solution)/shard_map/ppermute | solution.py:43
  6.4 1.0 %copy-start.3 = (bf16[1,512,512]{2,1,0:T(8,128)(2,1)S(1)}, bf16[1,512,512]{2,1,0:T(8,128)(2,1)}, u32[]{:S(2)}) copy-start(bf16[1,512,512]{2,1,0:T(8,128)(2,1)} %param.9) | copy-start | bytes 1572868
  6.5 22.3 %collective-permute-start = (bf16[2,512,256]{2,1,0:T(8,128)(2,1)S(1)}, bf16[2,512,256]{2,1,0:T(8,128)(2,1)S(1)}, u32[]{:S(2)}, u32[]{:S(2)}) collective-permute-start(bf16[2,512,256]{2,1,0:T(8,128)(2,1)S(1)} %get-tuple-element.39), channel_id=1, source_target_pairs={{0,1},{1,0},{2,3},{3,2},{4,5},{5,4},{6,7},{7,6},{8,9},{9,8},{10,11... | collective-permute-start | bytes 1572872 | tf_op jit(solution)/shard_map/ppermute | solution.py:18
  7.5 0.7 %copy-start.2 = (s32[2]{0:T(128)S(1)}, s32[2]{0:T(128)}, u32[]{:S(2)}) copy-start(s32[2]{0:T(128)} %param.11) | copy-start | bytes 28
  7.5 22.9 %collective-permute-start.1 = (bf16[512,512]{1,0:T(8,128)(2,1)S(1)}, bf16[512,512]{1,0:T(8,128)(2,1)}, u32[]{:S(2)}, u32[]{:S(2)}) collective-permute-start(bf16[512,512]{1,0:T(8,128)(2,1)S(1)} %bitcast.49), channel_id=1, source_target_pairs={{0,1},{1,0},{2,3},{3,2},{4,5},{5,4},{6,7},{7,6},{8,9},{9,8},{10,11... | collective-permute-start | bytes 1572872 | tf_op jit(solution)/shard_map/ppermute | solution.py:18
  12.5 1.4 %collective-permute-start.5 = (bf16[2,128,256]{2,1,0:T(8,128)(2,1)S(1)}, bf16[2,128,256]{2,1,0:T(8,128)(2,1)S(1)}, u32[]{:S(2)}, u32[]{:S(2)}) collective-permute-start(bf16[2,128,256]{2,1,0:T(8,128)(2,1)S(1)} %get-tuple-element.43), channel_id=1, source_target_pairs={{0,1},{1,0},{2,3},{3,2},{4,5},{5,4},{6,7},{7,6},{8,9},{9,8},{10,11... | collective-permute-start | bytes 393224 | tf_op jit(solution)/shard_map/ppermute | solution.py:18
  13.9 6.4 %collective-permute-start.6 = (bf16[2,128,256]{2,1,0:T(8,128)(2,1)S(1)}, bf16[2,128,256]{2,1,0:T(8,128)(2,1)S(1)}, u32[]{:S(2)}, u32[]{:S(2)}) collective-permute-start(bf16[2,128,256]{2,1,0:T(8,128)(2,1)S(1)} %get-tuple-element.42), channel_id=1, source_target_pairs={{0,8},{1,17},{2,10},{3,19},{4,12},{5,21},{6,14},{7,23},{8,0},{9,25... | collective-permute-start | bytes 393224 | tf_op jit(solution)/shard_map/ppermute | solution.py:43
  15.6 7.8 %collective-permute-start.8 = (bf16[2,128,256]{2,1,0:T(8,128)(2,1)S(1)}, bf16[2,128,256]{2,1,0:T(8,128)(2,1)S(1)}, u32[]{:S(2)}, u32[]{:S(2)}) collective-permute-start(bf16[2,128,256]{2,1,0:T(8,128)(2,1)S(1)} %get-tuple-element.41), channel_id=1, source_target_pairs={{0,8},{1,17},{2,10},{3,19},{4,12},{5,21},{6,14},{7,23},{8,0},{9,25... | collective-permute-start | bytes 393224 | tf_op jit(solution)/shard_map/ppermute | solution.py:43
  20.3 6.5 %collective-permute-start.7 = (bf16[2,128,256]{2,1,0:T(8,128)(2,1)S(1)}, bf16[2,128,256]{2,1,0:T(8,128)(2,1)S(1)}, u32[]{:S(2)}, u32[]{:S(2)}) collective-permute-start(bf16[2,128,256]{2,1,0:T(8,128)(2,1)S(1)} %broadcast_select_fusion.3), channel_id=1, source_target_pairs={{0,16},{1,9},{2,18},{3,11},{4,20},{5,13},{6,22},{7,15},{8,24},{9,1... | collective-permute-start | bytes 393224 | tf_op jit(solution)/shard_map/ppermute | solution.py:43
  23.3 8.5 %collective-permute-start.12 = (bf16[2,128,256]{2,1,0:T(8,128)(2,1)S(1)}, bf16[2,128,256]{2,1,0:T(8,128)(2,1)S(1)}, u32[]{:S(2)}, u32[]{:S(2)}) collective-permute-start(bf16[2,128,256]{2,1,0:T(8,128)(2,1)S(1)} %broadcast_select_fusion.2), channel_id=1, source_target_pairs={{0,16},{1,9},{2,18},{3,11},{4,20},{5,13},{6,22},{7,15},{8,24},{9,1... | collective-permute-start | bytes 393224 | tf_op jit(solution)/shard_map/ppermute | solution.py:43
  26.8 7.1 %collective-permute-start.10 = (bf16[2,128,256]{2,1,0:T(8,128)(2,1)S(1)}, bf16[2,128,256]{2,1,0:T(8,128)(2,1)S(1)}, u32[]{:S(2)}, u32[]{:S(2)}) collective-permute-start(bf16[2,128,256]{2,1,0:T(8,128)(2,1)S(1)} %broadcast_select_fusion.4), channel_id=1, source_target_pairs={{0,2},{1,3},{2,0},{3,1},{4,6},{5,7},{6,4},{7,5},{8,10},{9,11},{10,... | collective-permute-start | bytes 393224 | tf_op jit(solution)/shard_map/ppermute | solution.py:43
  28.4 7.0 %collective-permute-start.11 = (bf16[2,128,256]{2,1,0:T(8,128)(2,1)S(1)}, bf16[2,128,256]{2,1,0:T(8,128)(2,1)S(1)}, u32[]{:S(2)}, u32[]{:S(2)}) collective-permute-start(bf16[2,128,256]{2,1,0:T(8,128)(2,1)S(1)} %broadcast_select_fusion.4), channel_id=1, source_target_pairs={{0,4},{1,5},{2,6},{3,7},{4,0},{5,1},{6,2},{7,3},{8,12},{9,13},{10,... | collective-permute-start | bytes 393224 | tf_op jit(solution)/shard_map/ppermute | solution.py:43
  28.8 7.3 %collective-permute-start.9 = (bf16[2,128,256]{2,1,0:T(8,128)(2,1)S(1)}, bf16[2,128,256]{2,1,0:T(8,128)(2,1)S(1)}, u32[]{:S(2)}, u32[]{:S(2)}) collective-permute-start(bf16[2,128,256]{2,1,0:T(8,128)(2,1)S(1)} %broadcast_select_fusion.4), channel_id=1, source_target_pairs={{0,6},{1,7},{2,4},{3,5},{4,2},{5,3},{6,0},{7,1},{8,14},{9,15},{10,... | collective-permute-start | bytes 393224 | tf_op jit(solution)/shard_map/ppermute | solution.py:43
  31.9 6.5 %collective-permute-start.15 = (bf16[2,128,256]{2,1,0:T(8,128)(2,1)S(1)}, bf16[2,128,256]{2,1,0:T(8,128)(2,1)S(1)}, u32[]{:S(2)}, u32[]{:S(2)}) collective-permute-start(bf16[2,128,256]{2,1,0:T(8,128)(2,1)S(1)} %broadcast_select_fusion.1), channel_id=1, source_target_pairs={{0,4},{1,5},{2,6},{3,7},{4,0},{5,1},{6,2},{7,3},{8,12},{9,13},{10,... | collective-permute-start | bytes 393224 | tf_op jit(solution)/shard_map/ppermute | solution.py:43
  33.4 5.0 %collective-permute-start.14 = (bf16[2,128,256]{2,1,0:T(8,128)(2,1)S(1)}, bf16[2,128,256]{2,1,0:T(8,128)(2,1)S(1)}, u32[]{:S(2)}, u32[]{:S(2)}) collective-permute-start(bf16[2,128,256]{2,1,0:T(8,128)(2,1)S(1)} %broadcast_select_fusion.1), channel_id=1, source_target_pairs={{0,2},{1,3},{2,0},{3,1},{4,6},{5,7},{6,4},{7,5},{8,10},{9,11},{10,... | collective-permute-start | bytes 393224 | tf_op jit(solution)/shard_map/ppermute | solution.py:43
  33.9 5.9 %collective-permute-start.13 = (bf16[2,128,256]{2,1,0:T(8,128)(2,1)S(1)}, bf16[2,128,256]{2,1,0:T(8,128)(2,1)S(1)}, u32[]{:S(2)}, u32[]{:S(2)}) collective-permute-start(bf16[2,128,256]{2,1,0:T(8,128)(2,1)S(1)} %broadcast_select_fusion.1), channel_id=1, source_target_pairs={{0,6},{1,7},{2,4},{3,5},{4,2},{5,3},{6,0},{7,1},{8,14},{9,15},{10,... | collective-permute-start | bytes 393224 | tf_op jit(solution)/shard_map/ppermute | solution.py:43
  38.2 1.7 %copy-start.4 = (bf16[512,512]{1,0:T(8,128)(2,1)S(1)}, bf16[512,512]{1,0:T(8,128)(2,1)}, u32[]{:S(2)}) copy-start(bf16[512,512]{1,0:T(8,128)(2,1)} %param.6) | copy-start | bytes 1572868

commit v5 on v4

--- a/solution.py
+++ b/solution.py
@@ -104,13 +104,13 @@
     came_two = second.cross(two, second.high[0])
     last = len(first.high) - 1
     for step in range(last):
-        one = first.spread(one, after(came_one, two), step)
+        one = first.spread(one, came_one, step)
         came_one = first.cross(one, first.high[step + 1])
         two = second.spread(two, after(came_two, one), step)
         came_two = second.cross(two, second.high[step + 1])
-    one = first.spread(one, after(came_one, (two, base)), last)
+    one = first.spread(one, after(came_one, two), last)
     parts_one = first.gather_start(one)
-    two = second.spread(two, after(came_two, (one, solved)), last)
+    two = second.spread(two, after(came_two, (one, solved, base)), last)
     parts_two = second.gather_start(two)
 
     right_col = first.gather_end(parts_one)

time: 41.6 us -> 41.6 us (level)
  no operation moved by 1% of the time
where the time goes in v5:
time: 41.6 us; the launch traced here: 41.3 us
  starting transfers between devices  17.8 us (43%)
  waiting for transfers between devices  14.5 us (35%)
  matrix products  4.9 us (12%)
  other arithmetic  1.67 us (4%)
  local copies, waits for them, and re-layouts  1.55 us (4%)
  between operations  0.92 us (2%)
    ppermute x13, starting transfers between devices, cross(): return lax.ppermute(block, ('row', 'col'), pairs)  17.6 us
    ppermute x13, waiting for transfers between devices, cross(): return lax.ppermute(block, ('row', 'col'), pairs)  13.2 us
    dot_general x1, matrix products, local(): jnp.einsum('ktr,kts->krs', solved, solved_col, preferred_element_type=jnp...  1.68 us
    unnamed x10, local copies, waits for them, and re-layouts  1.55 us
    dot_general x1, matrix products, local(): solved = solve(inverse, right).astype(jnp.bfloat16)  1.48 us
    dot_general x1, matrix products, local(): jnp.einsum('kts,kus->tu', mixed, left_col, preferred_element_type=jnp.flo...  1.45 us
    ppermute x3, waiting for transfers between devices, swap_cols(): return lax.ppermute(block, 'col', [(0, 1), (1, 0)])  1.33 us
    select_n x2, other arithmetic, local(): jnp.where(keep[None, :], w_factor[0, 0], jnp.zeros((), jnp.bfloat16))  1.04 us
  transfers between devices with their start and end apart: 16, of which 10 were waited for; matrix products, arithmetic and copies ran while one was open for 10% of the time, Pallas kernels for 0%

profile of v5, /device:TPU:0, one launch (start us, length us, event | category | flops | bytes accessed | tf_op | source)
XLA Modules:
  0.0 41.3 jit_solution(15047446900174327430)
XLA Ops:
  0.7 1.0 %broadcast_select_fusion = bf16[1,4,128,256]{3,2,1,0:T(8,128)(2,1)S(1)} fusion(bf16[1,4,128,256]{3,2,1,0:T(8,128)(2,1)} %bitcast.45, pred[256]{0:T(512)(128)(4,1)S(1)} %iota_compare_fusion), kind=kLoop, calls=%fused_computation.44 | loop fusion | flops 131072 | bytes 524544 | tf_op jit(solution)/shard_map/jit(_where)/select_n | solution.py:89
  1.8 4.0 %collective-permute-start.2 = (bf16[2,128,256]{2,1,0:T(8,128)(2,1)S(1)}, bf16[2,128,256]{2,1,0:T(8,128)(2,1)S(1)}, u32[]{:S(2)}, u32[]{:S(2)}) collective-permute-start(bf16[2,128,256]{2,1,0:T(8,128)(2,1)S(1)} %get-tuple-element.33), channel_id=1, source_target_pairs={{0,6},{1,7},{2,4},{3,5},{4,2},{5,3},{6,0},{7,1},{8,14},{9,15},{10,... | collective-permute-start | bytes 393224 | tf_op jit(solution)/shard_map/ppermute | solution.py:43
  5.8 0.5 %collective-permute-start.3 = (bf16[2,128,256]{2,1,0:T(8,128)(2,1)S(1)}, bf16[2,128,256]{2,1,0:T(8,128)(2,1)S(1)}, u32[]{:S(2)}, u32[]{:S(2)}) collective-permute-start(bf16[2,128,256]{2,1,0:T(8,128)(2,1)S(1)} %get-tuple-element.34), channel_id=1, source_target_pairs={{0,4},{1,5},{2,6},{3,7},{4,0},{5,1},{6,2},{7,3},{8,12},{9,13},{10,... | collective-permute-start | bytes 393224 | tf_op jit(solution)/shard_map/ppermute | solution.py:43
  6.3 0.1 collective-permute-start.4
  6.6 0.9 %copy-done.3 = bf16[1,512,512]{2,1,0:T(8,128)(2,1)S(1)} copy-done((bf16[1,512,512]{2,1,0:T(8,128)(2,1)S(1)}, bf16[1,512,512]{2,1,0:T(8,128)(2,1)}, u32[]{:S(2)}) %copy-start.3) | copy-done | bytes 524312
  7.5 0.7 %copy-done.2 = s32[2]{0:T(128)S(1)} copy-done((s32[2]{0:T(128)S(1)}, s32[2]{0:T(128)}, u32[]{:S(2)}) %copy-start.2) | copy-done | bytes 32
  8.2 0.1 select_reduce_fusion
  8.3 1.4 %collective-permute-done.2 = bf16[2,128,256]{2,1,0:T(8,128)(2,1)S(1)} collective-permute-done((bf16[2,128,256]{2,1,0:T(8,128)(2,1)S(1)}, bf16[2,128,256]{2,1,0:T(8,128)(2,1)S(1)}, u32[]{:S(2)}, u32[]{:S(2)}) %collective-permute-start.2) | collective-permute-done | bytes 131104 | tf_op jit(solution)/shard_map/ppermute | solution.py:43
  9.7 2.4 %collective-permute-done.3 = bf16[2,128,256]{2,1,0:T(8,128)(2,1)S(1)} collective-permute-done((bf16[2,128,256]{2,1,0:T(8,128)(2,1)S(1)}, bf16[2,128,256]{2,1,0:T(8,128)(2,1)S(1)}, u32[]{:S(2)}, u32[]{:S(2)}) %collective-permute-start.3) | collective-permute-done | bytes 131104 | tf_op jit(solution)/shard_map/ppermute | solution.py:43
  12.1 0.2 collective-permute-done.4
  12.3 0.1 select_select_fusion
  12.6 1.3 %collective-permute-done.5 = bf16[2,128,256]{2,1,0:T(8,128)(2,1)S(1)} collective-permute-done((bf16[2,128,256]{2,1,0:T(8,128)(2,1)S(1)}, bf16[2,128,256]{2,1,0:T(8,128)(2,1)S(1)}, u32[]{:S(2)}, u32[]{:S(2)}) %collective-permute-start.5) | collective-permute-done | bytes 131104 | tf_op jit(solution)/shard_map/ppermute | solution.py:18
  13.9 1.6 %collective-permute-start.6 = (bf16[2,128,256]{2,1,0:T(8,128)(2,1)S(1)}, bf16[2,128,256]{2,1,0:T(8,128)(2,1)S(1)}, u32[]{:S(2)}, u32[]{:S(2)}) collective-permute-start(bf16[2,128,256]{2,1,0:T(8,128)(2,1)S(1)} %get-tuple-element.40), channel_id=1, source_target_pairs={{0,8},{1,17},{2,10},{3,19},{4,12},{5,21},{6,14},{7,23},{8,0},{9,25... | collective-permute-start | bytes 393224 | tf_op jit(solution)/shard_map/ppermute | solution.py:43
  15.6 0.4 %collective-permute-start.8 = (bf16[2,128,256]{2,1,0:T(8,128)(2,1)S(1)}, bf16[2,128,256]{2,1,0:T(8,128)(2,1)S(1)}, u32[]{:S(2)}, u32[]{:S(2)}) collective-permute-start(bf16[2,128,256]{2,1,0:T(8,128)(2,1)S(1)} %get-tuple-element.39), channel_id=1, source_target_pairs={{0,8},{1,17},{2,10},{3,19},{4,12},{5,21},{6,14},{7,23},{8,0},{9,25... | collective-permute-start | bytes 393224 | tf_op jit(solution)/shard_map/ppermute | solution.py:43
  16.0 4.3 %collective-permute-done.6 = bf16[2,128,256]{2,1,0:T(8,128)(2,1)S(1)} collective-permute-done((bf16[2,128,256]{2,1,0:T(8,128)(2,1)S(1)}, bf16[2,128,256]{2,1,0:T(8,128)(2,1)S(1)}, u32[]{:S(2)}, u32[]{:S(2)}) %collective-permute-start.6) | collective-permute-done | bytes 131104 | tf_op jit(solution)/shard_map/ppermute | solution.py:43
  20.3 2.2 %collective-permute-start.7 = (bf16[2,128,256]{2,1,0:T(8,128)(2,1)S(1)}, bf16[2,128,256]{2,1,0:T(8,128)(2,1)S(1)}, u32[]{:S(2)}, u32[]{:S(2)}) collective-permute-start(bf16[2,128,256]{2,1,0:T(8,128)(2,1)S(1)} %broadcast_select_fusion.3), channel_id=1, source_target_pairs={{0,16},{1,9},{2,18},{3,11},{4,20},{5,13},{6,22},{7,15},{8,24},{9,1... | collective-permute-start | bytes 393224 | tf_op jit(solution)/shard_map/ppermute | solution.py:43
  22.5 0.8 %collective-permute-done.8 = bf16[2,128,256]{2,1,0:T(8,128)(2,1)S(1)} collective-permute-done((bf16[2,128,256]{2,1,0:T(8,128)(2,1)S(1)}, bf16[2,128,256]{2,1,0:T(8,128)(2,1)S(1)}, u32[]{:S(2)}, u32[]{:S(2)}) %collective-permute-start.8) | collective-permute-done | bytes 131104 | tf_op jit(solution)/shard_map/ppermute | solution.py:43
  23.3 1.6 %collective-permute-start.12 = (bf16[2,128,256]{2,1,0:T(8,128)(2,1)S(1)}, bf16[2,128,256]{2,1,0:T(8,128)(2,1)S(1)}, u32[]{:S(2)}, u32[]{:S(2)}) collective-permute-start(bf16[2,128,256]{2,1,0:T(8,128)(2,1)S(1)} %broadcast_select_fusion.2), channel_id=1, source_target_pairs={{0,16},{1,9},{2,18},{3,11},{4,20},{5,13},{6,22},{7,15},{8,24},{9,1... | collective-permute-start | bytes 393224 | tf_op jit(solution)/shard_map/ppermute | solution.py:43
  24.9 1.8 %collective-permute-done.7 = bf16[2,128,256]{2,1,0:T(8,128)(2,1)S(1)} collective-permute-done((bf16[2,128,256]{2,1,0:T(8,128)(2,1)S(1)}, bf16[2,128,256]{2,1,0:T(8,128)(2,1)S(1)}, u32[]{:S(2)}, u32[]{:S(2)}) %collective-permute-start.7) | collective-permute-done | bytes 131104 | tf_op jit(solution)/shard_map/ppermute | solution.py:43
  26.8 1.6 %collective-permute-start.10 = (bf16[2,128,256]{2,1,0:T(8,128)(2,1)S(1)}, bf16[2,128,256]{2,1,0:T(8,128)(2,1)S(1)}, u32[]{:S(2)}, u32[]{:S(2)}) collective-permute-start(bf16[2,128,256]{2,1,0:T(8,128)(2,1)S(1)} %broadcast_select_fusion.4), channel_id=1, source_target_pairs={{0,2},{1,3},{2,0},{3,1},{4,6},{5,7},{6,4},{7,5},{8,10},{9,11},{10,... | collective-permute-start | bytes 393224 | tf_op jit(solution)/shard_map/ppermute | solution.py:43
  28.4 0.4 %collective-permute-start.11 = (bf16[2,128,256]{2,1,0:T(8,128)(2,1)S(1)}, bf16[2,128,256]{2,1,0:T(8,128)(2,1)S(1)}, u32[]{:S(2)}, u32[]{:S(2)}) collective-permute-start(bf16[2,128,256]{2,1,0:T(8,128)(2,1)S(1)} %broadcast_select_fusion.4), channel_id=1, source_target_pairs={{0,4},{1,5},{2,6},{3,7},{4,0},{5,1},{6,2},{7,3},{8,12},{9,13},{10,... | collective-permute-start | bytes 393224 | tf_op jit(solution)/shard_map/ppermute | solution.py:43
  28.8 1.5 %collective-permute-start.9 = (bf16[2,128,256]{2,1,0:T(8,128)(2,1)S(1)}, bf16[2,128,256]{2,1,0:T(8,128)(2,1)S(1)}, u32[]{:S(2)}, u32[]{:S(2)}) collective-permute-start(bf16[2,128,256]{2,1,0:T(8,128)(2,1)S(1)} %broadcast_select_fusion.4), channel_id=1, source_target_pairs={{0,6},{1,7},{2,4},{3,5},{4,2},{5,3},{6,0},{7,1},{8,14},{9,15},{10,... | collective-permute-start | bytes 393224 | tf_op jit(solution)/shard_map/ppermute | solution.py:43
  30.3 1.5 %convolution_convert_fusion.2 = bf16[2,512,256]{2,1,0:T(8,128)(2,1)S(1)} fusion(bf16[1,512,512]{2,1,0:T(8,128)(2,1)} %bitcast.9, bf16[1,512,512]{2,1,0:T(8,128)(2,1)S(1)} %copy-done.3, bf16[1,2,512,256]{3,2,0,1:T(8,128)(2,1)S(1)} %get-tuple-element.38, bf16[1,2,512,256]{3,2,0,1:T(8,128)(2,1)S(1)} %bitcast.50), kind=kOutput, calls=%fused_computation.9 | convolution fusion | flops 269484032 | bytes 2621440 | tf_op jit(solution)/shard_map/ktu,kur->ktr/dot_general | solution.py:98
  31.9 1.5 %collective-permute-start.15 = (bf16[2,128,256]{2,1,0:T(8,128)(2,1)S(1)}, bf16[2,128,256]{2,1,0:T(8,128)(2,1)S(1)}, u32[]{:S(2)}, u32[]{:S(2)}) collective-permute-start(bf16[2,128,256]{2,1,0:T(8,128)(2,1)S(1)} %broadcast_select_fusion.1), channel_id=1, source_target_pairs={{0,4},{1,5},{2,6},{3,7},{4,0},{5,1},{6,2},{7,3},{8,12},{9,13},{10,... | collective-permute-start | bytes 393224 | tf_op jit(solution)/shard_map/ppermute | solution.py:43
  33.4 0.5 %collective-permute-start.14 = (bf16[2,128,256]{2,1,0:T(8,128)(2,1)S(1)}, bf16[2,128,256]{2,1,0:T(8,128)(2,1)S(1)}, u32[]{:S(2)}, u32[]{:S(2)}) collective-permute-start(bf16[2,128,256]{2,1,0:T(8,128)(2,1)S(1)} %broadcast_select_fusion.1), channel_id=1, source_target_pairs={{0,2},{1,3},{2,0},{3,1},{4,6},{5,7},{6,4},{7,5},{8,10},{9,11},{10,... | collective-permute-start | bytes 393224 | tf_op jit(solution)/shard_map/ppermute | solution.py:43
  33.9 1.5 %collective-permute-start.13 = (bf16[2,128,256]{2,1,0:T(8,128)(2,1)S(1)}, bf16[2,128,256]{2,1,0:T(8,128)(2,1)S(1)}, u32[]{:S(2)}, u32[]{:S(2)}) collective-permute-start(bf16[2,128,256]{2,1,0:T(8,128)(2,1)S(1)} %broadcast_select_fusion.1), channel_id=1, source_target_pairs={{0,6},{1,7},{2,4},{3,5},{4,2},{5,3},{6,0},{7,1},{8,14},{9,15},{10,... | collective-permute-start | bytes 393224 | tf_op jit(solution)/shard_map/ppermute | solution.py:43
  35.4 0.7 %collective-permute-done.9 = bf16[2,128,256]{2,1,0:T(8,128)(2,1)S(1)} collective-permute-done((bf16[2,128,256]{2,1,0:T(8,128)(2,1)S(1)}, bf16[2,128,256]{2,1,0:T(8,128)(2,1)S(1)}, u32[]{:S(2)}, u32[]{:S(2)}) %collective-permute-start.9) | collective-permute-done | bytes 131104 | tf_op jit(solution)/shard_map/ppermute | solution.py:43
  36.2 1.7 %fusion.2 = bf16[2,256,256]{2,1,0:T(8,128)(2,1)S(1)} fusion(bf16[2,512,256]{2,1,0:T(8,128)(2,1)S(1)} %convolution_convert_fusion.2, bf16[1,512,512]{2,1,0:T(8,128)(2,1)} %bitcast.9, bf16[1,512,512]{2,1,0:T(8,128)(2,1)S(1)} %copy-done.3, bf16[2,128,256]{2,1,0:T(8,128)(2,1)S(1)} %get-tuple-element.30, bf16[2,128,256]{2,1,0:T(8,128)(2,1)S(1)} %get-tuple-element.31, ...), kind=kOutput, calls=%fused_computation.11 | convolution fusion | flops 405667840 | bytes 2359296 | tf_op jit(solution)/shard_map/ktr,kts->krs/dot_general | solution.py:118
  37.9 0.3 convolution_convert_fusion
  38.2 0.1 collective-permute-done.15
  38.4 1.4 %collective-permute-done.13 = bf16[2,128,256]{2,1,0:T(8,128)(2,1)S(1)} collective-permute-done((bf16[2,128,256]{2,1,0:T(8,128)(2,1)S(1)}, bf16[2,128,256]{2,1,0:T(8,128)(2,1)S(1)}, u32[]{:S(2)}, u32[]{:S(2)}) %collective-permute-start.13) | collective-permute-done | bytes 131104 | tf_op jit(solution)/shard_map/ppermute | solution.py:43
  39.9 1.4 %fusion = f32[512,512]{1,0:T(8,128)} fusion(bf16[2,512,256]{2,1,0:T(8,128)(2,1)S(1)} %convolution_convert_fusion, bf16[2,128,256]{2,1,0:T(8,128)(2,1)S(1)} %get-tuple-element.26, bf16[2,128,256]{2,1,0:T(8,128)(2,1)S(1)} %get-tuple-element.27, bf16[2,128,256]{2,1,0:T(8,128)(2,1)S(1)} %get-tuple-element.28, bf16[2,128,256]{2,1,0:T(8,128)(2,1)S(1)} %get-tuple-element.25, ...), kind=kOutput, calls=%fused_computation.6 | convolution fusion | flops 271056896 | bytes 2621440 | tf_op jit(solution)/shard_map/kts,kus->tu/dot_general | solution.py:123
  (35 shorter events, 0.7 us)
Async XLA Ops:
  0.7 1.0 %copy-start.1 = (bf16[1,1,512,256]{3,2,1,0:T(8,128)(2,1)S(1)}, bf16[1,1,512,256]{3,2,1,0:T(8,128)(2,1)}, u32[]{:S(2)}) copy-start(bf16[1,1,512,256]{3,2,1,0:T(8,128)(2,1)} %param.7) | copy-start | bytes 786436
  1.7 4.7 %copy-start = (bf16[1,1,512,256]{3,2,1,0:T(8,128)(2,1)S(1)}, bf16[1,1,512,256]{3,2,1,0:T(8,128)(2,1)}, u32[]{:S(2)}) copy-start(bf16[1,1,512,256]{3,2,1,0:T(8,128)(2,1)} %param.8) | copy-start | bytes 786436
  1.8 7.9 %collective-permute-start.2 = (bf16[2,128,256]{2,1,0:T(8,128)(2,1)S(1)}, bf16[2,128,256]{2,1,0:T(8,128)(2,1)S(1)}, u32[]{:S(2)}, u32[]{:S(2)}) collective-permute-start(bf16[2,128,256]{2,1,0:T(8,128)(2,1)S(1)} %get-tuple-element.33), channel_id=1, source_target_pairs={{0,6},{1,7},{2,4},{3,5},{4,2},{5,3},{6,0},{7,1},{8,14},{9,15},{10,... | collective-permute-start | bytes 393224 | tf_op jit(solution)/shard_map/ppermute | solution.py:43
  5.8 6.3 %collective-permute-start.3 = (bf16[2,128,256]{2,1,0:T(8,128)(2,1)S(1)}, bf16[2,128,256]{2,1,0:T(8,128)(2,1)S(1)}, u32[]{:S(2)}, u32[]{:S(2)}) collective-permute-start(bf16[2,128,256]{2,1,0:T(8,128)(2,1)S(1)} %get-tuple-element.34), channel_id=1, source_target_pairs={{0,4},{1,5},{2,6},{3,7},{4,0},{5,1},{6,2},{7,3},{8,12},{9,13},{10,... | collective-permute-start | bytes 393224 | tf_op jit(solution)/shard_map/ppermute | solution.py:43
  6.3 6.0 %collective-permute-start.4 = (bf16[2,128,256]{2,1,0:T(8,128)(2,1)S(1)}, bf16[2,128,256]{2,1,0:T(8,128)(2,1)S(1)}, u32[]{:S(2)}, u32[]{:S(2)}) collective-permute-start(bf16[2,128,256]{2,1,0:T(8,128)(2,1)S(1)} %get-tuple-element.35), channel_id=1, source_target_pairs={{0,2},{1,3},{2,0},{3,1},{4,6},{5,7},{6,4},{7,5},{8,10},{9,11},{10,... | collective-permute-start | bytes 393224 | tf_op jit(solution)/shard_map/ppermute | solution.py:43
  6.4 1.0 %copy-start.3 = (bf16[1,512,512]{2,1,0:T(8,128)(2,1)S(1)}, bf16[1,512,512]{2,1,0:T(8,128)(2,1)}, u32[]{:S(2)}) copy-start(bf16[1,512,512]{2,1,0:T(8,128)(2,1)} %param.9) | copy-start | bytes 1572868
  6.5 22.3 %collective-permute-start = (bf16[2,512,256]{2,1,0:T(8,128)(2,1)S(1)}, bf16[2,512,256]{2,1,0:T(8,128)(2,1)S(1)}, u32[]{:S(2)}, u32[]{:S(2)}) collective-permute-start(bf16[2,512,256]{2,1,0:T(8,128)(2,1)S(1)} %get-tuple-element.37), channel_id=1, source_target_pairs={{0,1},{1,0},{2,3},{3,2},{4,5},{5,4},{6,7},{7,6},{8,9},{9,8},{10,11... | collective-permute-start | bytes 1572872 | tf_op jit(solution)/shard_map/ppermute | solution.py:18
  7.5 0.7 %copy-start.2 = (s32[2]{0:T(128)S(1)}, s32[2]{0:T(128)}, u32[]{:S(2)}) copy-start(s32[2]{0:T(128)} %param.11) | copy-start | bytes 28
  7.5 22.8 %collective-permute-start.1 = (bf16[512,512]{1,0:T(8,128)(2,1)S(1)}, bf16[512,512]{1,0:T(8,128)(2,1)}, u32[]{:S(2)}, u32[]{:S(2)}) collective-permute-start(bf16[512,512]{1,0:T(8,128)(2,1)S(1)} %bitcast.49), channel_id=1, source_target_pairs={{0,1},{1,0},{2,3},{3,2},{4,5},{5,4},{6,7},{7,6},{8,9},{9,8},{10,11... | collective-permute-start | bytes 1572872 | tf_op jit(solution)/shard_map/ppermute | solution.py:18
  12.5 1.4 %collective-permute-start.5 = (bf16[2,128,256]{2,1,0:T(8,128)(2,1)S(1)}, bf16[2,128,256]{2,1,0:T(8,128)(2,1)S(1)}, u32[]{:S(2)}, u32[]{:S(2)}) collective-permute-start(bf16[2,128,256]{2,1,0:T(8,128)(2,1)S(1)} %get-tuple-element.41), channel_id=1, source_target_pairs={{0,1},{1,0},{2,3},{3,2},{4,5},{5,4},{6,7},{7,6},{8,9},{9,8},{10,11... | collective-permute-start | bytes 393224 | tf_op jit(solution)/shard_map/ppermute | solution.py:18
  13.9 6.4 %collective-permute-start.6 = (bf16[2,128,256]{2,1,0:T(8,128)(2,1)S(1)}, bf16[2,128,256]{2,1,0:T(8,128)(2,1)S(1)}, u32[]{:S(2)}, u32[]{:S(2)}) collective-permute-start(bf16[2,128,256]{2,1,0:T(8,128)(2,1)S(1)} %get-tuple-element.40), channel_id=1, source_target_pairs={{0,8},{1,17},{2,10},{3,19},{4,12},{5,21},{6,14},{7,23},{8,0},{9,25... | collective-permute-start | bytes 393224 | tf_op jit(solution)/shard_map/ppermute | solution.py:43
  15.6 7.8 %collective-permute-start.8 = (bf16[2,128,256]{2,1,0:T(8,128)(2,1)S(1)}, bf16[2,128,256]{2,1,0:T(8,128)(2,1)S(1)}, u32[]{:S(2)}, u32[]{:S(2)}) collective-permute-start(bf16[2,128,256]{2,1,0:T(8,128)(2,1)S(1)} %get-tuple-element.39), channel_id=1, source_target_pairs={{0,8},{1,17},{2,10},{3,19},{4,12},{5,21},{6,14},{7,23},{8,0},{9,25... | collective-permute-start | bytes 393224 | tf_op jit(solution)/shard_map/ppermute | solution.py:43
  20.3 6.5 %collective-permute-start.7 = (bf16[2,128,256]{2,1,0:T(8,128)(2,1)S(1)}, bf16[2,128,256]{2,1,0:T(8,128)(2,1)S(1)}, u32[]{:S(2)}, u32[]{:S(2)}) collective-permute-start(bf16[2,128,256]{2,1,0:T(8,128)(2,1)S(1)} %broadcast_select_fusion.3), channel_id=1, source_target_pairs={{0,16},{1,9},{2,18},{3,11},{4,20},{5,13},{6,22},{7,15},{8,24},{9,1... | collective-permute-start | bytes 393224 | tf_op jit(solution)/shard_map/ppermute | solution.py:43
  23.3 8.5 %collective-permute-start.12 = (bf16[2,128,256]{2,1,0:T(8,128)(2,1)S(1)}, bf16[2,128,256]{2,1,0:T(8,128)(2,1)S(1)}, u32[]{:S(2)}, u32[]{:S(2)}) collective-permute-start(bf16[2,128,256]{2,1,0:T(8,128)(2,1)S(1)} %broadcast_select_fusion.2), channel_id=1, source_target_pairs={{0,16},{1,9},{2,18},{3,11},{4,20},{5,13},{6,22},{7,15},{8,24},{9,1... | collective-permute-start | bytes 393224 | tf_op jit(solution)/shard_map/ppermute | solution.py:43
  26.8 7.1 %collective-permute-start.10 = (bf16[2,128,256]{2,1,0:T(8,128)(2,1)S(1)}, bf16[2,128,256]{2,1,0:T(8,128)(2,1)S(1)}, u32[]{:S(2)}, u32[]{:S(2)}) collective-permute-start(bf16[2,128,256]{2,1,0:T(8,128)(2,1)S(1)} %broadcast_select_fusion.4), channel_id=1, source_target_pairs={{0,2},{1,3},{2,0},{3,1},{4,6},{5,7},{6,4},{7,5},{8,10},{9,11},{10,... | collective-permute-start | bytes 393224 | tf_op jit(solution)/shard_map/ppermute | solution.py:43
  28.4 7.0 %collective-permute-start.11 = (bf16[2,128,256]{2,1,0:T(8,128)(2,1)S(1)}, bf16[2,128,256]{2,1,0:T(8,128)(2,1)S(1)}, u32[]{:S(2)}, u32[]{:S(2)}) collective-permute-start(bf16[2,128,256]{2,1,0:T(8,128)(2,1)S(1)} %broadcast_select_fusion.4), channel_id=1, source_target_pairs={{0,4},{1,5},{2,6},{3,7},{4,0},{5,1},{6,2},{7,3},{8,12},{9,13},{10,... | collective-permute-start | bytes 393224 | tf_op jit(solution)/shard_map/ppermute | solution.py:43
  28.8 7.3 %collective-permute-start.9 = (bf16[2,128,256]{2,1,0:T(8,128)(2,1)S(1)}, bf16[2,128,256]{2,1,0:T(8,128)(2,1)S(1)}, u32[]{:S(2)}, u32[]{:S(2)}) collective-permute-start(bf16[2,128,256]{2,1,0:T(8,128)(2,1)S(1)} %broadcast_select_fusion.4), channel_id=1, source_target_pairs={{0,6},{1,7},{2,4},{3,5},{4,2},{5,3},{6,0},{7,1},{8,14},{9,15},{10,... | collective-permute-start | bytes 393224 | tf_op jit(solution)/shard_map/ppermute | solution.py:43
  31.9 6.5 %collective-permute-start.15 = (bf16[2,128,256]{2,1,0:T(8,128)(2,1)S(1)}, bf16[2,128,256]{2,1,0:T(8,128)(2,1)S(1)}, u32[]{:S(2)}, u32[]{:S(2)}) collective-permute-start(bf16[2,128,256]{2,1,0:T(8,128)(2,1)S(1)} %broadcast_select_fusion.1), channel_id=1, source_target_pairs={{0,4},{1,5},{2,6},{3,7},{4,0},{5,1},{6,2},{7,3},{8,12},{9,13},{10,... | collective-permute-start | bytes 393224 | tf_op jit(solution)/shard_map/ppermute | solution.py:43
  33.4 5.0 %collective-permute-start.14 = (bf16[2,128,256]{2,1,0:T(8,128)(2,1)S(1)}, bf16[2,128,256]{2,1,0:T(8,128)(2,1)S(1)}, u32[]{:S(2)}, u32[]{:S(2)}) collective-permute-start(bf16[2,128,256]{2,1,0:T(8,128)(2,1)S(1)} %broadcast_select_fusion.1), channel_id=1, source_target_pairs={{0,2},{1,3},{2,0},{3,1},{4,6},{5,7},{6,4},{7,5},{8,10},{9,11},{10,... | collective-permute-start | bytes 393224 | tf_op jit(solution)/shard_map/ppermute | solution.py:43
  33.9 5.9 %collective-permute-start.13 = (bf16[2,128,256]{2,1,0:T(8,128)(2,1)S(1)}, bf16[2,128,256]{2,1,0:T(8,128)(2,1)S(1)}, u32[]{:S(2)}, u32[]{:S(2)}) collective-permute-start(bf16[2,128,256]{2,1,0:T(8,128)(2,1)S(1)} %broadcast_select_fusion.1), channel_id=1, source_target_pairs={{0,6},{1,7},{2,4},{3,5},{4,2},{5,3},{6,0},{7,1},{8,14},{9,15},{10,... | collective-permute-start | bytes 393224 | tf_op jit(solution)/shard_map/ppermute | solution.py:43
  38.2 1.7 %copy-start.4 = (bf16[512,512]{1,0:T(8,128)(2,1)S(1)}, bf16[512,512]{1,0:T(8,128)(2,1)}, u32[]{:S(2)}) copy-start(bf16[512,512]{1,0:T(8,128)(2,1)} %param.6) | copy-start | bytes 1572868

commit v6 on v4

--- a/solution.py
+++ b/solution.py
@@ -8,6 +8,7 @@
 LOW = 2
 FAN = ((1, 1), (2, 2), (3, 3))
 BACK = ((2, 2), (1, 1), (3, 3))
+BACK_LEFT = ((1, 1), (2, 2), (3, 3))
 
 
 def after(value, earlier):
@@ -67,11 +68,11 @@
             return jnp.stack([mine, swap_cols(other)])
         return jnp.roll(lax.all_to_all(slots, "col", 0, 0, tiled=True), -self.col, axis=0)
 
-    def gather_start(self, held):
-        return [held, *(self.cross(held, masks) for masks in BACK)]
+    def gather_start(self, held, fan=BACK):
+        return [held, *(self.cross(held, masks) for masks in fan)]
 
-    def gather_end(self, parts):
-        masks = [self.of(masks) for masks in BACK]
+    def gather_end(self, parts, fan=BACK):
+        masks = [self.of(masks) for masks in fan]
         whole = []
         for q in range(1 << LOW):
             part = parts[0]
@@ -111,7 +112,7 @@
     one = first.spread(one, after(came_one, (two, base)), last)
     parts_one = first.gather_start(one)
     two = second.spread(two, after(came_two, (one, solved)), last)
-    parts_two = second.gather_start(two)
+    parts_two = second.gather_start(two, BACK_LEFT)
 
     right_col = first.gather_end(parts_one)
     solved_col = solve(inverse, right_col).astype(jnp.bfloat16)
@@ -119,7 +120,7 @@
     core = core.astype(jnp.bfloat16)
     mixed = jnp.einsum("ktr,krs->kts", left, core, preferred_element_type=jnp.float32)
     mixed = mixed.astype(jnp.bfloat16)
-    left_col = second.gather_end([after(part, mixed) for part in parts_two])
+    left_col = second.gather_end([after(part, mixed) for part in parts_two], BACK_LEFT)
     change = jnp.einsum("kts,kus->tu", mixed, left_col, preferred_element_type=jnp.float32)
     return base - change
 

time: 41.6 us -> 42.2 us (1.014)
  waiting for transfers between devices: 14.5 us -> 15.1 us
    ppermute x13, waiting for transfers between devices: 13.3 us -> 13.9 us  [cross(): return lax.ppermute(block, ('row', 'col'), pairs)]
  transfers between devices with their start and end apart: 16 -> 16, of which waited for: 10 -> 9; matrix products, arithmetic and copies ran while one was open for 10% -> 10% of each run, Pallas kernels for 0% -> 0%
where the time goes in v6:
time: 42.2 us; the launch traced here: 41.9 us
  starting transfers between devices  17.8 us (42%)
  waiting for transfers between devices  15.1 us (36%)
  matrix products  4.9 us (12%)
  other arithmetic  1.67 us (4%)
  local copies, waits for them, and re-layouts  1.55 us (4%)
  between operations  0.93 us (2%)
    ppermute x13, starting transfers between devices, cross(): return lax.ppermute(block, ('row', 'col'), pairs)  17.6 us
    ppermute x13, waiting for transfers between devices, cross(): return lax.ppermute(block, ('row', 'col'), pairs)  13.9 us
    dot_general x1, matrix products, local(): jnp.einsum('ktr,kts->krs', solved, solved_col, preferred_element_type=jnp...  1.68 us
    unnamed x10, local copies, waits for them, and re-layouts  1.55 us
    dot_general x1, matrix products, local(): solved = solve(inverse, right).astype(jnp.bfloat16)  1.48 us
    dot_general x1, matrix products, local(): jnp.einsum('kts,kus->tu', mixed, left_col, preferred_element_type=jnp.flo...  1.44 us
    ppermute x3, waiting for transfers between devices, swap_cols(): return lax.ppermute(block, 'col', [(0, 1), (1, 0)])  1.19 us
    select_n x2, other arithmetic, local(): jnp.where(keep[None, :], w_factor[0, 0], jnp.zeros((), jnp.bfloat16))  1.04 us
  transfers between devices with their start and end apart: 16, of which 9 were waited for; matrix products, arithmetic and copies ran while one was open for 10% of the time, Pallas kernels for 0%

profile of v6, /device:TPU:0, one launch (start us, length us, event | category | flops | bytes accessed | tf_op | source)
XLA Modules:
  0.0 41.9 jit_solution(2655986375128598270)
XLA Ops:
  0.7 1.0 %broadcast_select_fusion = bf16[1,4,128,256]{3,2,1,0:T(8,128)(2,1)S(1)} fusion(bf16[1,4,128,256]{3,2,1,0:T(8,128)(2,1)} %bitcast.45, pred[256]{0:T(512)(128)(4,1)S(1)} %iota_compare_fusion), kind=kLoop, calls=%fused_computation.44 | loop fusion | flops 131072 | bytes 524544 | tf_op jit(solution)/shard_map/jit(_where)/select_n | solution.py:90
  1.8 4.0 %collective-permute-start.2 = (bf16[2,128,256]{2,1,0:T(8,128)(2,1)S(1)}, bf16[2,128,256]{2,1,0:T(8,128)(2,1)S(1)}, u32[]{:S(2)}, u32[]{:S(2)}) collective-permute-start(bf16[2,128,256]{2,1,0:T(8,128)(2,1)S(1)} %get-tuple-element.35), channel_id=1, source_target_pairs={{0,6},{1,7},{2,4},{3,5},{4,2},{5,3},{6,0},{7,1},{8,14},{9,15},{10,... | collective-permute-start | bytes 393224 | tf_op jit(solution)/shard_map/ppermute | solution.py:44
  5.8 0.5 %collective-permute-start.3 = (bf16[2,128,256]{2,1,0:T(8,128)(2,1)S(1)}, bf16[2,128,256]{2,1,0:T(8,128)(2,1)S(1)}, u32[]{:S(2)}, u32[]{:S(2)}) collective-permute-start(bf16[2,128,256]{2,1,0:T(8,128)(2,1)S(1)} %get-tuple-element.36), channel_id=1, source_target_pairs={{0,4},{1,5},{2,6},{3,7},{4,0},{5,1},{6,2},{7,3},{8,12},{9,13},{10,... | collective-permute-start | bytes 393224 | tf_op jit(solution)/shard_map/ppermute | solution.py:44
  6.3 0.1 collective-permute-start.4
  6.5 0.1 collective-permute-start
  6.6 0.9 %copy-done.3 = bf16[1,512,512]{2,1,0:T(8,128)(2,1)S(1)} copy-done((bf16[1,512,512]{2,1,0:T(8,128)(2,1)S(1)}, bf16[1,512,512]{2,1,0:T(8,128)(2,1)}, u32[]{:S(2)}) %copy-start.3) | copy-done | bytes 524312
  7.5 0.7 %copy-done.2 = s32[2]{0:T(128)S(1)} copy-done((s32[2]{0:T(128)S(1)}, s32[2]{0:T(128)}, u32[]{:S(2)}) %copy-start.2) | copy-done | bytes 32
  8.2 1.5 %collective-permute-done.2 = bf16[2,128,256]{2,1,0:T(8,128)(2,1)S(1)} collective-permute-done((bf16[2,128,256]{2,1,0:T(8,128)(2,1)S(1)}, bf16[2,128,256]{2,1,0:T(8,128)(2,1)S(1)}, u32[]{:S(2)}, u32[]{:S(2)}) %collective-permute-start.2) | collective-permute-done | bytes 131104 | tf_op jit(solution)/shard_map/ppermute | solution.py:44
  9.7 2.4 %collective-permute-done.3 = bf16[2,128,256]{2,1,0:T(8,128)(2,1)S(1)} collective-permute-done((bf16[2,128,256]{2,1,0:T(8,128)(2,1)S(1)}, bf16[2,128,256]{2,1,0:T(8,128)(2,1)S(1)}, u32[]{:S(2)}, u32[]{:S(2)}) %collective-permute-start.3) | collective-permute-done | bytes 131104 | tf_op jit(solution)/shard_map/ppermute | solution.py:44
  12.1 0.2 collective-permute-done.4
  12.3 0.1 select_select_fusion
  12.6 0.1 select_reduce_fusion
  12.7 1.2 %collective-permute-done.5 = bf16[2,128,256]{2,1,0:T(8,128)(2,1)S(1)} collective-permute-done((bf16[2,128,256]{2,1,0:T(8,128)(2,1)S(1)}, bf16[2,128,256]{2,1,0:T(8,128)(2,1)S(1)}, u32[]{:S(2)}, u32[]{:S(2)}) %collective-permute-start.5) | collective-permute-done | bytes 131104 | tf_op jit(solution)/shard_map/ppermute | solution.py:19
  13.9 1.6 %collective-permute-start.6 = (bf16[2,128,256]{2,1,0:T(8,128)(2,1)S(1)}, bf16[2,128,256]{2,1,0:T(8,128)(2,1)S(1)}, u32[]{:S(2)}, u32[]{:S(2)}) collective-permute-start(bf16[2,128,256]{2,1,0:T(8,128)(2,1)S(1)} %get-tuple-element.42), channel_id=1, source_target_pairs={{0,8},{1,17},{2,10},{3,19},{4,12},{5,21},{6,14},{7,23},{8,0},{9,25... | collective-permute-start | bytes 393224 | tf_op jit(solution)/shard_map/ppermute | solution.py:44
  15.6 0.4 %collective-permute-start.8 = (bf16[2,128,256]{2,1,0:T(8,128)(2,1)S(1)}, bf16[2,128,256]{2,1,0:T(8,128)(2,1)S(1)}, u32[]{:S(2)}, u32[]{:S(2)}) collective-permute-start(bf16[2,128,256]{2,1,0:T(8,128)(2,1)S(1)} %get-tuple-element.41), channel_id=1, source_target_pairs={{0,8},{1,17},{2,10},{3,19},{4,12},{5,21},{6,14},{7,23},{8,0},{9,25... | collective-permute-start | bytes 393224 | tf_op jit(solution)/shard_map/ppermute | solution.py:44
  16.0 4.3 %collective-permute-done.6 = bf16[2,128,256]{2,1,0:T(8,128)(2,1)S(1)} collective-permute-done((bf16[2,128,256]{2,1,0:T(8,128)(2,1)S(1)}, bf16[2,128,256]{2,1,0:T(8,128)(2,1)S(1)}, u32[]{:S(2)}, u32[]{:S(2)}) %collective-permute-start.6) | collective-permute-done | bytes 131104 | tf_op jit(solution)/shard_map/ppermute | solution.py:44
  20.3 2.2 %collective-permute-start.7 = (bf16[2,128,256]{2,1,0:T(8,128)(2,1)S(1)}, bf16[2,128,256]{2,1,0:T(8,128)(2,1)S(1)}, u32[]{:S(2)}, u32[]{:S(2)}) collective-permute-start(bf16[2,128,256]{2,1,0:T(8,128)(2,1)S(1)} %broadcast_select_fusion.3), channel_id=1, source_target_pairs={{0,16},{1,9},{2,18},{3,11},{4,20},{5,13},{6,22},{7,15},{8,24},{9,1... | collective-permute-start | bytes 393224 | tf_op jit(solution)/shard_map/ppermute | solution.py:44
  22.5 0.8 %collective-permute-done.8 = bf16[2,128,256]{2,1,0:T(8,128)(2,1)S(1)} collective-permute-done((bf16[2,128,256]{2,1,0:T(8,128)(2,1)S(1)}, bf16[2,128,256]{2,1,0:T(8,128)(2,1)S(1)}, u32[]{:S(2)}, u32[]{:S(2)}) %collective-permute-start.8) | collective-permute-done | bytes 131104 | tf_op jit(solution)/shard_map/ppermute | solution.py:44
  23.3 1.6 %collective-permute-start.12 = (bf16[2,128,256]{2,1,0:T(8,128)(2,1)S(1)}, bf16[2,128,256]{2,1,0:T(8,128)(2,1)S(1)}, u32[]{:S(2)}, u32[]{:S(2)}) collective-permute-start(bf16[2,128,256]{2,1,0:T(8,128)(2,1)S(1)} %broadcast_select_fusion.2), channel_id=1, source_target_pairs={{0,16},{1,9},{2,18},{3,11},{4,20},{5,13},{6,22},{7,15},{8,24},{9,1... | collective-permute-start | bytes 393224 | tf_op jit(solution)/shard_map/ppermute | solution.py:44
  24.9 1.8 %collective-permute-done.7 = bf16[2,128,256]{2,1,0:T(8,128)(2,1)S(1)} collective-permute-done((bf16[2,128,256]{2,1,0:T(8,128)(2,1)S(1)}, bf16[2,128,256]{2,1,0:T(8,128)(2,1)S(1)}, u32[]{:S(2)}, u32[]{:S(2)}) %collective-permute-start.7) | collective-permute-done | bytes 131104 | tf_op jit(solution)/shard_map/ppermute | solution.py:44
  26.8 1.6 %collective-permute-start.10 = (bf16[2,128,256]{2,1,0:T(8,128)(2,1)S(1)}, bf16[2,128,256]{2,1,0:T(8,128)(2,1)S(1)}, u32[]{:S(2)}, u32[]{:S(2)}) collective-permute-start(bf16[2,128,256]{2,1,0:T(8,128)(2,1)S(1)} %broadcast_select_fusion.4), channel_id=1, source_target_pairs={{0,2},{1,3},{2,0},{3,1},{4,6},{5,7},{6,4},{7,5},{8,10},{9,11},{10,... | collective-permute-start | bytes 393224 | tf_op jit(solution)/shard_map/ppermute | solution.py:44
  28.4 0.4 %collective-permute-start.11 = (bf16[2,128,256]{2,1,0:T(8,128)(2,1)S(1)}, bf16[2,128,256]{2,1,0:T(8,128)(2,1)S(1)}, u32[]{:S(2)}, u32[]{:S(2)}) collective-permute-start(bf16[2,128,256]{2,1,0:T(8,128)(2,1)S(1)} %broadcast_select_fusion.4), channel_id=1, source_target_pairs={{0,4},{1,5},{2,6},{3,7},{4,0},{5,1},{6,2},{7,3},{8,12},{9,13},{10,... | collective-permute-start | bytes 393224 | tf_op jit(solution)/shard_map/ppermute | solution.py:44
  28.8 1.5 %collective-permute-start.9 = (bf16[2,128,256]{2,1,0:T(8,128)(2,1)S(1)}, bf16[2,128,256]{2,1,0:T(8,128)(2,1)S(1)}, u32[]{:S(2)}, u32[]{:S(2)}) collective-permute-start(bf16[2,128,256]{2,1,0:T(8,128)(2,1)S(1)} %broadcast_select_fusion.4), channel_id=1, source_target_pairs={{0,6},{1,7},{2,4},{3,5},{4,2},{5,3},{6,0},{7,1},{8,14},{9,15},{10,... | collective-permute-start | bytes 393224 | tf_op jit(solution)/shard_map/ppermute | solution.py:44
  30.3 1.5 %convolution_convert_fusion.2 = bf16[2,512,256]{2,1,0:T(8,128)(2,1)S(1)} fusion(bf16[1,512,512]{2,1,0:T(8,128)(2,1)} %bitcast.9, bf16[1,512,512]{2,1,0:T(8,128)(2,1)S(1)} %copy-done.3, bf16[1,2,512,256]{3,2,0,1:T(8,128)(2,1)S(1)} %get-tuple-element.40, bf16[1,2,512,256]{3,2,0,1:T(8,128)(2,1)S(1)} %bitcast.50), kind=kOutput, calls=%fused_computation.9 | convolution fusion | flops 269484032 | bytes 2621440 | tf_op jit(solution)/shard_map/ktu,kur->ktr/dot_general | solution.py:99
  31.9 1.6 %collective-permute-start.15 = (bf16[2,128,256]{2,1,0:T(8,128)(2,1)S(1)}, bf16[2,128,256]{2,1,0:T(8,128)(2,1)S(1)}, u32[]{:S(2)}, u32[]{:S(2)}) collective-permute-start(bf16[2,128,256]{2,1,0:T(8,128)(2,1)S(1)} %broadcast_select_fusion.1), channel_id=1, source_target_pairs={{0,2},{1,3},{2,0},{3,1},{4,6},{5,7},{6,4},{7,5},{8,10},{9,11},{10,... | collective-permute-start | bytes 393224 | tf_op jit(solution)/shard_map/ppermute | solution.py:44
  33.5 0.4 %collective-permute-start.14 = (bf16[2,128,256]{2,1,0:T(8,128)(2,1)S(1)}, bf16[2,128,256]{2,1,0:T(8,128)(2,1)S(1)}, u32[]{:S(2)}, u32[]{:S(2)}) collective-permute-start(bf16[2,128,256]{2,1,0:T(8,128)(2,1)S(1)} %broadcast_select_fusion.1), channel_id=1, source_target_pairs={{0,4},{1,5},{2,6},{3,7},{4,0},{5,1},{6,2},{7,3},{8,12},{9,13},{10,... | collective-permute-start | bytes 393224 | tf_op jit(solution)/shard_map/ppermute | solution.py:44
  33.9 1.5 %collective-permute-start.13 = (bf16[2,128,256]{2,1,0:T(8,128)(2,1)S(1)}, bf16[2,128,256]{2,1,0:T(8,128)(2,1)S(1)}, u32[]{:S(2)}, u32[]{:S(2)}) collective-permute-start(bf16[2,128,256]{2,1,0:T(8,128)(2,1)S(1)} %broadcast_select_fusion.1), channel_id=1, source_target_pairs={{0,6},{1,7},{2,4},{3,5},{4,2},{5,3},{6,0},{7,1},{8,14},{9,15},{10,... | collective-permute-start | bytes 393224 | tf_op jit(solution)/shard_map/ppermute | solution.py:44
  35.4 0.8 %collective-permute-done.9 = bf16[2,128,256]{2,1,0:T(8,128)(2,1)S(1)} collective-permute-done((bf16[2,128,256]{2,1,0:T(8,128)(2,1)S(1)}, bf16[2,128,256]{2,1,0:T(8,128)(2,1)S(1)}, u32[]{:S(2)}, u32[]{:S(2)}) %collective-permute-start.9) | collective-permute-done | bytes 131104 | tf_op jit(solution)/shard_map/ppermute | solution.py:44
  36.3 1.7 %fusion.2 = bf16[2,256,256]{2,1,0:T(8,128)(2,1)S(1)} fusion(bf16[2,512,256]{2,1,0:T(8,128)(2,1)S(1)} %convolution_convert_fusion.2, bf16[1,512,512]{2,1,0:T(8,128)(2,1)} %bitcast.9, bf16[1,512,512]{2,1,0:T(8,128)(2,1)S(1)} %copy-done.3, bf16[2,128,256]{2,1,0:T(8,128)(2,1)S(1)} %get-tuple-element.32, bf16[2,128,256]{2,1,0:T(8,128)(2,1)S(1)} %get-tuple-element.33, ...), kind=kOutput, calls=%fused_computation.11 | convolution fusion | flops 405667840 | bytes 2359296 | tf_op jit(solution)/shard_map/ktr,kts->krs/dot_general | solution.py:119
  38.0 0.3 convolution_convert_fusion
  38.3 2.1 %collective-permute-done.14 = bf16[2,128,256]{2,1,0:T(8,128)(2,1)S(1)} collective-permute-done((bf16[2,128,256]{2,1,0:T(8,128)(2,1)S(1)}, bf16[2,128,256]{2,1,0:T(8,128)(2,1)S(1)}, u32[]{:S(2)}, u32[]{:S(2)}) %collective-permute-start.14) | collective-permute-done | bytes 131104 | tf_op jit(solution)/shard_map/ppermute | solution.py:44
  40.5 1.4 %fusion = f32[512,512]{1,0:T(8,128)} fusion(bf16[2,512,256]{2,1,0:T(8,128)(2,1)S(1)} %convolution_convert_fusion, bf16[2,128,256]{2,1,0:T(8,128)(2,1)S(1)} %get-tuple-element.28, bf16[2,128,256]{2,1,0:T(8,128)(2,1)S(1)} %get-tuple-element.29, bf16[2,128,256]{2,1,0:T(8,128)(2,1)S(1)} %get-tuple-element.30, bf16[2,128,256]{2,1,0:T(8,128)(2,1)S(1)} %get-tuple-element.27, ...), kind=kOutput, calls=%fused_computation.6 | convolution fusion | flops 271056896 | bytes 2621440 | tf_op jit(solution)/shard_map/kts,kus->tu/dot_general | solution.py:124
  (34 shorter events, 0.6 us)
Async XLA Ops:
  0.7 1.0 %copy-start.1 = (bf16[1,1,512,256]{3,2,1,0:T(8,128)(2,1)S(1)}, bf16[1,1,512,256]{3,2,1,0:T(8,128)(2,1)}, u32[]{:S(2)}) copy-start(bf16[1,1,512,256]{3,2,1,0:T(8,128)(2,1)} %param.7) | copy-start | bytes 786436
  1.7 4.7 %copy-start = (bf16[1,1,512,256]{3,2,1,0:T(8,128)(2,1)S(1)}, bf16[1,1,512,256]{3,2,1,0:T(8,128)(2,1)}, u32[]{:S(2)}) copy-start(bf16[1,1,512,256]{3,2,1,0:T(8,128)(2,1)} %param.8) | copy-start | bytes 786436
  1.8 7.9 %collective-permute-start.2 = (bf16[2,128,256]{2,1,0:T(8,128)(2,1)S(1)}, bf16[2,128,256]{2,1,0:T(8,128)(2,1)S(1)}, u32[]{:S(2)}, u32[]{:S(2)}) collective-permute-start(bf16[2,128,256]{2,1,0:T(8,128)(2,1)S(1)} %get-tuple-element.35), channel_id=1, source_target_pairs={{0,6},{1,7},{2,4},{3,5},{4,2},{5,3},{6,0},{7,1},{8,14},{9,15},{10,... | collective-permute-start | bytes 393224 | tf_op jit(solution)/shard_map/ppermute | solution.py:44
  5.8 6.3 %collective-permute-start.3 = (bf16[2,128,256]{2,1,0:T(8,128)(2,1)S(1)}, bf16[2,128,256]{2,1,0:T(8,128)(2,1)S(1)}, u32[]{:S(2)}, u32[]{:S(2)}) collective-permute-start(bf16[2,128,256]{2,1,0:T(8,128)(2,1)S(1)} %get-tuple-element.36), channel_id=1, source_target_pairs={{0,4},{1,5},{2,6},{3,7},{4,0},{5,1},{6,2},{7,3},{8,12},{9,13},{10,... | collective-permute-start | bytes 393224 | tf_op jit(solution)/shard_map/ppermute | solution.py:44
  6.3 6.0 %collective-permute-start.4 = (bf16[2,128,256]{2,1,0:T(8,128)(2,1)S(1)}, bf16[2,128,256]{2,1,0:T(8,128)(2,1)S(1)}, u32[]{:S(2)}, u32[]{:S(2)}) collective-permute-start(bf16[2,128,256]{2,1,0:T(8,128)(2,1)S(1)} %get-tuple-element.37), channel_id=1, source_target_pairs={{0,2},{1,3},{2,0},{3,1},{4,6},{5,7},{6,4},{7,5},{8,10},{9,11},{10,... | collective-permute-start | bytes 393224 | tf_op jit(solution)/shard_map/ppermute | solution.py:44
  6.4 1.0 %copy-start.3 = (bf16[1,512,512]{2,1,0:T(8,128)(2,1)S(1)}, bf16[1,512,512]{2,1,0:T(8,128)(2,1)}, u32[]{:S(2)}) copy-start(bf16[1,512,512]{2,1,0:T(8,128)(2,1)} %param.9) | copy-start | bytes 1572868
  6.5 22.3 %collective-permute-start = (bf16[2,512,256]{2,1,0:T(8,128)(2,1)S(1)}, bf16[2,512,256]{2,1,0:T(8,128)(2,1)S(1)}, u32[]{:S(2)}, u32[]{:S(2)}) collective-permute-start(bf16[2,512,256]{2,1,0:T(8,128)(2,1)S(1)} %get-tuple-element.39), channel_id=1, source_target_pairs={{0,1},{1,0},{2,3},{3,2},{4,5},{5,4},{6,7},{7,6},{8,9},{9,8},{10,11... | collective-permute-start | bytes 1572872 | tf_op jit(solution)/shard_map/ppermute | solution.py:19
  7.5 0.7 %copy-start.2 = (s32[2]{0:T(128)S(1)}, s32[2]{0:T(128)}, u32[]{:S(2)}) copy-start(s32[2]{0:T(128)} %param.11) | copy-start | bytes 28
  7.5 22.9 %collective-permute-start.1 = (bf16[512,512]{1,0:T(8,128)(2,1)S(1)}, bf16[512,512]{1,0:T(8,128)(2,1)}, u32[]{:S(2)}, u32[]{:S(2)}) collective-permute-start(bf16[512,512]{1,0:T(8,128)(2,1)S(1)} %bitcast.49), channel_id=1, source_target_pairs={{0,1},{1,0},{2,3},{3,2},{4,5},{5,4},{6,7},{7,6},{8,9},{9,8},{10,11... | collective-permute-start | bytes 1572872 | tf_op jit(solution)/shard_map/ppermute | solution.py:19
  12.5 1.4 %collective-permute-start.5 = (bf16[2,128,256]{2,1,0:T(8,128)(2,1)S(1)}, bf16[2,128,256]{2,1,0:T(8,128)(2,1)S(1)}, u32[]{:S(2)}, u32[]{:S(2)}) collective-permute-start(bf16[2,128,256]{2,1,0:T(8,128)(2,1)S(1)} %get-tuple-element.43), channel_id=1, source_target_pairs={{0,1},{1,0},{2,3},{3,2},{4,5},{5,4},{6,7},{7,6},{8,9},{9,8},{10,11... | collective-permute-start | bytes 393224 | tf_op jit(solution)/shard_map/ppermute | solution.py:19
  13.9 6.4 %collective-permute-start.6 = (bf16[2,128,256]{2,1,0:T(8,128)(2,1)S(1)}, bf16[2,128,256]{2,1,0:T(8,128)(2,1)S(1)}, u32[]{:S(2)}, u32[]{:S(2)}) collective-permute-start(bf16[2,128,256]{2,1,0:T(8,128)(2,1)S(1)} %get-tuple-element.42), channel_id=1, source_target_pairs={{0,8},{1,17},{2,10},{3,19},{4,12},{5,21},{6,14},{7,23},{8,0},{9,25... | collective-permute-start | bytes 393224 | tf_op jit(solution)/shard_map/ppermute | solution.py:44
  15.6 7.8 %collective-permute-start.8 = (bf16[2,128,256]{2,1,0:T(8,128)(2,1)S(1)}, bf16[2,128,256]{2,1,0:T(8,128)(2,1)S(1)}, u32[]{:S(2)}, u32[]{:S(2)}) collective-permute-start(bf16[2,128,256]{2,1,0:T(8,128)(2,1)S(1)} %get-tuple-element.41), channel_id=1, source_target_pairs={{0,8},{1,17},{2,10},{3,19},{4,12},{5,21},{6,14},{7,23},{8,0},{9,25... | collective-permute-start | bytes 393224 | tf_op jit(solution)/shard_map/ppermute | solution.py:44
  20.3 6.5 %collective-permute-start.7 = (bf16[2,128,256]{2,1,0:T(8,128)(2,1)S(1)}, bf16[2,128,256]{2,1,0:T(8,128)(2,1)S(1)}, u32[]{:S(2)}, u32[]{:S(2)}) collective-permute-start(bf16[2,128,256]{2,1,0:T(8,128)(2,1)S(1)} %broadcast_select_fusion.3), channel_id=1, source_target_pairs={{0,16},{1,9},{2,18},{3,11},{4,20},{5,13},{6,22},{7,15},{8,24},{9,1... | collective-permute-start | bytes 393224 | tf_op jit(solution)/shard_map/ppermute | solution.py:44
  23.3 8.5 %collective-permute-start.12 = (bf16[2,128,256]{2,1,0:T(8,128)(2,1)S(1)}, bf16[2,128,256]{2,1,0:T(8,128)(2,1)S(1)}, u32[]{:S(2)}, u32[]{:S(2)}) collective-permute-start(bf16[2,128,256]{2,1,0:T(8,128)(2,1)S(1)} %broadcast_select_fusion.2), channel_id=1, source_target_pairs={{0,16},{1,9},{2,18},{3,11},{4,20},{5,13},{6,22},{7,15},{8,24},{9,1... | collective-permute-start | bytes 393224 | tf_op jit(solution)/shard_map/ppermute | solution.py:44
  26.8 7.1 %collective-permute-start.10 = (bf16[2,128,256]{2,1,0:T(8,128)(2,1)S(1)}, bf16[2,128,256]{2,1,0:T(8,128)(2,1)S(1)}, u32[]{:S(2)}, u32[]{:S(2)}) collective-permute-start(bf16[2,128,256]{2,1,0:T(8,128)(2,1)S(1)} %broadcast_select_fusion.4), channel_id=1, source_target_pairs={{0,2},{1,3},{2,0},{3,1},{4,6},{5,7},{6,4},{7,5},{8,10},{9,11},{10,... | collective-permute-start | bytes 393224 | tf_op jit(solution)/shard_map/ppermute | solution.py:44
  28.4 7.0 %collective-permute-start.11 = (bf16[2,128,256]{2,1,0:T(8,128)(2,1)S(1)}, bf16[2,128,256]{2,1,0:T(8,128)(2,1)S(1)}, u32[]{:S(2)}, u32[]{:S(2)}) collective-permute-start(bf16[2,128,256]{2,1,0:T(8,128)(2,1)S(1)} %broadcast_select_fusion.4), channel_id=1, source_target_pairs={{0,4},{1,5},{2,6},{3,7},{4,0},{5,1},{6,2},{7,3},{8,12},{9,13},{10,... | collective-permute-start | bytes 393224 | tf_op jit(solution)/shard_map/ppermute | solution.py:44
  28.8 7.4 %collective-permute-start.9 = (bf16[2,128,256]{2,1,0:T(8,128)(2,1)S(1)}, bf16[2,128,256]{2,1,0:T(8,128)(2,1)S(1)}, u32[]{:S(2)}, u32[]{:S(2)}) collective-permute-start(bf16[2,128,256]{2,1,0:T(8,128)(2,1)S(1)} %broadcast_select_fusion.4), channel_id=1, source_target_pairs={{0,6},{1,7},{2,4},{3,5},{4,2},{5,3},{6,0},{7,1},{8,14},{9,15},{10,... | collective-permute-start | bytes 393224 | tf_op jit(solution)/shard_map/ppermute | solution.py:44
  31.9 6.4 %collective-permute-start.15 = (bf16[2,128,256]{2,1,0:T(8,128)(2,1)S(1)}, bf16[2,128,256]{2,1,0:T(8,128)(2,1)S(1)}, u32[]{:S(2)}, u32[]{:S(2)}) collective-permute-start(bf16[2,128,256]{2,1,0:T(8,128)(2,1)S(1)} %broadcast_select_fusion.1), channel_id=1, source_target_pairs={{0,2},{1,3},{2,0},{3,1},{4,6},{5,7},{6,4},{7,5},{8,10},{9,11},{10,... | collective-permute-start | bytes 393224 | tf_op jit(solution)/shard_map/ppermute | solution.py:44
  33.5 6.9 %collective-permute-start.14 = (bf16[2,128,256]{2,1,0:T(8,128)(2,1)S(1)}, bf16[2,128,256]{2,1,0:T(8,128)(2,1)S(1)}, u32[]{:S(2)}, u32[]{:S(2)}) collective-permute-start(bf16[2,128,256]{2,1,0:T(8,128)(2,1)S(1)} %broadcast_select_fusion.1), channel_id=1, source_target_pairs={{0,4},{1,5},{2,6},{3,7},{4,0},{5,1},{6,2},{7,3},{8,12},{9,13},{10,... | collective-permute-start | bytes 393224 | tf_op jit(solution)/shard_map/ppermute | solution.py:44
  33.9 6.5 %collective-permute-start.13 = (bf16[2,128,256]{2,1,0:T(8,128)(2,1)S(1)}, bf16[2,128,256]{2,1,0:T(8,128)(2,1)S(1)}, u32[]{:S(2)}, u32[]{:S(2)}) collective-permute-start(bf16[2,128,256]{2,1,0:T(8,128)(2,1)S(1)} %broadcast_select_fusion.1), channel_id=1, source_target_pairs={{0,6},{1,7},{2,4},{3,5},{4,2},{5,3},{6,0},{7,1},{8,14},{9,15},{10,... | collective-permute-start | bytes 393224 | tf_op jit(solution)/shard_map/ppermute | solution.py:44
  38.3 2.2 %copy-start.4 = (bf16[512,512]{1,0:T(8,128)(2,1)S(1)}, bf16[512,512]{1,0:T(8,128)(2,1)}, u32[]{:S(2)}) copy-start(bf16[512,512]{1,0:T(8,128)(2,1)} %param.6) | copy-start | bytes 1572868
